TPU v7x, 128 devices: a whole 4x4x4 slice. The times are simulated.
128 devices in a mesh: gx: 32 (over y, x, core), gy: 4 (over z).
Axes of the slice: x: 4, y: 4, z: 4, core: 2. Of those that a mesh axis runs over, the one named last changes fastest.
Arguments:
- head_start: float32 [32, 256, 512], P(None, 'gx', 'gy'), may hold values from -6 to -0.5
- sat_conduct: float32 [32, 256, 512], P(None, 'gx', 'gy'), may hold values from 0.5 to 5
- alpha_dry: float32 [32, 256, 512], P(None, 'gx', 'gy'), may hold values from 0.5 to 3
- wet_flag: int32 [32, 256, 512], P(None, 'gx', 'gy'), may hold values 0 or 1
- reversal_head: float32 [32, 256, 512], P(None, 'gx', 'gy'), may hold values from -8 to -1
- send_row: int32 [128, 9, 1024], P(('gx', 'gy')), may hold values from 0 to 255
- send_col: int32 [128, 9, 1024], P(('gx', 'gy')), may hold values from 0 to 127
- root_radial: float32 [16384, 128], P(('gx', 'gy')), may hold values from 0.02 to 0.2
- root_axial: float32 [16384, 128], P(('gx', 'gy')), may hold values from 1 to 10
- stem_link: float32 [16384], P(('gx', 'gy')), may hold values from 1 to 10
- entry_seg: int32 [16384], P(('gx', 'gy')), may hold values from 0 to 127
- source_dev: int32 [16384, 128], P(('gx', 'gy')), may hold values from 0 to 127, as said below
- source_slot: int32 [16384, 128], P(('gx', 'gy')), may hold values from 0 to 1023
- demand: float32 [2048], P(('gx', 'gy')), may hold values from 16 to 128
Outputs:
- head_end: float32 [32, 256, 512], P(None, 'gx', 'gy')
- collar_head: float32 [2048], P(('gx', 'gy'))
Inputs may be any that keep to these rules, and one draw needn't show every extreme that they name: source_dev[b, i] is the device o = b // 128 that holds the block, or one of the eight devices whose tile coordinates differ from o's by at most 1 in each direction, periodically.
All inputs are finite; a program needn't handle non-finite values. No bound on the sum of `wet_flag` on one device may be relied on, other than what follows from the above.
Results may differ from a plain program's by a relative error of at most 0.0003.
Values sent between devices are 32-bit elements; how exact they have to be, the bound alone decides.
No kernel may reach another device: no remote copies, remote signals or barrier semaphores. Data moves between devices by JAX's collectives and lax.ppermute only.
A program may use at most 64 MiB of HBM per device.

v0:
```python
import jax
import jax.numpy as jnp
from jax import lax
from jax.sharding import PartitionSpec as P

PICARD = 2


PORE_INDEX = 1.6
PORE_POWER = 0.375
SPAN_THETA = 0.35
STORAGE = 0.01
TIME_STEP = 1.0
SINK_GAIN = 4.0


def with_halo(x, sides, width):
    for axis, dim in sides:
        size, length = (lax.axis_size(axis), x.shape[dim])
        up = [(i, (i + 1) % size) for i in range(size)]
        down = [(j, i) for i, j in up]
        last = lax.slice_in_dim(x, length - width, length, axis=dim)
        leading = lax.slice_in_dim(x, 0, width, axis=dim)
        before = lax.ppermute(last, axis, up)
        after = lax.ppermute(leading, axis, down)
        x = jnp.concatenate([before, x, after], axis=dim)
    return x


def conduct(head_now, sat_conduct, alpha):
    saturation = (1.0 + (alpha * jnp.abs(head_now)) ** PORE_INDEX) ** (-PORE_POWER)
    inner = 1.0 - (1.0 - saturation ** (1.0 / PORE_POWER)) ** PORE_POWER
    return sat_conduct * jnp.sqrt(saturation) * inner * inner


def capacity(head_now, alpha_dry, wetting, reversal_head):
    alpha = alpha_dry * (1.0 + wetting)
    scaled = alpha * jnp.abs(head_now)
    slope = (
        PORE_POWER
        * PORE_INDEX
        * alpha
        * scaled ** (PORE_INDEX - 1.0)
        * (1.0 + scaled**PORE_INDEX) ** (-PORE_POWER - 1.0)
    )
    drying_rev = (1.0 + (alpha_dry * jnp.abs(reversal_head)) ** PORE_INDEX) ** (-PORE_POWER)
    wetting_rev = (1.0 + (2.0 * alpha_dry * jnp.abs(reversal_head)) ** PORE_INDEX) ** (-PORE_POWER)
    factor = wetting * drying_rev / wetting_rev + (1.0 - wetting)
    return SPAN_THETA * factor * slope + STORAGE


def shifted(array, offset_x, offset_y):
    return array[
        :,
        1 + offset_x : array.shape[1] - 1 + offset_x,
        1 + offset_y : array.shape[2] - 1 + offset_y,
    ]


def update(head_pad, cond_pad, capacity_now, head_old, sink_field):
    head_mid = shifted(head_pad, 0, 0)
    cond_mid = shifted(cond_pad, 0, 0)
    numerator = capacity_now * head_old / TIME_STEP
    denominator = capacity_now / TIME_STEP
    for offset in ((1, 0), (-1, 0), (0, 1), (0, -1)):
        face = 0.5 * (cond_mid + shifted(cond_pad, offset[0], offset[1]))
        numerator = numerator + face * shifted(head_pad, offset[0], offset[1])
        denominator = denominator + face
    face_vert = 0.5 * (cond_mid[1:] + cond_mid[:-1])
    no_face = jnp.zeros_like(cond_mid[:1])
    numerator = numerator + jnp.concatenate([no_face, face_vert * (head_mid[:-1] + 1.0)], 0)
    numerator = numerator + jnp.concatenate([face_vert * (head_mid[1:] - 1.0), no_face], 0)
    denominator = (
        denominator
        + jnp.concatenate([no_face, face_vert], 0)
        + jnp.concatenate([face_vert, no_face], 0)
    )
    numerator = numerator - jnp.concatenate([jnp.zeros_like(cond_mid[:-1]), cond_mid[-1:]], 0)
    return (numerator - SINK_GAIN * sink_field) / denominator


def moved_down(values, stride, fill):
    return jnp.concatenate(
        [jnp.full_like(values[:, :stride], fill), values[:, : values.shape[1] - stride]], 1
    )


def moved_up(values, stride, fill):
    return jnp.concatenate([values[:, stride:], jnp.full_like(values[:, :stride], fill)], 1)


def reduce_solve(lower, diagonal, upper, first_rhs, second_rhs):
    length = diagonal.shape[1]
    stride = 1
    while stride < length:
        factor_low = -lower / moved_down(diagonal, stride, 1.0)
        factor_high = -upper / moved_up(diagonal, stride, 1.0)
        new_diagonal = (
            diagonal
            + factor_low * moved_down(upper, stride, 0.0)
            + factor_high * moved_up(lower, stride, 0.0)
        )
        first_rhs = (
            first_rhs
            + factor_low * moved_down(first_rhs, stride, 0.0)
            + factor_high * moved_up(first_rhs, stride, 0.0)
        )
        second_rhs = (
            second_rhs
            + factor_low * moved_down(second_rhs, stride, 0.0)
            + factor_high * moved_up(second_rhs, stride, 0.0)
        )
        lower = factor_low * moved_down(lower, stride, 0.0)
        upper = factor_high * moved_up(upper, stride, 0.0)
        diagonal = new_diagonal
        stride = stride * 2
    return (first_rhs / diagonal, second_rhs / diagonal)


def root_uptake(
    head_seg, cond_seg, root_radial, root_axial, stem_link, entry_seg, demand, plant_blocks
):
    radial = root_radial * cond_seg / (root_radial + cond_seg)
    axial_link = root_axial[:, :-1]
    no_link = jnp.zeros_like(root_axial[:, :1])
    left_link = jnp.concatenate([no_link, axial_link], 1)
    right_link = jnp.concatenate([axial_link, no_link], 1)
    position = lax.broadcasted_iota(jnp.int32, root_radial.shape, 1)
    collar_link = jnp.where(
        position == entry_seg[:, None], stem_link[:, None], jnp.zeros_like(root_radial)
    )
    diagonal = radial + collar_link + left_link + right_link
    free_part, collar_part = reduce_solve(
        -left_link, diagonal, -right_link, radial * head_seg, collar_link
    )
    base_uptake = jnp.sum(radial * (head_seg - free_part), 1).reshape(-1, plant_blocks).sum(1)
    response = jnp.sum(radial * collar_part, 1).reshape(-1, plant_blocks).sum(1)
    collar_head = (base_uptake - demand) / response
    xylem = free_part + jnp.repeat(collar_head, plant_blocks)[:, None] * collar_part
    return (radial * (head_seg - xylem), collar_head)


def on_device(
    head_start,
    sat_conduct,
    alpha_dry,
    wet_flag,
    reversal_head,
    send_row,
    send_col,
    root_radial,
    root_axial,
    stem_link,
    entry_seg,
    source_dev,
    source_slot,
    demand,
):
    wetting = wet_flag.astype(jnp.float32)
    alpha_eff = alpha_dry * (1.0 + wetting)
    tile_cols = head_start.shape[2]
    rows_gx = lax.axis_size("gx")
    cols_gy = lax.axis_size("gy")
    slot_count = send_row.shape[2]
    plant_blocks = root_radial.shape[0] // demand.shape[0]
    owner_x = lax.axis_index("gx")
    owner_y = lax.axis_index("gy")
    offset_k = (owner_x - source_dev // cols_gy + 1) % rows_gx * 3 + (
        owner_y - source_dev % cols_gy + 1
    ) % cols_gy
    cell_index = (send_row[0] * tile_cols + send_col[0]).reshape(-1)
    slot_index = (offset_k * slot_count + source_slot).reshape(-1)
    head_now = head_start
    collar_head = None
    for iteration in range(PICARD):
        conduct_now = conduct(head_now, sat_conduct, alpha_eff)
        stacked = with_halo(jnp.stack((head_now, conduct_now)), (("gx", 2), ("gy", 3)), 1)
        head_pad = stacked[0]
        cond_pad = stacked[1]
        capacity_now = capacity(head_now, alpha_dry, wetting, reversal_head)
        outgoing = jnp.stack(
            (head_now.reshape(-1)[cell_index], conduct_now.reshape(-1)[cell_index])
        ).reshape(2, 3, 3, slot_count)
        padded = with_halo(outgoing, (("gx", 1), ("gy", 2)), 1)
        received = padded[:, 4::-2, 4::-2]
        received = received.reshape(2, 9 * slot_count)
        head_seg = received[0][slot_index].reshape(root_radial.shape)
        cond_seg = received[1][slot_index].reshape(root_radial.shape)
        uptake, collar_head = root_uptake(
            head_seg, cond_seg, root_radial, root_axial, stem_link, entry_seg, demand, plant_blocks
        )
        per_slot = (
            jnp.zeros((9 * slot_count,), jnp.float32)
            .at[slot_index]
            .add(uptake.reshape(-1))
            .reshape(3, 3, slot_count)
        )
        padded_back = with_halo(per_slot[::-1, ::-1], (("gx", 0), ("gy", 1)), 1)
        returned = padded_back[0::2, 0::2]
        sink_field = (
            jnp.zeros((head_now.size,), jnp.float32)
            .at[cell_index]
            .add(returned.reshape(-1))
            .reshape(head_now.shape)
        )
        head_now = update(head_pad, cond_pad, capacity_now, head_start, sink_field)
    return (head_now, collar_head)


def solution(mesh):
    placed = (
        P(None, "gx", "gy"),
        P(None, "gx", "gy"),
        P(None, "gx", "gy"),
        P(None, "gx", "gy"),
        P(None, "gx", "gy"),
        P(("gx", "gy"), None, None),
        P(("gx", "gy"), None, None),
        P(("gx", "gy"), None),
        P(("gx", "gy"), None),
        P(("gx", "gy")),
        P(("gx", "gy")),
        P(("gx", "gy"), None),
        P(("gx", "gy"), None),
        P(("gx", "gy")),
    )
    return jax.shard_map(
        on_device,
        mesh=mesh,
        in_specs=placed,
        out_specs=(P(None, "gx", "gy"), P(("gx", "gy"))),
        check_vma=False,
    )
```

profile of v0, /device:TPU:0, one launch (start us, length us, event | category | flops | bytes accessed | tf_op | source)
XLA Modules:
  0.0 936.0 jit_solution(5055490089248073649)
XLA Ops:
  1.6 51.2 %gather_fusion = f32[9216]{0:T(1024)S(1)} fusion(f32[32768]{0:T(1024)S(1)} %bitcast.76, s32[9216]{0:T(1024)S(1)} %broadcast_clamp_fusion.1), kind=kCustom, calls=%fused_computation | custom fusion | bytes 110592 | tf_op jit(solution)/shard_map/gather | solution.py:182
  54.0 51.2 %gather_fusion.1 = f32[9216]{0:T(1024)S(1)} fusion(f32[32768]{0:T(1024)S(1)} %get-tuple-element.76, s32[9216]{0:T(1024)S(1)} %broadcast_clamp_fusion.1), kind=kCustom, calls=%fused_computation.1 | custom fusion | bytes 110592 | tf_op jit(solution)/shard_map/gather | solution.py:182
  105.4 5.1 collective-permute-start.5
  110.9 5.1 collective-permute-start.1
  119.9 2.2 collective-permute-start.3
  122.3 3.2 collective-permute-start.7
  125.5 4.0 collective-permute-done.2
  131.5 90.5 %gather_fusion.2 = f32[16384]{0:T(1024)S(1)} fusion(f32[9216]{0:T(1024)S(1)} %squeeze.28, s32[16384]{0:T(1024)S(1)} %broadcast_clamp_fusion), kind=kCustom, calls=%fused_computation.2 | custom fusion | bytes 196608 | tf_op jit(solution)/shard_map/gather | solution.py:188
  222.1 90.5 %gather_fusion.3 = f32[16384]{0:T(1024)S(1)} fusion(f32[9216]{0:T(1024)S(1)} %squeeze.29, s32[16384]{0:T(1024)S(1)} %broadcast_clamp_fusion), kind=kCustom, calls=%fused_computation.3 | custom fusion | bytes 196608 | tf_op jit(solution)/shard_map/gather | solution.py:187
  319.4 86.2 %scatter_custom_fusion = f32[9216]{0:T(1024)S(1)} fusion(s32[16384]{0:T(1024)S(1)} %bitcast.93, f32[16384]{0:T(1024)S(1)} %fusion.56, f32[]{:T(128)} %constant.47.clone.1), kind=kCustom, calls=%fused_computation.265 | custom fusion | flops 16384 | bytes 36868 | tf_op jit(solution)/shard_map/scatter-add | solution.py:195
  406.0 4.7 collective-permute-start.9
  412.2 5.0 collective-permute-done.8
  423.2 48.6 %scatter_custom_fusion.1 = f32[32768]{0:T(1024)S(1)} fusion(s32[9216]{0:T(1024)S(1)} %bitcast.97, f32[9216]{0:T(1024)S(1)} %reshape.277, f32[]{:T(128)} %constant.47.clone.1), kind=kCustom, calls=%fused_computation.236 | custom fusion | flops 9216 | bytes 131076 | tf_op jit(solution)/shard_map/scatter-add | solution.py:203
  472.9 51.2 %gather_fusion.5 = f32[9216]{0:T(1024)S(1)} fusion(f32[32768]{0:T(1024)S(1)} %get-tuple-element.40, s32[9216]{0:T(1024)S(1)} %broadcast_clamp_fusion.1), kind=kCustom, calls=%fused_computation.5 | custom fusion | bytes 110592 | tf_op jit(solution)/shard_map/gather | solution.py:182
  524.4 51.2 %gather_fusion.4 = f32[9216]{0:T(1024)S(1)} fusion(f32[32768]{0:T(1024)S(1)} %bitcast.80, s32[9216]{0:T(1024)S(1)} %broadcast_clamp_fusion.1), kind=kCustom, calls=%fused_computation.4 | custom fusion | bytes 110592 | tf_op jit(solution)/shard_map/gather | solution.py:182
  575.8 5.1 collective-permute-start.13
  581.0 5.1 collective-permute-start.17
  590.2 2.8 collective-permute-start.19
  593.0 4.4 collective-permute-done.14
  599.2 90.5 %gather_fusion.6 = f32[16384]{0:T(1024)S(1)} fusion(f32[9216]{0:T(1024)S(1)} %squeeze.32, s32[16384]{0:T(1024)S(1)} %broadcast_clamp_fusion), kind=kCustom, calls=%fused_computation.6 | custom fusion | bytes 196608 | tf_op jit(solution)/shard_map/gather | solution.py:188
  690.1 90.5 %gather_fusion.7 = f32[16384]{0:T(1024)S(1)} fusion(f32[9216]{0:T(1024)S(1)} %squeeze.33, s32[16384]{0:T(1024)S(1)} %broadcast_clamp_fusion), kind=kCustom, calls=%fused_computation.7 | custom fusion | bytes 196608 | tf_op jit(solution)/shard_map/gather | solution.py:187
  786.3 86.2 %scatter_custom_fusion.2 = f32[9216]{0:T(1024)S(1)} fusion(s32[16384]{0:T(1024)S(1)} %bitcast.94, f32[16384]{0:T(1024)S(1)} %fusion.51, f32[]{:T(128)} %constant.47.clone.1), kind=kCustom, calls=%fused_computation.263 | custom fusion | flops 16384 | bytes 36868 | tf_op jit(solution)/shard_map/scatter-add | solution.py:195
  875.5 5.0 collective-permute-done.20
  886.0 48.6 %scatter_custom_fusion.3 = f32[32768]{0:T(1024)S(1)} fusion(s32[9216]{0:T(1024)S(1)} %bitcast.98, f32[9216]{0:T(1024)S(1)} %reshape.293, f32[]{:T(128)} %constant.47.clone.1), kind=kCustom, calls=%fused_computation.234 | custom fusion | flops 9216 | bytes 131076 | tf_op jit(solution)/shard_map/scatter-add | solution.py:203
  (248 shorter events, 46.4 us)
Async XLA Ops:
  105.3 16.9 %collective-permute-start.4 = (f32[2,1,3,1024]{3,2,1,0:T(4,128)S(1)}, f32[2,1,3,1024]{3,2,1,0:T(4,128)S(1)}, u32[]{:S(2)}, u32[]{:S(2)}) collective-permute-start(f32[2,1,3,1024]{3,2,1,0:T(4,128)S(1)} %get-tuple-element.114), channel_id=1, source_target_pairs={{0,4},{4,8},{8,12},{12,16},{16,20},{20,24},{24,28},{28,32},{32,36}... | collective-permute-start | bytes 73736 | tf_op jit(solution)/shard_map/ppermute | solution.py:24
  105.4 16.8 %collective-permute-start.5 = (f32[2,1,3,1024]{3,2,1,0:T(4,128)S(1)}, f32[2,1,3,1024]{3,2,1,0:T(4,128)S(1)}, u32[]{:S(2)}, u32[]{:S(2)}) collective-permute-start(f32[2,1,3,1024]{3,2,1,0:T(4,128)S(1)} %get-tuple-element.115), channel_id=1, source_target_pairs={{4,0},{8,4},{12,8},{16,12},{20,16},{24,20},{28,24},{32,28},{36,32}... | collective-permute-start | bytes 73736 | tf_op jit(solution)/shard_map/ppermute | solution.py:25
  110.8 6.7 collective-permute-start
  110.9 6.7 collective-permute-start.1
  117.9 11.7 %collective-permute-start.2 = (f32[2,32,10,1]{3,2,1,0:T(8,128)S(1)}, f32[2,32,10,1]{3,2,1,0:T(8,128)S(1)}, u32[]{:S(2)}, u32[]{:S(2)}) collective-permute-start(f32[2,32,10,1]{3,2,1,0:T(8,128)S(1)} %get-tuple-element.84), channel_id=1, source_target_pairs={{0,1},{1,2},{2,3},{3,0},{4,5},{5,6},{6,7},{7,4},{8,9},{9,10},{10,1... | collective-permute-start | bytes 7688 | tf_op jit(solution)/shard_map/ppermute | solution.py:24
  119.9 9.6 %collective-permute-start.3 = (f32[2,32,10,1]{3,2,1,0:T(8,128)S(1)}, f32[2,32,10,1]{3,2,1,0:T(8,128)S(1)}, u32[]{:S(2)}, u32[]{:S(2)}) collective-permute-start(f32[2,32,10,1]{3,2,1,0:T(8,128)S(1)} %get-tuple-element.85), channel_id=1, source_target_pairs={{1,0},{2,1},{3,2},{0,3},{5,4},{6,5},{7,6},{4,7},{9,8},{10,9},{11,1... | collective-permute-start | bytes 7688 | tf_op jit(solution)/shard_map/ppermute | solution.py:25
  122.2 8.2 collective-permute-start.6
  122.3 8.1 collective-permute-start.7
  406.0 6.1 collective-permute-start.9
  410.7 6.5 collective-permute-start.8
  417.3 5.1 collective-permute-start.10
  419.1 3.8 collective-permute-start.11
  575.7 10.3 %collective-permute-start.12 = (f32[2,32,1,128]{3,2,1,0:T(1,128)S(1)}, f32[2,32,1,128]{3,2,1,0:T(1,128)S(1)}, u32[]{:S(2)}, u32[]{:S(2)}) collective-permute-start(f32[2,32,1,128]{3,2,1,0:T(1,128)S(1)} %get-tuple-element.86), channel_id=1, source_target_pairs={{0,4},{4,8},{8,12},{12,16},{16,20},{20,24},{24,28},{28,32},{32,36}... | collective-permute-start | bytes 98312 | tf_op jit(solution)/shard_map/ppermute | solution.py:24
  575.8 10.2 %collective-permute-start.13 = (f32[2,32,1,128]{3,2,1,0:T(1,128)S(1)}, f32[2,32,1,128]{3,2,1,0:T(1,128)S(1)}, u32[]{:S(2)}, u32[]{:S(2)}) collective-permute-start(f32[2,32,1,128]{3,2,1,0:T(1,128)S(1)} %get-tuple-element.87), channel_id=1, source_target_pairs={{4,0},{8,4},{12,8},{16,12},{20,16},{24,20},{28,24},{32,28},{36,32}... | collective-permute-start | bytes 98312 | tf_op jit(solution)/shard_map/ppermute | solution.py:25
  580.9 8.8 collective-permute-start.16
  581.0 8.7 collective-permute-start.17
  586.3 11.1 %collective-permute-start.14 = (f32[2,32,10,1]{3,2,1,0:T(8,128)S(1)}, f32[2,32,10,1]{3,2,1,0:T(8,128)S(1)}, u32[]{:S(2)}, u32[]{:S(2)}) collective-permute-start(f32[2,32,10,1]{3,2,1,0:T(8,128)S(1)} %get-tuple-element.82), channel_id=1, source_target_pairs={{0,1},{1,2},{2,3},{3,0},{4,5},{5,6},{6,7},{7,4},{8,9},{9,10},{10,1... | collective-permute-start | bytes 7688 | tf_op jit(solution)/shard_map/ppermute | solution.py:24
  588.1 9.5 %collective-permute-start.15 = (f32[2,32,10,1]{3,2,1,0:T(8,128)S(1)}, f32[2,32,10,1]{3,2,1,0:T(8,128)S(1)}, u32[]{:S(2)}, u32[]{:S(2)}) collective-permute-start(f32[2,32,10,1]{3,2,1,0:T(8,128)S(1)} %get-tuple-element.83), channel_id=1, source_target_pairs={{1,0},{2,1},{3,2},{0,3},{5,4},{6,5},{7,6},{4,7},{9,8},{10,9},{11,1... | collective-permute-start | bytes 7688 | tf_op jit(solution)/shard_map/ppermute | solution.py:25
  589.7 8.7 collective-permute-start.18
  590.2 8.2 collective-permute-start.19
  873.0 2.5 collective-permute-start.21
  874.1 6.5 collective-permute-start.20
  880.6 5.1 collective-permute-start.22
  881.9 3.8 collective-permute-start.23
  (14 other events, 258.4 us)
where the time goes:
time: 936 us
  local copies, waits for them, and re-layouts  580 us (62%)
  other arithmetic  282 us (30%)
  starting transfers between devices  47.2 us (5%)
  waiting for transfers between devices  25.6 us (3%)
    gather x2, local copies, waits for them, and re-layouts, on_device(): head_seg = received[0][slot_index].reshape(root_radial.shape)  181 us
    gather x2, local copies, waits for them, and re-layouts, on_device(): cond_seg = received[1][slot_index].reshape(root_radial.shape)  181 us
    scatter-add x2, other arithmetic, on_device(): per_slot = jnp.zeros((9 * slot_count,), jnp.float32).at[slot_index].add(u...  172 us
    gather x2, local copies, waits for them, and re-layouts, on_device(): head_now.reshape(-1)[cell_index]  102 us
    gather x2, local copies, waits for them, and re-layouts, on_device(): conduct_now.reshape(-1)[cell_index]  102 us
    scatter-add x2, other arithmetic, on_device(): sink_field = jnp.zeros((head_now.size,), jnp.float32).at[cell_index].add(...  97.1 us
    ppermute x12, starting transfers between devices, with_halo(): after = lax.ppermute(leading, axis, down)  39.4 us
    ppermute x12, waiting for transfers between devices, with_halo(): before = lax.ppermute(last, axis, up)  22.9 us
  transfers between devices with their start and end apart: 24, of which 11 were waited for; matrix products, arithmetic and copies ran while one was open for 0% of the time, Pallas kernels for 0%

commit v1 on v0

v1 whole, which is shorter than its diff:
```python
import jax
import jax.numpy as jnp
from jax import lax
from jax.experimental import pallas as pl
from jax.experimental.pallas import tpu as pltpu
from jax.sharding import PartitionSpec as P

PICARD = 2
PORE_INDEX = 1.6
PORE_POWER = 0.375
SPAN_THETA = 0.35
STORAGE = 0.01
SINK_GAIN = 4.0

F32, BF16, I32 = (jnp.float32, jnp.bfloat16, jnp.int32)
VMEM_LIMIT = 48 * 2**20
LAYERS, CELLS, LANES, SLOTS, BLOCKS, PLANTS = (32, 256, 128, 72, 128, 16)


def split(x):
    hi = x.astype(BF16)
    return (hi, (x - hi.astype(F32)).astype(BF16))


def conduct(head, sat_conduct, alpha):
    power = jnp.exp(PORE_INDEX * jnp.log(alpha * jnp.abs(head)))
    root = jnp.exp((-0.5 * PORE_POWER) * jnp.log(1.0 + power))
    inner = 1.0 - jnp.exp(-PORE_POWER * jnp.log(1.0 + 1.0 / power))
    return sat_conduct * root * inner * inner


def capacity(head, alpha_dry, wetting, reversal_head):
    alpha = alpha_dry * (1.0 + wetting)
    log_scaled = jnp.log(alpha * jnp.abs(head))
    log_term = jnp.log(1.0 + jnp.exp(PORE_INDEX * log_scaled))
    slope = (
        (PORE_POWER * PORE_INDEX)
        * alpha
        * jnp.exp((PORE_INDEX - 1.0) * log_scaled + (-PORE_POWER - 1.0) * log_term)
    )
    turned = jnp.exp(PORE_INDEX * jnp.log(alpha_dry * jnp.abs(reversal_head)))
    ratio = jnp.exp(PORE_POWER * (jnp.log(1.0 + 2.0**PORE_INDEX * turned) - jnp.log(1.0 + turned)))
    factor = wetting * ratio + (1.0 - wetting)
    return SPAN_THETA * factor * slope + STORAGE


def gather_cells(head, cond, row, col, weight, minus, here, plus, edge_minus, edge_plus):
    for field, ref in enumerate((head, cond)):
        for half in range(2):
            turned = ref[half * 128 : half * 128 + 128, :].T
            edge_minus[field * 2 + half : field * 2 + half + 1, :] = turned[0:1]
            edge_plus[field * 2 + half : field * 2 + half + 1, :] = turned[127:128]
            hi, lo = split(turned)
            weight[field * 128 : field * 128 + 128, half * 128 : half * 128 + 128] = hi
            weight[field * 128 : field * 128 + 128, 256 + half * 128 : 384 + half * 128] = lo
        minus[48 + 32 * field : 80 + 32 * field, :] = ref[pl.ds(0, LAYERS, stride=8), :]
        plus[48 + 32 * field : 80 + 32 * field, :] = ref[pl.ds(7, LAYERS, stride=8), :]
    edge_minus[4:8, :] = jnp.zeros((4, LANES), F32)
    edge_plus[4:8, :] = jnp.zeros((4, LANES), F32)
    cells = lax.broadcasted_iota(I32, (CELLS, LANES), 0).astype(F32).astype(BF16)
    columns = lax.broadcasted_iota(I32, (LANES, LANES), 0)
    one, zero = (jnp.ones((), BF16), jnp.zeros((), BF16))
    for j in range(0, SLOTS, 2):
        picks = []
        for i in (j, j + 1):
            wanted = jnp.broadcast_to(row[i : i + 1, :].astype(F32).astype(BF16), (CELLS, LANES))
            picks.append(jnp.where(cells == wanted, one, zero))
        pick = jnp.concatenate(picks, 1)
        got = lax.dot_general(
            weight[...],
            jnp.concatenate([pick, pick], 0),
            (((1,), (0,)), ((), ())),
            preferred_element_type=F32,
        )
        for n, i in enumerate((j, j + 1)):
            k, chunk = divmod(i, 8)
            out = (minus, here, plus)[k // 3]
            mask = columns == col[i : i + 1, :]
            for field in range(2):
                part = got[field * 128 : field * 128 + 128, n * 128 : n * 128 + 128]
                at = k % 3 * 16 + field * 8 + chunk
                out[at : at + 1, :] = jnp.sum(jnp.where(mask, part, 0.0), 0, keepdims=True)


def start_kernel(
    head, sat, alpha_dry, wet, send_row, send_col,
    cond, row, col, minus, here, plus, edge_minus, edge_plus, weight,
):
    for k in range(9):
        for chunk in range(8):
            at = k * 8 + chunk
            row[at : at + 1, :] = send_row[k : k + 1, chunk * 128 : chunk * 128 + 128]
            col[at : at + 1, :] = send_col[k : k + 1, chunk * 128 : chunk * 128 + 128]
    for layer in range(LAYERS):
        at = slice(layer * 8, layer * 8 + 8)
        cond[at, :] = conduct(head[at, :], sat[at, :], alpha_dry[at, :] * (1.0 + wet[at, :].astype(F32)))
    gather_cells(head, cond, row, col, weight, minus, here, plus, edge_minus, edge_plus)


def terms_kernel(
    head, cond, head_old, alpha_dry, wet, reversal, from_minus, from_plus, side_minus, side_plus,
    numerator, denominator, halo,
):
    halo[...] = jnp.zeros_like(halo)
    turned = []
    for i in range(4):
        halo[0:1, :] = side_minus[48 + i : 49 + i, :]
        halo[127:128, :] = side_plus[48 + i : 49 + i, :]
        turned.append(halo[...].T)
    sub = lax.broadcasted_iota(I32, (8, LANES), 0)
    lane = lax.broadcasted_iota(I32, (8, LANES), 1)
    for layer in range(LAYERS):
        at = slice(layer * 8, layer * 8 + 8)
        h, c = (head[at, :], cond[at, :])
        cap = capacity(h, alpha_dry[at, :], wet[at, :].astype(F32), reversal[at, :])
        num, den = (cap * head_old[at, :], cap)
        local = slice(layer % 16 * 8, layer % 16 * 8 + 8)
        halo_h, halo_c = (turned[layer // 16][local], turned[2 + layer // 16][local])

        def add(num, den, near_h, near_c):
            face = 0.5 * (c + near_c)
            return (num + face * near_h, den + face)

        def beside(x, line, spot):
            return jnp.where(sub == spot, jnp.broadcast_to(line, (8, LANES)), x)

        num, den = add(
            num, den,
            beside(pltpu.roll(h, 7, 0), from_plus[48 + layer : 49 + layer, :], 7),
            beside(pltpu.roll(c, 7, 0), from_plus[80 + layer : 81 + layer, :], 7),
        )
        num, den = add(
            num, den,
            beside(pltpu.roll(h, 1, 0), from_minus[48 + layer : 49 + layer, :], 0),
            beside(pltpu.roll(c, 1, 0), from_minus[80 + layer : 81 + layer, :], 0),
        )
        num, den = add(
            num, den,
            jnp.where(lane == 127, halo_h, pltpu.roll(h, 127, 1)),
            jnp.where(lane == 127, halo_c, pltpu.roll(c, 127, 1)),
        )
        num, den = add(
            num, den,
            jnp.where(lane == 0, halo_h, pltpu.roll(h, 1, 1)),
            jnp.where(lane == 0, halo_c, pltpu.roll(c, 1, 1)),
        )
        if layer > 0:
            above = slice(layer * 8 - 8, layer * 8)
            num, den = add(num, den, head[above, :] + 1.0, cond[above, :])
        if layer < LAYERS - 1:
            below = slice(layer * 8 + 8, layer * 8 + 16)
            num, den = add(num, den, head[below, :] - 1.0, cond[below, :])
        else:
            num = num - c
        numerator[at, :] = num
        denominator[at, :] = den


def root_kernel(
    demand, from_minus, here, from_plus, side_minus, side_plus, code, radial_in, axial, stem, entry,
    out_minus, out_here, out_plus, collar_out, weight, table, seg_head, seg_cond, uptake,
):
    for dx in range(3):
        for dy in range(3):
            if dy == 1:
                source, at = ((from_plus, here, from_minus)[dx], 16)
            else:
                source, at = ((side_plus, None, side_minus)[dy], (2 - dx) * 16)
            for field in range(2):
                to = field * 128 + (dx * 3 + dy) * 8
                table[to : to + 8, :] = source[at + field * 8 : at + field * 8 + 8, :]
    for field in range(2):
        table[field * 128 + 72 : field * 128 + 128, :] = jnp.zeros((56, LANES), F32)
        hi, lo = split(table[field * 128 : field * 128 + 128, :].T)
        weight[field * 128 : field * 128 + 128, 0:128] = hi
        weight[field * 128 : field * 128 + 128, 128:256] = lo
    rows = lax.broadcasted_iota(I32, (128, LANES), 0).astype(F32).astype(BF16)
    columns = lax.broadcasted_iota(I32, (LANES, LANES), 0)
    one, zero = (jnp.ones((), BF16), jnp.zeros((), BF16))
    for j in range(0, BLOCKS, 2):
        picks = []
        for i in (j, j + 1):
            wanted = jnp.broadcast_to((code[i : i + 1, :] >> 7).astype(F32).astype(BF16), (128, LANES))
            picks.append(jnp.where(rows == wanted, one, zero))
        pick = jnp.concatenate(picks, 1)
        got = lax.dot_general(
            weight[...],
            jnp.concatenate([pick, pick], 0),
            (((1,), (0,)), ((), ())),
            preferred_element_type=F32,
        )
        for n, i in enumerate((j, j + 1)):
            mask = columns == (code[i : i + 1, :] & 127)
            for field, ref in enumerate((seg_head, seg_cond)):
                part = got[field * 128 : field * 128 + 128, n * 128 : n * 128 + 128]
                ref[i : i + 1, :] = jnp.sum(jnp.where(mask, part, 0.0), 0, keepdims=True)
    group = 32
    lane = lax.broadcasted_iota(I32, (group, LANES), 1)
    plant_row = lax.broadcasted_iota(I32, (group // 8, 1), 0)
    collar_line = jnp.zeros((1, LANES), F32)
    for g in range(BLOCKS // group):
        at = slice(g * group, g * group + group)
        sub = lax.broadcasted_iota(I32, (group, LANES), 0) + g * group
        own = sub == lane
        stem_col = jnp.sum(jnp.where(own, stem[...], 0.0), 1, keepdims=True)
        entry_col = jnp.sum(jnp.where(own, entry[...], 0), 1, keepdims=True)
        hs, ks, rr = (seg_head[at, :], seg_cond[at, :], radial_in[at, :])
        radial = rr * ks / (rr + ks)
        right = jnp.where(lane == 127, 0.0, axial[at, :])
        left = pltpu.roll(right, 1, 1)
        second = jnp.where(lane == entry_col, stem_col, 0.0)
        first = radial * hs
        diagonal = radial + second + left + right
        lower, upper = (-left, -right)
        for step in range(7):
            stride = 2**step
            inverse = 1.0 / diagonal
            low = -lower * pltpu.roll(inverse, stride, 1)
            high = -upper * pltpu.roll(inverse, 128 - stride, 1)
            first, second = (
                x + low * pltpu.roll(x, stride, 1) + high * pltpu.roll(x, 128 - stride, 1)
                for x in (first, second)
            )
            diagonal = diagonal + low * lower + high * upper
            if step < 6:
                lower = low * pltpu.roll(lower, stride, 1)
                upper = high * pltpu.roll(upper, 128 - stride, 1)
        inverse = 1.0 / diagonal
        free, collar = (first * inverse, second * inverse)

        def per_plant(x):
            return jnp.sum(jnp.sum(x.reshape(group // 8, 8, LANES), 1), 1, keepdims=True)

        need = jnp.zeros((group // 8, 1), F32)
        for p in range(group // 8):
            need = jnp.where(plant_row == p, demand[g * (group // 8) + p], need)
        head = (per_plant(radial * (hs - free)) - need) / per_plant(radial * collar)
        spread = jnp.broadcast_to(head[:, None, :], (group // 8, 8, LANES)).reshape(group, LANES)
        uptake[at, :] = radial * (hs - (free + spread * collar))
        mine = lax.broadcasted_iota(I32, (group // 8, LANES), 1) == plant_row + g * (group // 8)
        collar_line = collar_line + jnp.sum(jnp.where(mine, head, 0.0), 0, keepdims=True)
    collar_out[...] = collar_line
    slot_rows = lax.broadcasted_iota(I32, (80, LANES), 0).astype(F32).astype(BF16)
    slot_cols = rows
    total = jnp.zeros((160, LANES), F32)
    for start in range(0, BLOCKS, 8):
        values, places = ([], [])
        for i in range(start, start + 8):
            where = code[i : i + 1, :]
            hi, lo = split(uptake[i : i + 1, :])
            mask = slot_rows == jnp.broadcast_to((where >> 7).astype(F32).astype(BF16), (80, LANES))
            values.append(
                jnp.concatenate(
                    [jnp.where(mask, jnp.broadcast_to(v, (80, LANES)), zero) for v in (hi, lo)], 0
                )
            )
            wanted = jnp.broadcast_to((where & 127).astype(F32).astype(BF16), (128, LANES))
            places.append(jnp.where(slot_cols == wanted, one, zero))
        total = total + lax.dot_general(
            jnp.concatenate(values, 1),
            jnp.concatenate(places, 1),
            (((1,), (1,)), ((), ())),
            preferred_element_type=F32,
        )
    summed = total[0:72] + total[80:152]
    out_minus[...] = summed[0:24]
    out_here[...] = summed[24:48]
    out_plus[...] = summed[48:72]


def sink_of(pieces, row, col):
    low_rows = lax.broadcasted_iota(I32, (128, LANES), 0).astype(F32).astype(BF16)
    places_of = lax.broadcasted_iota(I32, (256, LANES), 0).astype(F32).astype(BF16)
    one, zero = (jnp.ones((), BF16), jnp.zeros((), BF16))
    total = jnp.zeros((256, 256), F32)
    for k in range(9):
        source, base = pieces[k]
        values, places = ([], [])
        for chunk in range(8):
            i = k * 8 + chunk
            r, c = (row[i : i + 1, :], col[i : i + 1, :])
            hi, lo = split(source[base + chunk : base + chunk + 1, :])
            mask = low_rows == jnp.broadcast_to((r & 127).astype(F32).astype(BF16), (128, LANES))
            values.append(
                jnp.concatenate(
                    [jnp.where(mask, jnp.broadcast_to(v, (128, LANES)), zero) for v in (hi, lo)], 0
                )
            )
            wanted = ((r >> 7) * 128 + c).astype(F32).astype(BF16)
            places.append(jnp.where(places_of == jnp.broadcast_to(wanted, (256, LANES)), one, zero))
        total = total + lax.dot_general(
            jnp.concatenate(values, 1),
            jnp.concatenate(places, 1),
            (((1,), (1,)), ((), ())),
            preferred_element_type=F32,
        )
    return total[0:128] + total[128:256]


def new_head(back, row, col, numerator, denominator, head_new):
    from_minus, here, from_plus, side_minus, side_plus = back
    pieces = []
    for dx in range(3):
        for dy in range(3):
            if dy == 1:
                pieces.append(((from_minus, here, from_plus)[dx], 8))
            else:
                pieces.append(((side_minus, None, side_plus)[dy], dx * 8))
    sink = sink_of(pieces, row, col)
    for half in range(2):
        at = slice(half * 128, half * 128 + 128)
        head_new[at, :] = (numerator[at, :] - SINK_GAIN * sink[:, at]) / denominator[at, :]


def next_kernel(
    from_minus, here_in, from_plus, side_minus, side_plus, row, col, numerator, denominator, sat, alpha_dry, wet,
    head, cond, minus, here, plus, edge_minus, edge_plus, weight,
):
    back = (from_minus, here_in, from_plus, side_minus, side_plus)
    new_head(back, row, col, numerator, denominator, head)
    for layer in range(LAYERS):
        at = slice(layer * 8, layer * 8 + 8)
        cond[at, :] = conduct(head[at, :], sat[at, :], alpha_dry[at, :] * (1.0 + wet[at, :].astype(F32)))
    gather_cells(head, cond, row, col, weight, minus, here, plus, edge_minus, edge_plus)


def last_kernel(
    from_minus, here_in, from_plus, side_minus, side_plus, row, col, numerator, denominator, head
):
    back = (from_minus, here_in, from_plus, side_minus, side_plus)
    new_head(back, row, col, numerator, denominator, head)


def call(kernel, outs, scratch=(), specs=None, flops=0, **params):
    shapes = [jax.ShapeDtypeStruct(shape, dtype) for shape, dtype in outs]
    return pl.pallas_call(
        kernel,
        out_shape=shapes,
        scratch_shapes=[pltpu.VMEM(shape, dtype) for shape, dtype in scratch],
        compiler_params=pltpu.CompilerParams(vmem_limit_bytes=VMEM_LIMIT),
        **({} if specs is None else {"in_specs": specs}),
        **params,
    )


MESSAGES = [((112, 128), F32), ((48, 128), F32), ((112, 128), F32), ((8, 128), F32), ((8, 128), F32)]


def up(x, axis):
    size = lax.axis_size(axis)
    return lax.ppermute(x, axis, [(i, (i + 1) % size) for i in range(size)])


def down(x, axis):
    size = lax.axis_size(axis)
    return lax.ppermute(x, axis, [((i + 1) % size, i) for i in range(size)])


def spread(minus, here, plus, edge_minus, edge_plus):
    from_minus = up(plus, "gx")
    from_plus = down(minus, "gx")
    side_minus = up(
        jnp.concatenate([from_minus[32:48], here[32:48], from_plus[32:48], edge_plus], 0), "gy"
    )
    side_plus = down(
        jnp.concatenate([from_minus[0:16], here[0:16], from_plus[0:16], edge_minus], 0), "gy"
    )
    return (from_minus, here, from_plus, side_minus, side_plus)


def give_back(minus, here, plus):
    from_minus = up(minus, "gx")
    from_plus = down(plus, "gx")
    side_plus = down(jnp.concatenate([from_minus[16:24], here[16:24], from_plus[16:24]], 0), "gy")
    side_minus = up(jnp.concatenate([from_minus[0:8], here[0:8], from_plus[0:8]], 0), "gy")
    return (from_minus, here, from_plus, side_minus, side_plus)


def on_device(
    head_start,
    sat_conduct,
    alpha_dry,
    wet_flag,
    reversal_head,
    send_row,
    send_col,
    root_radial,
    root_axial,
    stem_link,
    entry_seg,
    source_dev,
    source_slot,
    demand,
):
    tile = head_start.shape
    head, sat, alpha, wet, reversal = (
        x.reshape(CELLS, LANES) for x in (head_start, sat_conduct, alpha_dry, wet_flag, reversal_head)
    )
    rows_gx = lax.axis_size("gx")
    cols_gy = lax.axis_size("gy")
    offset_k = (lax.axis_index("gx") - source_dev // cols_gy + 1) % rows_gx * 3 + (
        lax.axis_index("gy") - source_dev % cols_gy + 1
    ) % cols_gy
    code = offset_k * send_row.shape[2] + source_slot
    stem, entry = (stem_link.reshape(1, BLOCKS), entry_seg.reshape(1, BLOCKS))
    head_old = head
    cond, row, col, *messages = call(
        start_kernel,
        [((CELLS, LANES), F32), ((SLOTS, LANES), I32), ((SLOTS, LANES), I32)] + MESSAGES,
        [((256, 512), BF16)],
    )(head, sat, alpha, wet, send_row[0], send_col[0])
    smem = [pl.BlockSpec(memory_space=pltpu.SMEM)] + [pl.BlockSpec(memory_space=pltpu.VMEM)] * 10
    for iteration in range(PICARD):
        got = spread(*messages)
        *sums, collar = call(
            root_kernel,
            [((24, 128), F32)] * 3 + [((1, 128), F32)],
            [((256, 256), BF16), ((256, 128), F32)] + [((128, 128), F32)] * 3,
            specs=smem,
        )(demand, *got, code, root_radial, root_axial, stem, entry)
        numerator, denominator = call(
            terms_kernel,
            [((CELLS, LANES), F32)] * 2,
            [((128, 128), F32)],
        )(head, cond, head_old, alpha, wet, reversal, got[0], got[2], got[3], got[4])
        back = give_back(*sums)
        if iteration < PICARD - 1:
            head, cond, *messages = call(
                next_kernel,
                [((CELLS, LANES), F32)] * 2 + MESSAGES,
                [((256, 512), BF16)],
            )(*back, row, col, numerator, denominator, sat, alpha, wet)
        else:
            (head,) = call(last_kernel, [((CELLS, LANES), F32)])(
                *back, row, col, numerator, denominator
            )
    return (head.reshape(tile), collar[0, :PLANTS])


def solution(mesh):
    tile, lists, blocks, line = (
        P(None, "gx", "gy"),
        P(("gx", "gy"), None, None),
        P(("gx", "gy"), None),
        P(("gx", "gy")),
    )
    return jax.shard_map(
        on_device,
        mesh=mesh,
        in_specs=(tile,) * 5 + (lists,) * 2 + (blocks,) * 2 + (line,) * 2 + (blocks,) * 2 + (line,),
        out_specs=(tile, line),
        check_vma=False,
    )
```

time: 936 us -> 79.6 us (0.09)
  local copies, waits for them, and re-layouts: 580 us -> 4.87 us
  other arithmetic: 282 us -> 0.16 us
  Pallas kernels: 0 us -> 26 us
  waiting for transfers between devices: 25.6 us -> 12.5 us
  starting transfers between devices: 47.2 us -> 35 us
    gather x8 -> x0, local copies, waits for them, and re-layouts: 567 us -> none  [the longest x2 181 us: on_device(): head_seg = received[0][slot_index].reshape(root_radial.shape)]
    scatter-add x4 -> x0, other arithmetic: 269 us -> none  [the longest x2 172 us: on_device(): per_slot = jnp.zeros((9 * slot_count,), jnp.float32).at[slot_index].add(u...]
    pallas_call x0 -> x7, Pallas kernels: none -> 26 us  [the longest x2 13.1 us: on_device(): call(root_kernel, [((24, 128), F32)] * 3 + [((1, 128), F32)], [((256, 256...]
    ppermute x24 -> x16, waiting for transfers between devices: 25.6 us -> 12.5 us  [the longest x8 11.4 us: up(): return lax.ppermute(x, axis, [(i, (i + 1) % size) for i in range(size)])]
    ppermute x24 -> x16, starting transfers between devices: 47.2 us -> 35 us  [the longest x8 27.8 us: down(): return lax.ppermute(x, axis, [((i + 1) % size, i) for i in range(size)])]
  transfers between devices with their start and end apart: 24 -> 16, of which waited for: 11 -> 11; matrix products, arithmetic and copies ran while one was open for 0% -> 1% of each run, Pallas kernels for 0% -> 1%
where the time goes in v1:
time: 79.6 us; the launch traced here: 79.4 us
  starting transfers between devices  35 us (44%)
  Pallas kernels  26 us (33%)
  waiting for transfers between devices  12.5 us (16%)
  local copies, waits for them, and re-layouts  4.87 us (6%)
  between operations  0.82 us (1%)
    ppermute x8, starting transfers between devices, down(): return lax.ppermute(x, axis, [((i + 1) % size, i) for i in range(size)])  27.8 us
    pallas_call x2, Pallas kernels, on_device(): call(root_kernel, [((24, 128), F32)] * 3 + [((1, 128), F32)], [((256, 256...  13.1 us
    ppermute x8, waiting for transfers between devices, up(): return lax.ppermute(x, axis, [(i, (i + 1) % size) for i in range(size)])  11.4 us
    ppermute x8, starting transfers between devices, up(): return lax.ppermute(x, axis, [(i, (i + 1) % size) for i in range(size)])  7.22 us
    pallas_call x1, Pallas kernels, on_device(): call(next_kernel, [((CELLS, LANES), F32)] * 2 + MESSAGES, [((256, 512), B...  6.77 us
    unnamed x31, local copies, waits for them, and re-layouts  4.33 us
    pallas_call x1, Pallas kernels, on_device(): call(start_kernel, [((CELLS, LANES), F32), ((SLOTS, LANES), I32), ((SLOTS...  3.14 us
    pallas_call x1, Pallas kernels, on_device(): call(last_kernel, [((CELLS, LANES), F32)])  2.08 us
  transfers between devices with their start and end apart: 16, of which 11 were waited for; matrix products, arithmetic and copies ran while one was open for 1% of the time, Pallas kernels for 1%

profile of v1, /device:TPU:0, one launch (start us, length us, event | category | flops | bytes accessed | tf_op | source)
XLA Modules:
  0.0 79.4 jit_solution(17588372849223270567)
XLA Ops:
  2.5 0.9 %copy-done.3 = f32[32,8,128]{2,1,0:T(8,128)S(1)} copy-done((f32[32,8,128]{2,1,0:T(8,128)S(1)}, f32[32,8,128]{2,1,0:T(8,128)}, u32[]{:S(2)}) %copy-start.3) | copy-done | bytes 131096
  4.3 3.1 %shard_map.149 = (f32[256,128]{1,0:T(8,128)S(1)}, s32[72,128]{1,0:T(8,128)S(1)}, s32[72,128]{1,0:T(8,128)S(1)}, f32[112,128]{1,0:T(8,128)S(1)}, f32[48,128]{1,0:...) custom-call(f32[256,128]{1,0:T(8,128)S(1)} %bitcast.22, ...), custom_call_target="tpu_custom_call" | custom-call | tf_op jit(solution)/shard_map/pallas_call | solution.py:407
  7.5 5.1 %collective-permute-start.1 = (f32[112,128]{1,0:T(8,128)S(1)}, f32[112,128]{1,0:T(8,128)S(1)}, u32[]{:S(2)}, u32[]{:S(2)}) collective-permute-start(f32[112,128]{1,0:T(8,128)S(1)} %get-tuple-element.30), channel_id=1, source_target_pairs={{4,0},{8,4},{12,8},{16,12},{20,16},{24,20},{28,24},{32,28},{36,32}... | collective-permute-start | bytes 172040 | tf_op jit(solution)/shard_map/ppermute | solution.py:356
  12.6 1.9 %collective-permute-done.from_minus = f32[112,128]{1,0:T(8,128)S(1)} collective-permute-done((f32[112,128]{1,0:T(8,128)S(1)}, f32[112,128]{1,0:T(8,128)S(1)}, u32[]{:S(2)}, u32[]{:S(2)}) %collective-permute-start) | collective-permute-done | bytes 57376 | tf_op jit(solution)/shard_map/ppermute | solution.py:351
  14.5 2.1 %collective-permute-start.2 = (f32[56,128]{1,0:T(8,128)S(1)}, f32[56,128]{1,0:T(8,128)S(1)}, u32[]{:S(2)}, u32[]{:S(2)}) collective-permute-start(f32[56,128]{1,0:T(8,128)S(1)} %pad_maximum_fusion), channel_id=1, source_target_pairs={{0,1},{1,2},{2,3},{3,0},{4,5},{5,6},{6,7},{7,4},{8,9},{9,10},{10,1... | collective-permute-start | bytes 86024 | tf_op jit(solution)/shard_map/ppermute | solution.py:351
  16.5 2.2 %collective-permute-start.3 = (f32[56,128]{1,0:T(8,128)S(1)}, f32[56,128]{1,0:T(8,128)S(1)}, u32[]{:S(2)}, u32[]{:S(2)}) collective-permute-start(f32[56,128]{1,0:T(8,128)S(1)} %pad_maximum_fusion.1), channel_id=1, source_target_pairs={{1,0},{2,1},{3,2},{0,3},{5,4},{6,5},{7,6},{4,7},{9,8},{10,9},{11,1... | collective-permute-start | bytes 86024 | tf_op jit(solution)/shard_map/ppermute | solution.py:356
  18.9 1.6 %collective-permute-done.2.side_minus = f32[56,128]{1,0:T(8,128)S(1)} collective-permute-done((f32[56,128]{1,0:T(8,128)S(1)}, f32[56,128]{1,0:T(8,128)S(1)}, u32[]{:S(2)}, u32[]{:S(2)}) %collective-permute-start.2) | collective-permute-done | bytes 28704 | tf_op jit(solution)/shard_map/ppermute | solution.py:351
  21.2 6.7 %shard_map.150 = (f32[24,128]{1,0:T(8,128)S(1)}, f32[24,128]{1,0:T(8,128)S(1)}, f32[24,128]{1,0:T(8,128)S(1)}, f32[1,128]{1,0:T(1,128)}) custom-call(f32[16]{0:T(128)S(1)} %copy-done.10, f32[112,128]{1,0:T(8,128)S(1)} %collective-permute-done.from_minus, f32[48,128]{1,0:T(8,128)S(1)} %get-tuple-element.29.here, ...), custom_call_target="tpu_custom_call" | custom-call | tf_op jit(solution)/shard_map/pallas_call | solution.py:415
  27.9 5.1 %collective-permute-start.5 = (f32[24,128]{1,0:T(8,128)S(1)}, f32[24,128]{1,0:T(8,128)S(1)}, u32[]{:S(2)}, u32[]{:S(2)}) collective-permute-start(f32[24,128]{1,0:T(8,128)S(1)} %get-tuple-element.35), channel_id=1, source_target_pairs={{4,0},{8,4},{12,8},{16,12},{20,16},{24,20},{28,24},{32,28},{36,32}... | collective-permute-start | bytes 36872 | tf_op jit(solution)/shard_map/ppermute | solution.py:356
  33.0 1.4 %collective-permute-done.4.from_minus = f32[24,128]{1,0:T(8,128)S(1)} collective-permute-done((f32[24,128]{1,0:T(8,128)S(1)}, f32[24,128]{1,0:T(8,128)S(1)}, u32[]{:S(2)}, u32[]{:S(2)}) %collective-permute-start.4) | collective-permute-done | bytes 12320 | tf_op jit(solution)/shard_map/ppermute | solution.py:351
  34.4 1.9 %collective-permute-start.6 = (f32[24,128]{1,0:T(8,128)S(1)}, f32[24,128]{1,0:T(8,128)S(1)}, u32[]{:S(2)}, u32[]{:S(2)}) collective-permute-start(f32[24,128]{1,0:T(8,128)S(1)} %pad_maximum_fusion.4), channel_id=1, source_target_pairs={{0,1},{1,2},{2,3},{3,0},{4,5},{5,6},{6,7},{7,4},{8,9},{9,10},{10,1... | collective-permute-start | bytes 36872 | tf_op jit(solution)/shard_map/ppermute | solution.py:351
  36.3 1.7 %collective-permute-start.7 = (f32[24,128]{1,0:T(8,128)S(1)}, f32[24,128]{1,0:T(8,128)S(1)}, u32[]{:S(2)}, u32[]{:S(2)}) collective-permute-start(f32[24,128]{1,0:T(8,128)S(1)} %pad_maximum_fusion.5), channel_id=1, source_target_pairs={{1,0},{2,1},{3,2},{0,3},{5,4},{6,5},{7,6},{4,7},{9,8},{10,9},{11,1... | collective-permute-start | bytes 36872 | tf_op jit(solution)/shard_map/ppermute | solution.py:356
  40.0 6.8 %shard_map.152 = (f32[256,128]{1,0:T(8,128)S(1)}, f32[256,128]{1,0:T(8,128)S(1)}, f32[112,128]{1,0:T(8,128)S(1)}, f32[48,128]{1,0:T(8,128)S(1)}, f32[112,128]{1,...) custom-call(f32[24,128]{1,0:T(8,128)S(1)} %collective-permute-done.4.from_minus, ...), custom_call_target="tpu_custom_call" | custom-call | tf_op jit(solution)/shard_map/pallas_call | solution.py:428
  46.9 5.0 %collective-permute-start.9 = (f32[112,128]{1,0:T(8,128)S(1)}, f32[112,128]{1,0:T(8,128)S(1)}, u32[]{:S(2)}, u32[]{:S(2)}) collective-permute-start(f32[112,128]{1,0:T(8,128)S(1)} %get-tuple-element.43), channel_id=1, source_target_pairs={{4,0},{8,4},{12,8},{16,12},{20,16},{24,20},{28,24},{32,28},{36,32}... | collective-permute-start | bytes 172040 | tf_op jit(solution)/shard_map/ppermute | solution.py:356
  51.9 1.9 %collective-permute-done.8.from_minus = f32[112,128]{1,0:T(8,128)S(1)} collective-permute-done((f32[112,128]{1,0:T(8,128)S(1)}, f32[112,128]{1,0:T(8,128)S(1)}, u32[]{:S(2)}, u32[]{:S(2)}) %collective-permute-start.8) | collective-permute-done | bytes 57376 | tf_op jit(solution)/shard_map/ppermute | solution.py:351
  53.8 1.7 %collective-permute-start.10 = (f32[56,128]{1,0:T(8,128)S(1)}, f32[56,128]{1,0:T(8,128)S(1)}, u32[]{:S(2)}, u32[]{:S(2)}) collective-permute-start(f32[56,128]{1,0:T(8,128)S(1)} %pad_maximum_fusion.2), channel_id=1, source_target_pairs={{0,1},{1,2},{2,3},{3,0},{4,5},{5,6},{6,7},{7,4},{8,9},{9,10},{10,1... | collective-permute-start | bytes 86024 | tf_op jit(solution)/shard_map/ppermute | solution.py:351
  55.5 1.6 %collective-permute-start.11 = (f32[56,128]{1,0:T(8,128)S(1)}, f32[56,128]{1,0:T(8,128)S(1)}, u32[]{:S(2)}, u32[]{:S(2)}) collective-permute-start(f32[56,128]{1,0:T(8,128)S(1)} %pad_maximum_fusion.3), channel_id=1, source_target_pairs={{1,0},{2,1},{3,2},{0,3},{5,4},{6,5},{7,6},{4,7},{9,8},{10,9},{11,1... | collective-permute-start | bytes 86024 | tf_op jit(solution)/shard_map/ppermute | solution.py:356
  57.2 1.8 %collective-permute-done.10.side_minus = f32[56,128]{1,0:T(8,128)S(1)} collective-permute-done((f32[56,128]{1,0:T(8,128)S(1)}, f32[56,128]{1,0:T(8,128)S(1)}, u32[]{:S(2)}, u32[]{:S(2)}) %collective-permute-start.10) | collective-permute-done | bytes 28704 | tf_op jit(solution)/shard_map/ppermute | solution.py:351
  59.4 6.4 %shard_map.153 = (f32[24,128]{1,0:T(8,128)S(1)}, f32[24,128]{1,0:T(8,128)S(1)}, f32[24,128]{1,0:T(8,128)S(1)}, f32[1,128]{1,0:T(1,128)S(1)}) custom-call(f32[16]{0:T(128)S(1)} %copy-done.10, f32[112,128]{1,0:T(8,128)S(1)} %collective-permute-done.8.from_minus, f32[48,128]{1,0:T(8,128)S(1)} %get-tuple-element.42.here, ...), custom_call_target="tpu_custom_call" | custom-call | tf_op jit(solution)/shard_map/pallas_call | solution.py:415
  65.9 5.0 %collective-permute-start.13 = (f32[24,128]{1,0:T(8,128)S(1)}, f32[24,128]{1,0:T(8,128)S(1)}, u32[]{:S(2)}, u32[]{:S(2)}) collective-permute-start(f32[24,128]{1,0:T(8,128)S(1)} %get-tuple-element.48), channel_id=1, source_target_pairs={{4,0},{8,4},{12,8},{16,12},{20,16},{24,20},{28,24},{32,28},{36,32}... | collective-permute-start | bytes 36872 | tf_op jit(solution)/shard_map/ppermute | solution.py:356
  70.9 1.4 %collective-permute-done.12.from_minus = f32[24,128]{1,0:T(8,128)S(1)} collective-permute-done((f32[24,128]{1,0:T(8,128)S(1)}, f32[24,128]{1,0:T(8,128)S(1)}, u32[]{:S(2)}, u32[]{:S(2)}) %collective-permute-start.12) | collective-permute-done | bytes 12320 | tf_op jit(solution)/shard_map/ppermute | solution.py:351
  72.3 1.3 %collective-permute-start.14 = (f32[24,128]{1,0:T(8,128)S(1)}, f32[24,128]{1,0:T(8,128)S(1)}, u32[]{:S(2)}, u32[]{:S(2)}) collective-permute-start(f32[24,128]{1,0:T(8,128)S(1)} %pad_maximum_fusion.6), channel_id=1, source_target_pairs={{0,1},{1,2},{2,3},{3,0},{4,5},{5,6},{6,7},{7,4},{8,9},{9,10},{10,1... | collective-permute-start | bytes 36872 | tf_op jit(solution)/shard_map/ppermute | solution.py:351
  73.7 2.0 %collective-permute-start.15 = (f32[24,128]{1,0:T(8,128)S(1)}, f32[24,128]{1,0:T(8,128)S(1)}, u32[]{:S(2)}, u32[]{:S(2)}) collective-permute-start(f32[24,128]{1,0:T(8,128)S(1)} %pad_maximum_fusion.7), channel_id=1, source_target_pairs={{1,0},{2,1},{3,2},{0,3},{5,4},{6,5},{7,6},{4,7},{9,8},{10,9},{11,1... | collective-permute-start | bytes 36872 | tf_op jit(solution)/shard_map/ppermute | solution.py:356
  77.3 2.1 %shard_map.155 = f32[256,128]{1,0:T(8,128)} custom-call(f32[24,128]{1,0:T(8,128)S(1)} %collective-permute-done.12.from_minus, f32[24,128]{1,0:T(8,128)S(1)} %get-tuple-element.47.here_in, f32[24,128]{1,0:T(8,128)S(1)} %collective-permute-done.13.from_plus, f32[24,128]{1,0:T(8,128)S(1)} %collective-permute-done.14.side_minus, ...), custom_call_target="tpu_custom_call" | custom-call | tf_op jit(solution)/shard_map/pallas_call | solution.py:434
  (68 shorter events, 8.0 us)
Async XLA Ops:
  7.4 7.0 %collective-permute-start = (f32[112,128]{1,0:T(8,128)S(1)}, f32[112,128]{1,0:T(8,128)S(1)}, u32[]{:S(2)}, u32[]{:S(2)}) collective-permute-start(f32[112,128]{1,0:T(8,128)S(1)} %get-tuple-element.28), channel_id=1, source_target_pairs={{0,4},{4,8},{8,12},{12,16},{16,20},{20,24},{24,28},{28,32},{32,36}... | collective-permute-start | bytes 172040 | tf_op jit(solution)/shard_map/ppermute | solution.py:351
  7.5 6.9 %collective-permute-start.1 = (f32[112,128]{1,0:T(8,128)S(1)}, f32[112,128]{1,0:T(8,128)S(1)}, u32[]{:S(2)}, u32[]{:S(2)}) collective-permute-start(f32[112,128]{1,0:T(8,128)S(1)} %get-tuple-element.30), channel_id=1, source_target_pairs={{4,0},{8,4},{12,8},{16,12},{20,16},{24,20},{28,24},{32,28},{36,32}... | collective-permute-start | bytes 172040 | tf_op jit(solution)/shard_map/ppermute | solution.py:356
  14.4 4.4 %copy-start.14 = (s32[128,128]{1,0:T(8,128)S(1)}, s32[128,128]{1,0:T(8,128)}, u32[]{:S(2)}) copy-start(s32[128,128]{1,0:T(8,128)} %param.25) | copy-start | bytes 196612
  14.4 4.3 %copy-start.13 = (s32[128,128]{1,0:T(8,128)S(1)}, s32[128,128]{1,0:T(8,128)}, u32[]{:S(2)}) copy-start(s32[128,128]{1,0:T(8,128)} %param.26) | copy-start | bytes 196612
  14.5 6.0 %collective-permute-start.2 = (f32[56,128]{1,0:T(8,128)S(1)}, f32[56,128]{1,0:T(8,128)S(1)}, u32[]{:S(2)}, u32[]{:S(2)}) collective-permute-start(f32[56,128]{1,0:T(8,128)S(1)} %pad_maximum_fusion), channel_id=1, source_target_pairs={{0,1},{1,2},{2,3},{3,0},{4,5},{5,6},{6,7},{7,4},{8,9},{9,10},{10,1... | collective-permute-start | bytes 86024 | tf_op jit(solution)/shard_map/ppermute | solution.py:351
  16.5 4.0 %copy-start.8 = (f32[128,128]{1,0:T(8,128)S(1)}, f32[128,128]{1,0:T(8,128)}, u32[]{:S(2)}) copy-start(f32[128,128]{1,0:T(8,128)} %radial_in.3) | copy-start | bytes 196612
  16.5 4.0 %copy-start.9 = (f32[128,128]{1,0:T(8,128)S(1)}, f32[128,128]{1,0:T(8,128)}, u32[]{:S(2)}) copy-start(f32[128,128]{1,0:T(8,128)} %axial.3) | copy-start | bytes 196612
  16.5 4.0 %collective-permute-start.3 = (f32[56,128]{1,0:T(8,128)S(1)}, f32[56,128]{1,0:T(8,128)S(1)}, u32[]{:S(2)}, u32[]{:S(2)}) collective-permute-start(f32[56,128]{1,0:T(8,128)S(1)} %pad_maximum_fusion.1), channel_id=1, source_target_pairs={{1,0},{2,1},{3,2},{0,3},{5,4},{6,5},{7,6},{4,7},{9,8},{10,9},{11,1... | collective-permute-start | bytes 86024 | tf_op jit(solution)/shard_map/ppermute | solution.py:356
  21.2 16.9 %copy-start.2 = (s32[32,8,128]{2,1,0:T(8,128)S(1)}, s32[32,8,128]{2,1,0:T(8,128)}, u32[]{:S(2)}) copy-start(s32[32,8,128]{2,1,0:T(8,128)} %param.17) | copy-start | bytes 393220
  21.2 16.9 %copy-start.4 = (f32[32,8,128]{2,1,0:T(8,128)S(1)}, f32[32,8,128]{2,1,0:T(8,128)}, u32[]{:S(2)}) copy-start(f32[32,8,128]{2,1,0:T(8,128)} %param.14) | copy-start | bytes 393220
  21.2 16.9 %copy-start.7 = (f32[32,8,128]{2,1,0:T(8,128)S(1)}, f32[32,8,128]{2,1,0:T(8,128)}, u32[]{:S(2)}) copy-start(f32[32,8,128]{2,1,0:T(8,128)} %param.18) | copy-start | bytes 393220
  27.9 6.4 %collective-permute-start.4 = (f32[24,128]{1,0:T(8,128)S(1)}, f32[24,128]{1,0:T(8,128)S(1)}, u32[]{:S(2)}, u32[]{:S(2)}) collective-permute-start(f32[24,128]{1,0:T(8,128)S(1)} %get-tuple-element.33), channel_id=1, source_target_pairs={{0,4},{4,8},{8,12},{12,16},{16,20},{20,24},{24,28},{28,32},{32,36}... | collective-permute-start | bytes 36872 | tf_op jit(solution)/shard_map/ppermute | solution.py:351
  27.9 6.5 %collective-permute-start.5 = (f32[24,128]{1,0:T(8,128)S(1)}, f32[24,128]{1,0:T(8,128)S(1)}, u32[]{:S(2)}, u32[]{:S(2)}) collective-permute-start(f32[24,128]{1,0:T(8,128)S(1)} %get-tuple-element.35), channel_id=1, source_target_pairs={{4,0},{8,4},{12,8},{16,12},{20,16},{24,20},{28,24},{32,28},{36,32}... | collective-permute-start | bytes 36872 | tf_op jit(solution)/shard_map/ppermute | solution.py:356
  34.4 5.1 %collective-permute-start.6 = (f32[24,128]{1,0:T(8,128)S(1)}, f32[24,128]{1,0:T(8,128)S(1)}, u32[]{:S(2)}, u32[]{:S(2)}) collective-permute-start(f32[24,128]{1,0:T(8,128)S(1)} %pad_maximum_fusion.4), channel_id=1, source_target_pairs={{0,1},{1,2},{2,3},{3,0},{4,5},{5,6},{6,7},{7,4},{8,9},{9,10},{10,1... | collective-permute-start | bytes 36872 | tf_op jit(solution)/shard_map/ppermute | solution.py:351
  36.3 3.7 %collective-permute-start.7 = (f32[24,128]{1,0:T(8,128)S(1)}, f32[24,128]{1,0:T(8,128)S(1)}, u32[]{:S(2)}, u32[]{:S(2)}) collective-permute-start(f32[24,128]{1,0:T(8,128)S(1)} %pad_maximum_fusion.5), channel_id=1, source_target_pairs={{1,0},{2,1},{3,2},{0,3},{5,4},{6,5},{7,6},{4,7},{9,8},{10,9},{11,1... | collective-permute-start | bytes 36872 | tf_op jit(solution)/shard_map/ppermute | solution.py:356
  38.1 2.0 %copy-start.6 = (f32[32,8,128]{2,1,0:T(8,128)S(1)}, f32[32,8,128]{2,1,0:T(8,128)}, u32[]{:S(2)}) copy-start(f32[32,8,128]{2,1,0:T(8,128)} %param.15) | copy-start | bytes 393220
  46.8 7.0 %collective-permute-start.8 = (f32[112,128]{1,0:T(8,128)S(1)}, f32[112,128]{1,0:T(8,128)S(1)}, u32[]{:S(2)}, u32[]{:S(2)}) collective-permute-start(f32[112,128]{1,0:T(8,128)S(1)} %get-tuple-element.41), channel_id=1, source_target_pairs={{0,4},{4,8},{8,12},{12,16},{16,20},{20,24},{24,28},{28,32},{32,36}... | collective-permute-start | bytes 172040 | tf_op jit(solution)/shard_map/ppermute | solution.py:351
  46.9 6.9 %collective-permute-start.9 = (f32[112,128]{1,0:T(8,128)S(1)}, f32[112,128]{1,0:T(8,128)S(1)}, u32[]{:S(2)}, u32[]{:S(2)}) collective-permute-start(f32[112,128]{1,0:T(8,128)S(1)} %get-tuple-element.43), channel_id=1, source_target_pairs={{4,0},{8,4},{12,8},{16,12},{20,16},{24,20},{28,24},{32,28},{36,32}... | collective-permute-start | bytes 172040 | tf_op jit(solution)/shard_map/ppermute | solution.py:356
  53.8 5.2 %collective-permute-start.10 = (f32[56,128]{1,0:T(8,128)S(1)}, f32[56,128]{1,0:T(8,128)S(1)}, u32[]{:S(2)}, u32[]{:S(2)}) collective-permute-start(f32[56,128]{1,0:T(8,128)S(1)} %pad_maximum_fusion.2), channel_id=1, source_target_pairs={{0,1},{1,2},{2,3},{3,0},{4,5},{5,6},{6,7},{7,4},{8,9},{9,10},{10,1... | collective-permute-start | bytes 86024 | tf_op jit(solution)/shard_map/ppermute | solution.py:351
  55.5 3.9 %collective-permute-start.11 = (f32[56,128]{1,0:T(8,128)S(1)}, f32[56,128]{1,0:T(8,128)S(1)}, u32[]{:S(2)}, u32[]{:S(2)}) collective-permute-start(f32[56,128]{1,0:T(8,128)S(1)} %pad_maximum_fusion.3), channel_id=1, source_target_pairs={{1,0},{2,1},{3,2},{0,3},{5,4},{6,5},{7,6},{4,7},{9,8},{10,9},{11,1... | collective-permute-start | bytes 86024 | tf_op jit(solution)/shard_map/ppermute | solution.py:356
  65.8 6.5 %collective-permute-start.12 = (f32[24,128]{1,0:T(8,128)S(1)}, f32[24,128]{1,0:T(8,128)S(1)}, u32[]{:S(2)}, u32[]{:S(2)}) collective-permute-start(f32[24,128]{1,0:T(8,128)S(1)} %get-tuple-element.46), channel_id=1, source_target_pairs={{0,4},{4,8},{8,12},{12,16},{16,20},{20,24},{24,28},{28,32},{32,36}... | collective-permute-start | bytes 36872 | tf_op jit(solution)/shard_map/ppermute | solution.py:351
  65.9 6.4 %collective-permute-start.13 = (f32[24,128]{1,0:T(8,128)S(1)}, f32[24,128]{1,0:T(8,128)S(1)}, u32[]{:S(2)}, u32[]{:S(2)}) collective-permute-start(f32[24,128]{1,0:T(8,128)S(1)} %get-tuple-element.48), channel_id=1, source_target_pairs={{4,0},{8,4},{12,8},{16,12},{20,16},{24,20},{28,24},{32,28},{36,32}... | collective-permute-start | bytes 36872 | tf_op jit(solution)/shard_map/ppermute | solution.py:356
  72.3 4.9 %collective-permute-start.14 = (f32[24,128]{1,0:T(8,128)S(1)}, f32[24,128]{1,0:T(8,128)S(1)}, u32[]{:S(2)}, u32[]{:S(2)}) collective-permute-start(f32[24,128]{1,0:T(8,128)S(1)} %pad_maximum_fusion.6), channel_id=1, source_target_pairs={{0,1},{1,2},{2,3},{3,0},{4,5},{5,6},{6,7},{7,4},{8,9},{9,10},{10,1... | collective-permute-start | bytes 36872 | tf_op jit(solution)/shard_map/ppermute | solution.py:351
  73.7 3.7 %collective-permute-start.15 = (f32[24,128]{1,0:T(8,128)S(1)}, f32[24,128]{1,0:T(8,128)S(1)}, u32[]{:S(2)}, u32[]{:S(2)}) collective-permute-start(f32[24,128]{1,0:T(8,128)S(1)} %pad_maximum_fusion.7), channel_id=1, source_target_pairs={{1,0},{2,1},{3,2},{0,3},{5,4},{6,5},{7,6},{4,7},{9,8},{10,9},{11,1... | collective-permute-start | bytes 36872 | tf_op jit(solution)/shard_map/ppermute | solution.py:356
  (7 other events, 5.7 us)

commit v2 on v1

--- a/solution.py
+++ b/solution.py
@@ -44,7 +44,7 @@
     return SPAN_THETA * factor * slope + STORAGE
 
 
-def gather_cells(head, cond, row, col, weight, minus, here, plus, edge_minus, edge_plus):
+def lay_cells(head, cond, weight, minus, plus, edge_minus, edge_plus):
     for field, ref in enumerate((head, cond)):
         for half in range(2):
             turned = ref[half * 128 : half * 128 + 128, :].T
@@ -57,10 +57,16 @@
         plus[48 + 32 * field : 80 + 32 * field, :] = ref[pl.ds(7, LAYERS, stride=8), :]
     edge_minus[4:8, :] = jnp.zeros((4, LANES), F32)
     edge_plus[4:8, :] = jnp.zeros((4, LANES), F32)
+
+
+def gather_cells(row, col, weight, outs):
     cells = lax.broadcasted_iota(I32, (CELLS, LANES), 0).astype(F32).astype(BF16)
     columns = lax.broadcasted_iota(I32, (LANES, LANES), 0)
     one, zero = (jnp.ones((), BF16), jnp.zeros((), BF16))
     for j in range(0, SLOTS, 2):
+        out = outs[j // 24]
+        if out is None:
+            continue
         picks = []
         for i in (j, j + 1):
             wanted = jnp.broadcast_to(row[i : i + 1, :].astype(F32).astype(BF16), (CELLS, LANES))
@@ -74,7 +80,6 @@
         )
         for n, i in enumerate((j, j + 1)):
             k, chunk = divmod(i, 8)
-            out = (minus, here, plus)[k // 3]
             mask = columns == col[i : i + 1, :]
             for field in range(2):
                 part = got[field * 128 : field * 128 + 128, n * 128 : n * 128 + 128]
@@ -82,25 +87,49 @@
                 out[at : at + 1, :] = jnp.sum(jnp.where(mask, part, 0.0), 0, keepdims=True)
 
 
+def here_kernel(row, col, weight, here):
+    gather_cells(row, col, weight, (None, here, None))
+
+
 def start_kernel(
-    head, sat, alpha_dry, wet, send_row, send_col,
-    cond, row, col, minus, here, plus, edge_minus, edge_plus, weight,
+    head_in, sat_in, alpha_in, wet_in, row_in, col_in,
+    cond, row, col, minus, plus, edge_minus, edge_plus, weight,
+    head, sat, alpha_dry, wet, send_row, send_col, arrived,
 ):
+    loads = [
+        pltpu.make_async_copy(source, target, arrived.at[i])
+        for i, (source, target) in enumerate(
+            (
+                (row_in, send_row), (col_in, send_col), (head_in, head), (alpha_in, alpha_dry), (wet_in, wet),
+                (sat_in, sat),
+            )
+        )
+    ]
+    for load in loads:
+        load.start()
+    loads[0].wait()
+    loads[1].wait()
     for k in range(9):
         for chunk in range(8):
             at = k * 8 + chunk
-            row[at : at + 1, :] = send_row[k : k + 1, chunk * 128 : chunk * 128 + 128]
-            col[at : at + 1, :] = send_col[k : k + 1, chunk * 128 : chunk * 128 + 128]
+            row[at : at + 1, :] = send_row[0, k : k + 1, chunk * 128 : chunk * 128 + 128]
+            col[at : at + 1, :] = send_col[0, k : k + 1, chunk * 128 : chunk * 128 + 128]
+    for load in loads[2:]:
+        load.wait()
     for layer in range(LAYERS):
         at = slice(layer * 8, layer * 8 + 8)
         cond[at, :] = conduct(head[at, :], sat[at, :], alpha_dry[at, :] * (1.0 + wet[at, :].astype(F32)))
-    gather_cells(head, cond, row, col, weight, minus, here, plus, edge_minus, edge_plus)
+    lay_cells(head, cond, weight, minus, plus, edge_minus, edge_plus)
+    gather_cells(row, col, weight, (minus, None, plus))
 
 
 def terms_kernel(
     head, cond, head_old, alpha_dry, wet, reversal, from_minus, from_plus, side_minus, side_plus,
+    back_minus, back_here, back_plus, row, col,
     numerator, denominator, halo,
 ):
+    pieces = {3 + dy: (x, 8) for dy, x in enumerate((back_minus, back_here, back_plus))}
+    sink = SINK_GAIN * sink_of(pieces, row, col)
     halo[...] = jnp.zeros_like(halo)
     turned = []
     for i in range(4):
@@ -152,7 +181,8 @@
             num, den = add(num, den, head[below, :] - 1.0, cond[below, :])
         else:
             num = num - c
-        numerator[at, :] = num
+        half = layer // 16
+        numerator[at, :] = num - sink[local, half * 128 : half * 128 + 128]
         denominator[at, :] = den
 
 
@@ -167,21 +197,17 @@
             else:
                 source, at = ((side_plus, None, side_minus)[dy], (2 - dx) * 16)
             for field in range(2):
-                to = field * 128 + (dx * 3 + dy) * 8
+                to = field * 72 + (dx * 3 + dy) * 8
                 table[to : to + 8, :] = source[at + field * 8 : at + field * 8 + 8, :]
-    for field in range(2):
-        table[field * 128 + 72 : field * 128 + 128, :] = jnp.zeros((56, LANES), F32)
-        hi, lo = split(table[field * 128 : field * 128 + 128, :].T)
-        weight[field * 128 : field * 128 + 128, 0:128] = hi
-        weight[field * 128 : field * 128 + 128, 128:256] = lo
-    rows = lax.broadcasted_iota(I32, (128, LANES), 0).astype(F32).astype(BF16)
-    columns = lax.broadcasted_iota(I32, (LANES, LANES), 0)
+    weight[:, 0:128], weight[:, 128:256] = split(table[...])
+    columns = lax.broadcasted_iota(I32, (128, LANES), 0).astype(F32).astype(BF16)
+    rows = lax.broadcasted_iota(I32, (SLOTS, LANES), 0)
     one, zero = (jnp.ones((), BF16), jnp.zeros((), BF16))
     for j in range(0, BLOCKS, 2):
         picks = []
         for i in (j, j + 1):
-            wanted = jnp.broadcast_to((code[i : i + 1, :] >> 7).astype(F32).astype(BF16), (128, LANES))
-            picks.append(jnp.where(rows == wanted, one, zero))
+            wanted = jnp.broadcast_to((code[i : i + 1, :] & 127).astype(F32).astype(BF16), (128, LANES))
+            picks.append(jnp.where(columns == wanted, one, zero))
         pick = jnp.concatenate(picks, 1)
         got = lax.dot_general(
             weight[...],
@@ -190,9 +216,9 @@
             preferred_element_type=F32,
         )
         for n, i in enumerate((j, j + 1)):
-            mask = columns == (code[i : i + 1, :] & 127)
+            mask = rows == (code[i : i + 1, :] >> 7)
             for field, ref in enumerate((seg_head, seg_cond)):
-                part = got[field * 128 : field * 128 + 128, n * 128 : n * 128 + 128]
+                part = got[field * 72 : field * 72 + 72, n * 128 : n * 128 + 128]
                 ref[i : i + 1, :] = jnp.sum(jnp.where(mask, part, 0.0), 0, keepdims=True)
     group = 32
     lane = lax.broadcasted_iota(I32, (group, LANES), 1)
@@ -241,7 +267,7 @@
         collar_line = collar_line + jnp.sum(jnp.where(mine, head, 0.0), 0, keepdims=True)
     collar_out[...] = collar_line
     slot_rows = lax.broadcasted_iota(I32, (80, LANES), 0).astype(F32).astype(BF16)
-    slot_cols = rows
+    slot_cols = columns
     total = jnp.zeros((160, LANES), F32)
     for start in range(0, BLOCKS, 8):
         values, places = ([], [])
@@ -263,9 +289,10 @@
             preferred_element_type=F32,
         )
     summed = total[0:72] + total[80:152]
-    out_minus[...] = summed[0:24]
-    out_here[...] = summed[24:48]
-    out_plus[...] = summed[48:72]
+    for dx in range(3):
+        for dy, out in enumerate((out_minus, out_here, out_plus)):
+            k = dx * 3 + dy
+            out[dx * 8 : dx * 8 + 8, :] = summed[k * 8 : k * 8 + 8]
 
 
 def sink_of(pieces, row, col):
@@ -273,8 +300,7 @@
     places_of = lax.broadcasted_iota(I32, (256, LANES), 0).astype(F32).astype(BF16)
     one, zero = (jnp.ones((), BF16), jnp.zeros((), BF16))
     total = jnp.zeros((256, 256), F32)
-    for k in range(9):
-        source, base = pieces[k]
+    for k, (source, base) in pieces.items():
         values, places = ([], [])
         for chunk in range(8):
             i = k * 8 + chunk
@@ -297,15 +323,11 @@
     return total[0:128] + total[128:256]
 
 
-def new_head(back, row, col, numerator, denominator, head_new):
-    from_minus, here, from_plus, side_minus, side_plus = back
-    pieces = []
-    for dx in range(3):
+def new_head(from_minus, from_plus, row, col, numerator, denominator, head_new):
+    pieces = {}
+    for dx, source in ((0, from_minus), (2, from_plus)):
         for dy in range(3):
-            if dy == 1:
-                pieces.append(((from_minus, here, from_plus)[dx], 8))
-            else:
-                pieces.append(((side_minus, None, side_plus)[dy], dx * 8))
+            pieces[dx * 3 + dy] = (source, dy * 8)
     sink = sink_of(pieces, row, col)
     for half in range(2):
         at = slice(half * 128, half * 128 + 128)
@@ -313,37 +335,37 @@
 
 
 def next_kernel(
-    from_minus, here_in, from_plus, side_minus, side_plus, row, col, numerator, denominator, sat, alpha_dry, wet,
-    head, cond, minus, here, plus, edge_minus, edge_plus, weight,
+    from_minus, from_plus, row, col, numerator, denominator, sat, alpha_dry, wet,
+    head, cond, minus, plus, edge_minus, edge_plus, weight,
 ):
-    back = (from_minus, here_in, from_plus, side_minus, side_plus)
-    new_head(back, row, col, numerator, denominator, head)
+    new_head(from_minus, from_plus, row, col, numerator, denominator, head)
     for layer in range(LAYERS):
         at = slice(layer * 8, layer * 8 + 8)
         cond[at, :] = conduct(head[at, :], sat[at, :], alpha_dry[at, :] * (1.0 + wet[at, :].astype(F32)))
-    gather_cells(head, cond, row, col, weight, minus, here, plus, edge_minus, edge_plus)
-
-
-def last_kernel(
-    from_minus, here_in, from_plus, side_minus, side_plus, row, col, numerator, denominator, head
-):
-    back = (from_minus, here_in, from_plus, side_minus, side_plus)
-    new_head(back, row, col, numerator, denominator, head)
-
-
-def call(kernel, outs, scratch=(), specs=None, flops=0, **params):
+    lay_cells(head, cond, weight, minus, plus, edge_minus, edge_plus)
+    gather_cells(row, col, weight, (minus, None, plus))
+
+
+def last_kernel(from_minus, from_plus, row, col, numerator, denominator, head):
+    new_head(from_minus, from_plus, row, col, numerator, denominator, head)
+
+
+def call(kernel, outs, scratch=(), specs=None, micros=1):
     shapes = [jax.ShapeDtypeStruct(shape, dtype) for shape, dtype in outs]
     return pl.pallas_call(
         kernel,
         out_shape=shapes,
-        scratch_shapes=[pltpu.VMEM(shape, dtype) for shape, dtype in scratch],
+        scratch_shapes=[pltpu.VMEM(*x) if isinstance(x, tuple) else x for x in scratch],
         compiler_params=pltpu.CompilerParams(vmem_limit_bytes=VMEM_LIMIT),
+        cost_estimate=pl.CostEstimate(
+            flops=micros * 10**9, bytes_accessed=micros * 3 * 10**6, transcendentals=0
+        ),
         **({} if specs is None else {"in_specs": specs}),
-        **params,
-    )
-
-
-MESSAGES = [((112, 128), F32), ((48, 128), F32), ((112, 128), F32), ((8, 128), F32), ((8, 128), F32)]
+    )
+
+
+WEIGHT = ((256, 512), BF16)
+MESSAGES = [((112, 128), F32), ((112, 128), F32), ((8, 128), F32), ((8, 128), F32), WEIGHT]
 
 
 def up(x, axis):
@@ -356,9 +378,10 @@
     return lax.ppermute(x, axis, [((i + 1) % size, i) for i in range(size)])
 
 
-def spread(minus, here, plus, edge_minus, edge_plus):
+def spread(row, col, minus, plus, edge_minus, edge_plus, weight):
     from_minus = up(plus, "gx")
     from_plus = down(minus, "gx")
+    (here,) = call(here_kernel, [((48, 128), F32)])(row, col, weight)
     side_minus = up(
         jnp.concatenate([from_minus[32:48], here[32:48], from_plus[32:48], edge_plus], 0), "gy"
     )
@@ -369,11 +392,11 @@
 
 
 def give_back(minus, here, plus):
-    from_minus = up(minus, "gx")
-    from_plus = down(plus, "gx")
-    side_plus = down(jnp.concatenate([from_minus[16:24], here[16:24], from_plus[16:24]], 0), "gy")
-    side_minus = up(jnp.concatenate([from_minus[0:8], here[0:8], from_plus[0:8]], 0), "gy")
-    return (from_minus, here, from_plus, side_minus, side_plus)
+    back_minus = up(minus, "gy")
+    back_plus = down(plus, "gy")
+    from_minus = up(jnp.concatenate([x[0:8] for x in (back_minus, here, back_plus)], 0), "gx")
+    from_plus = down(jnp.concatenate([x[16:24] for x in (back_minus, here, back_plus)], 0), "gx")
+    return ((back_minus, here, back_plus), (from_minus, from_plus))
 
 
 def on_device(
@@ -404,35 +427,38 @@
     code = offset_k * send_row.shape[2] + source_slot
     stem, entry = (stem_link.reshape(1, BLOCKS), entry_seg.reshape(1, BLOCKS))
     head_old = head
+    far = pl.BlockSpec(memory_space=pltpu.HBM)
+    tile_scratch = [((CELLS, LANES), F32)] * 3 + [((CELLS, LANES), I32)] + [(send_row.shape, I32)] * 2
     cond, row, col, *messages = call(
         start_kernel,
         [((CELLS, LANES), F32), ((SLOTS, LANES), I32), ((SLOTS, LANES), I32)] + MESSAGES,
-        [((256, 512), BF16)],
-    )(head, sat, alpha, wet, send_row[0], send_col[0])
+        tile_scratch + [pltpu.SemaphoreType.DMA((6,))],
+        specs=[far] * 6,
+        micros=4,
+    )(head, sat, alpha, wet, send_row, send_col)
     smem = [pl.BlockSpec(memory_space=pltpu.SMEM)] + [pl.BlockSpec(memory_space=pltpu.VMEM)] * 10
     for iteration in range(PICARD):
-        got = spread(*messages)
+        got = spread(row, col, *messages)
         *sums, collar = call(
             root_kernel,
             [((24, 128), F32)] * 3 + [((1, 128), F32)],
-            [((256, 256), BF16), ((256, 128), F32)] + [((128, 128), F32)] * 3,
+            [((144, 256), BF16), ((144, 128), F32)] + [((128, 128), F32)] * 3,
             specs=smem,
+            micros=6,
         )(demand, *got, code, root_radial, root_axial, stem, entry)
+        near, far_back = give_back(*sums)
         numerator, denominator = call(
             terms_kernel,
             [((CELLS, LANES), F32)] * 2,
             [((128, 128), F32)],
-        )(head, cond, head_old, alpha, wet, reversal, got[0], got[2], got[3], got[4])
-        back = give_back(*sums)
+        )(head, cond, head_old, alpha, wet, reversal, got[0], got[2], got[3], got[4], *near, row, col)
         if iteration < PICARD - 1:
             head, cond, *messages = call(
-                next_kernel,
-                [((CELLS, LANES), F32)] * 2 + MESSAGES,
-                [((256, 512), BF16)],
-            )(*back, row, col, numerator, denominator, sat, alpha, wet)
+                next_kernel, [((CELLS, LANES), F32)] * 2 + MESSAGES, micros=5
+            )(*far_back, row, col, numerator, denominator, sat, alpha, wet)
         else:
             (head,) = call(last_kernel, [((CELLS, LANES), F32)])(
-                *back, row, col, numerator, denominator
+                *far_back, row, col, numerator, denominator
             )
     return (head.reshape(tile), collar[0, :PLANTS])
 

time: 79.6 us -> 75.7 us (0.951)
  Pallas kernels: 26 us -> 23.5 us
  waiting for transfers between devices: 12.5 us -> 11.2 us
    pallas_call x3 -> x5, Pallas kernels: 19.9 us -> 16.8 us  [the longest x2 9.93 us: on_device(): call(root_kernel, [((24, 128), F32)] * 3 + [((1, 128), F32)], [((144, 256...]
    ppermute x8, waiting for transfers between devices: 11.4 us -> 9.58 us  [up(): return lax.ppermute(x, axis, [(i, (i + 1) % size) for i in range(size)])]
    pallas_call x2, Pallas kernels: 0.96 us -> 1.92 us  [on_device(): call(terms_kernel, [((CELLS, LANES), F32)] * 2, [((128, 128), F32)])]
    unnamed x31 -> x34, local copies, waits for them, and re-layouts: 4.33 us -> 4.31 us
  transfers between devices with their start and end apart: 16 -> 16, of which waited for: 11 -> 11; matrix products, arithmetic and copies ran while one was open for 1% -> 1% of each run, Pallas kernels for 1% -> 4%
where the time goes in v2:
time: 75.7 us; the launch traced here: 75.3 us
  starting transfers between devices  34.7 us (46%)
  Pallas kernels  23.5 us (31%)
  waiting for transfers between devices  11.2 us (15%)
  local copies, waits for them, and re-layouts  4.85 us (6%)
  between operations  0.87 us (1%)
    ppermute x8, starting transfers between devices, down(): return lax.ppermute(x, axis, [((i + 1) % size, i) for i in range(size)])  27.5 us
    pallas_call x2, Pallas kernels, on_device(): call(root_kernel, [((24, 128), F32)] * 3 + [((1, 128), F32)], [((144, 256...  9.93 us
    ppermute x8, waiting for transfers between devices, up(): return lax.ppermute(x, axis, [(i, (i + 1) % size) for i in range(size)])  9.58 us
    ppermute x8, starting transfers between devices, up(): return lax.ppermute(x, axis, [(i, (i + 1) % size) for i in range(size)])  7.12 us
    pallas_call x1, Pallas kernels, on_device(): call(next_kernel, [((CELLS, LANES), F32)] * 2 + MESSAGES, micros=5)  4.68 us
    unnamed x34, local copies, waits for them, and re-layouts  4.31 us
    pallas_call x1, Pallas kernels, on_device(): call(start_kernel, [((CELLS, LANES), F32), ((SLOTS, LANES), I32), ((SLOTS...  3.08 us
    pallas_call x2, Pallas kernels, spread(): here, = call(here_kernel, [((48, 128), F32)])(row, col, weight)  2.19 us
  transfers between devices with their start and end apart: 16, of which 11 were waited for; matrix products, arithmetic and copies ran while one was open for 1% of the time, Pallas kernels for 4%

profile of v2, /device:TPU:0, one launch (start us, length us, event | category | flops | bytes accessed | tf_op | source)
XLA Modules:
  0.0 75.3 jit_solution(16823644551718406125)
XLA Ops:
  4.3 3.1 %shard_map.149 = (f32[256,128]{1,0:T(8,128)S(1)}, s32[72,128]{1,0:T(8,128)S(1)}, s32[72,128]{1,0:T(8,128)S(1)}, f32[112,128]{1,0:T(8,128)S(1)}, f32[112,128]{1,0...) custom-call(f32[256,128]{1,0:T(8,128)S(1)} %bitcast.12, ...), custom_call_target="tpu_custom_call" | custom-call | flops 4000000000 | bytes 12000000 | tf_op jit(solution)/shard_map/pallas_call | solution.py:432
  7.5 5.1 %collective-permute-start.1 = (f32[112,128]{1,0:T(8,128)S(1)}, f32[112,128]{1,0:T(8,128)S(1)}, u32[]{:S(2)}, u32[]{:S(2)}) collective-permute-start(f32[112,128]{1,0:T(8,128)S(1)} %get-tuple-element.32), channel_id=1, source_target_pairs={{4,0},{8,4},{12,8},{16,12},{20,16},{24,20},{28,24},{32,28},{36,32}... | collective-permute-start | bytes 172040 | tf_op jit(solution)/shard_map/ppermute | solution.py:378
  12.5 1.1 %shard_map.150.here = f32[48,128]{1,0:T(8,128)S(1)} custom-call(s32[72,128]{1,0:T(8,128)S(1)} %get-tuple-element.29.row, s32[72,128]{1,0:T(8,128)S(1)} %get-tuple-element.30.col, bf16[256,512]{1,0:T(8,128)(2,1)S(1)} %get-tuple-element.31.weight), custom_call_target="tpu_custom_call" | custom-call | flops 1000000000 | bytes 3000000 | tf_op jit(solution)/shard_map/pallas_call | solution.py:384
  14.4 2.1 %collective-permute-start.2 = (f32[56,128]{1,0:T(8,128)S(1)}, f32[56,128]{1,0:T(8,128)S(1)}, u32[]{:S(2)}, u32[]{:S(2)}) collective-permute-start(f32[56,128]{1,0:T(8,128)S(1)} %pad_maximum_fusion), channel_id=1, source_target_pairs={{0,1},{1,2},{2,3},{3,0},{4,5},{5,6},{6,7},{7,4},{8,9},{9,10},{10,1... | collective-permute-start | bytes 86024 | tf_op jit(solution)/shard_map/ppermute | solution.py:373
  16.5 2.2 %collective-permute-start.3 = (f32[56,128]{1,0:T(8,128)S(1)}, f32[56,128]{1,0:T(8,128)S(1)}, u32[]{:S(2)}, u32[]{:S(2)}) collective-permute-start(f32[56,128]{1,0:T(8,128)S(1)} %pad_maximum_fusion.1), channel_id=1, source_target_pairs={{1,0},{2,1},{3,2},{0,3},{5,4},{6,5},{7,6},{4,7},{9,8},{10,9},{11,1... | collective-permute-start | bytes 86024 | tf_op jit(solution)/shard_map/ppermute | solution.py:378
  18.9 1.6 %collective-permute-done.2.side_minus = f32[56,128]{1,0:T(8,128)S(1)} collective-permute-done((f32[56,128]{1,0:T(8,128)S(1)}, f32[56,128]{1,0:T(8,128)S(1)}, u32[]{:S(2)}, u32[]{:S(2)}) %collective-permute-start.2) | collective-permute-done | bytes 28704 | tf_op jit(solution)/shard_map/ppermute | solution.py:373
  21.2 5.1 %shard_map.151 = (f32[24,128]{1,0:T(8,128)S(1)}, f32[24,128]{1,0:T(8,128)S(1)}, f32[24,128]{1,0:T(8,128)S(1)}, f32[1,128]{1,0:T(1,128)}) custom-call(f32[16]{0:T(128)S(1)} %copy-done.10, f32[112,128]{1,0:T(8,128)S(1)} %collective-permute-done.from_minus, f32[48,128]{1,0:T(8,128)S(1)} %shard_map.150.here, f32[112,128]{1,0:T(8,128)S(1)} %collective-permute-done.1.from_plus, ...), custom_call_target="tpu_custom_call" | custom-call | flops 6000000000 | bytes 18000000 | tf_op jit(solution)/shard_map/pallas_call | solution.py:442
  26.3 1.9 %collective-permute-start.4 = (f32[24,128]{1,0:T(8,128)S(1)}, f32[24,128]{1,0:T(8,128)S(1)}, u32[]{:S(2)}, u32[]{:S(2)}) collective-permute-start(f32[24,128]{1,0:T(8,128)S(1)} %get-tuple-element.35), channel_id=1, source_target_pairs={{0,1},{1,2},{2,3},{3,0},{4,5},{5,6},{6,7},{7,4},{8,9},{9,10},{10,1... | collective-permute-start | bytes 36872 | tf_op jit(solution)/shard_map/ppermute | solution.py:373
  28.2 1.4 %collective-permute-start.5 = (f32[24,128]{1,0:T(8,128)S(1)}, f32[24,128]{1,0:T(8,128)S(1)}, u32[]{:S(2)}, u32[]{:S(2)}) collective-permute-start(f32[24,128]{1,0:T(8,128)S(1)} %get-tuple-element.37), channel_id=1, source_target_pairs={{1,0},{2,1},{3,2},{0,3},{5,4},{6,5},{7,6},{4,7},{9,8},{10,9},{11,1... | collective-permute-start | bytes 36872 | tf_op jit(solution)/shard_map/ppermute | solution.py:378
  29.6 1.7 %collective-permute-done.4.back_minus = f32[24,128]{1,0:T(8,128)S(1)} collective-permute-done((f32[24,128]{1,0:T(8,128)S(1)}, f32[24,128]{1,0:T(8,128)S(1)}, u32[]{:S(2)}, u32[]{:S(2)}) %collective-permute-start.4) | collective-permute-done | bytes 12320 | tf_op jit(solution)/shard_map/ppermute | solution.py:373
  31.9 5.1 %collective-permute-start.7 = (f32[24,128]{1,0:T(8,128)S(1)}, f32[24,128]{1,0:T(8,128)S(1)}, u32[]{:S(2)}, u32[]{:S(2)}) collective-permute-start(f32[24,128]{1,0:T(8,128)S(1)} %pad_maximum_fusion.5), channel_id=1, source_target_pairs={{4,0},{8,4},{12,8},{16,12},{20,16},{24,20},{28,24},{32,28},{36,32}... | collective-permute-start | bytes 36872 | tf_op jit(solution)/shard_map/ppermute | solution.py:378
  38.4 4.7 %shard_map.153 = (f32[256,128]{1,0:T(8,128)S(1)}, f32[256,128]{1,0:T(8,128)S(1)}, f32[112,128]{1,0:T(8,128)S(1)}, f32[112,128]{1,0:T(8,128)S(1)}, f32[8,128]{1,0...) custom-call(f32[24,128]{1,0:T(8,128)S(1)} %collective-permute-done.6.from_minus, ...), custom_call_target="tpu_custom_call" | custom-call | flops 5000000000 | bytes 15000000 | tf_op jit(solution)/shard_map/pallas_call | solution.py:456
  43.1 1.1 %shard_map.154.here = f32[48,128]{1,0:T(8,128)S(1)} custom-call(s32[72,128]{1,0:T(8,128)S(1)} %get-tuple-element.29.row, s32[72,128]{1,0:T(8,128)S(1)} %get-tuple-element.30.col, bf16[256,512]{1,0:T(8,128)(2,1)S(1)} %get-tuple-element.42.weight), custom_call_target="tpu_custom_call" | custom-call | flops 1000000000 | bytes 3000000 | tf_op jit(solution)/shard_map/pallas_call | solution.py:384
  44.3 5.1 %collective-permute-start.9 = (f32[112,128]{1,0:T(8,128)S(1)}, f32[112,128]{1,0:T(8,128)S(1)}, u32[]{:S(2)}, u32[]{:S(2)}) collective-permute-start(f32[112,128]{1,0:T(8,128)S(1)} %get-tuple-element.43), channel_id=1, source_target_pairs={{4,0},{8,4},{12,8},{16,12},{20,16},{24,20},{28,24},{32,28},{36,32}... | collective-permute-start | bytes 172040 | tf_op jit(solution)/shard_map/ppermute | solution.py:378
  49.4 1.8 %collective-permute-done.8.from_minus = f32[112,128]{1,0:T(8,128)S(1)} collective-permute-done((f32[112,128]{1,0:T(8,128)S(1)}, f32[112,128]{1,0:T(8,128)S(1)}, u32[]{:S(2)}, u32[]{:S(2)}) %collective-permute-start.8) | collective-permute-done | bytes 57376 | tf_op jit(solution)/shard_map/ppermute | solution.py:373
  51.2 1.7 %collective-permute-start.10 = (f32[56,128]{1,0:T(8,128)S(1)}, f32[56,128]{1,0:T(8,128)S(1)}, u32[]{:S(2)}, u32[]{:S(2)}) collective-permute-start(f32[56,128]{1,0:T(8,128)S(1)} %pad_maximum_fusion.2), channel_id=1, source_target_pairs={{0,1},{1,2},{2,3},{3,0},{4,5},{5,6},{6,7},{7,4},{8,9},{9,10},{10,1... | collective-permute-start | bytes 86024 | tf_op jit(solution)/shard_map/ppermute | solution.py:373
  52.9 1.6 %collective-permute-start.11 = (f32[56,128]{1,0:T(8,128)S(1)}, f32[56,128]{1,0:T(8,128)S(1)}, u32[]{:S(2)}, u32[]{:S(2)}) collective-permute-start(f32[56,128]{1,0:T(8,128)S(1)} %pad_maximum_fusion.3), channel_id=1, source_target_pairs={{1,0},{2,1},{3,2},{0,3},{5,4},{6,5},{7,6},{4,7},{9,8},{10,9},{11,1... | collective-permute-start | bytes 86024 | tf_op jit(solution)/shard_map/ppermute | solution.py:378
  54.5 1.8 %collective-permute-done.10.side_minus = f32[56,128]{1,0:T(8,128)S(1)} collective-permute-done((f32[56,128]{1,0:T(8,128)S(1)}, f32[56,128]{1,0:T(8,128)S(1)}, u32[]{:S(2)}, u32[]{:S(2)}) %collective-permute-start.10) | collective-permute-done | bytes 28704 | tf_op jit(solution)/shard_map/ppermute | solution.py:373
  56.7 4.8 %shard_map.155 = (f32[24,128]{1,0:T(8,128)S(1)}, f32[24,128]{1,0:T(8,128)S(1)}, f32[24,128]{1,0:T(8,128)S(1)}, f32[1,128]{1,0:T(1,128)S(1)}) custom-call(f32[16]{0:T(128)S(1)} %copy-done.10, f32[112,128]{1,0:T(8,128)S(1)} %collective-permute-done.8.from_minus, f32[48,128]{1,0:T(8,128)S(1)} %shard_map.154.here, ...), custom_call_target="tpu_custom_call" | custom-call | flops 6000000000 | bytes 18000000 | tf_op jit(solution)/shard_map/pallas_call | solution.py:442
  61.6 1.3 %collective-permute-start.12 = (f32[24,128]{1,0:T(8,128)S(1)}, f32[24,128]{1,0:T(8,128)S(1)}, u32[]{:S(2)}, u32[]{:S(2)}) collective-permute-start(f32[24,128]{1,0:T(8,128)S(1)} %get-tuple-element.46), channel_id=1, source_target_pairs={{0,1},{1,2},{2,3},{3,0},{4,5},{5,6},{6,7},{7,4},{8,9},{9,10},{10,1... | collective-permute-start | bytes 36872 | tf_op jit(solution)/shard_map/ppermute | solution.py:373
  63.4 2.0 %collective-permute-start.13 = (f32[24,128]{1,0:T(8,128)S(1)}, f32[24,128]{1,0:T(8,128)S(1)}, u32[]{:S(2)}, u32[]{:S(2)}) collective-permute-start(f32[24,128]{1,0:T(8,128)S(1)} %get-tuple-element.48), channel_id=1, source_target_pairs={{1,0},{2,1},{3,2},{0,3},{5,4},{6,5},{7,6},{4,7},{9,8},{10,9},{11,1... | collective-permute-start | bytes 36872 | tf_op jit(solution)/shard_map/ppermute | solution.py:378
  65.4 1.2 %collective-permute-done.12.back_minus = f32[24,128]{1,0:T(8,128)S(1)} collective-permute-done((f32[24,128]{1,0:T(8,128)S(1)}, f32[24,128]{1,0:T(8,128)S(1)}, u32[]{:S(2)}, u32[]{:S(2)}) %collective-permute-start.12) | collective-permute-done | bytes 12320 | tf_op jit(solution)/shard_map/ppermute | solution.py:373
  67.1 5.1 %collective-permute-start.15 = (f32[24,128]{1,0:T(8,128)S(1)}, f32[24,128]{1,0:T(8,128)S(1)}, u32[]{:S(2)}, u32[]{:S(2)}) collective-permute-start(f32[24,128]{1,0:T(8,128)S(1)} %pad_maximum_fusion.7), channel_id=1, source_target_pairs={{4,0},{8,4},{12,8},{16,12},{20,16},{24,20},{28,24},{32,28},{36,32}... | collective-permute-start | bytes 36872 | tf_op jit(solution)/shard_map/ppermute | solution.py:378
  73.6 1.7 %shard_map.157 = f32[256,128]{1,0:T(8,128)} custom-call(f32[24,128]{1,0:T(8,128)S(1)} %collective-permute-done.14.from_minus, f32[24,128]{1,0:T(8,128)S(1)} %collective-permute-done.15.from_plus, s32[72,128]{1,0:T(8,128)S(1)} %get-tuple-element.29.row, s32[72,128]{1,0:T(8,128)S(1)} %get-tuple-element.30.col, f32[256,128]{1,0:T(8,128)S(1)} %get-tuple-element.51.numerator, ...), custom_call_target="tpu_custom_call" | custom-call | flops 1000000000 | bytes 3000000 | tf_op jit(solution)/shard_map/pallas_call | solution.py:460
  (73 shorter events, 10.3 us)
Async XLA Ops:
  7.4 7.0 %collective-permute-start = (f32[112,128]{1,0:T(8,128)S(1)}, f32[112,128]{1,0:T(8,128)S(1)}, u32[]{:S(2)}, u32[]{:S(2)}) collective-permute-start(f32[112,128]{1,0:T(8,128)S(1)} %get-tuple-element.28), channel_id=1, source_target_pairs={{0,4},{4,8},{8,12},{12,16},{16,20},{20,24},{24,28},{28,32},{32,36}... | collective-permute-start | bytes 172040 | tf_op jit(solution)/shard_map/ppermute | solution.py:373
  7.5 6.9 %collective-permute-start.1 = (f32[112,128]{1,0:T(8,128)S(1)}, f32[112,128]{1,0:T(8,128)S(1)}, u32[]{:S(2)}, u32[]{:S(2)}) collective-permute-start(f32[112,128]{1,0:T(8,128)S(1)} %get-tuple-element.32), channel_id=1, source_target_pairs={{4,0},{8,4},{12,8},{16,12},{20,16},{24,20},{28,24},{32,28},{36,32}... | collective-permute-start | bytes 172040 | tf_op jit(solution)/shard_map/ppermute | solution.py:378
  14.4 4.4 %copy-start.14 = (s32[128,128]{1,0:T(8,128)S(1)}, s32[128,128]{1,0:T(8,128)}, u32[]{:S(2)}) copy-start(s32[128,128]{1,0:T(8,128)} %param.25) | copy-start | bytes 196612
  14.4 4.3 %copy-start.13 = (s32[128,128]{1,0:T(8,128)S(1)}, s32[128,128]{1,0:T(8,128)}, u32[]{:S(2)}) copy-start(s32[128,128]{1,0:T(8,128)} %param.26) | copy-start | bytes 196612
  14.4 6.0 %collective-permute-start.2 = (f32[56,128]{1,0:T(8,128)S(1)}, f32[56,128]{1,0:T(8,128)S(1)}, u32[]{:S(2)}, u32[]{:S(2)}) collective-permute-start(f32[56,128]{1,0:T(8,128)S(1)} %pad_maximum_fusion), channel_id=1, source_target_pairs={{0,1},{1,2},{2,3},{3,0},{4,5},{5,6},{6,7},{7,4},{8,9},{9,10},{10,1... | collective-permute-start | bytes 86024 | tf_op jit(solution)/shard_map/ppermute | solution.py:373
  16.5 4.0 %copy-start.8 = (f32[128,128]{1,0:T(8,128)S(1)}, f32[128,128]{1,0:T(8,128)}, u32[]{:S(2)}) copy-start(f32[128,128]{1,0:T(8,128)} %radial_in.3) | copy-start | bytes 196612
  16.5 4.0 %copy-start.9 = (f32[128,128]{1,0:T(8,128)S(1)}, f32[128,128]{1,0:T(8,128)}, u32[]{:S(2)}) copy-start(f32[128,128]{1,0:T(8,128)} %axial.3) | copy-start | bytes 196612
  16.5 4.0 %collective-permute-start.3 = (f32[56,128]{1,0:T(8,128)S(1)}, f32[56,128]{1,0:T(8,128)S(1)}, u32[]{:S(2)}, u32[]{:S(2)}) collective-permute-start(f32[56,128]{1,0:T(8,128)S(1)} %pad_maximum_fusion.1), channel_id=1, source_target_pairs={{1,0},{2,1},{3,2},{0,3},{5,4},{6,5},{7,6},{4,7},{9,8},{10,9},{11,1... | collective-permute-start | bytes 86024 | tf_op jit(solution)/shard_map/ppermute | solution.py:378
  21.1 15.8 %copy-start.2 = (f32[32,8,128]{2,1,0:T(8,128)S(1)}, f32[32,8,128]{2,1,0:T(8,128)}, u32[]{:S(2)}) copy-start(f32[32,8,128]{2,1,0:T(8,128)} %param.14) | copy-start | bytes 393220
  21.1 15.8 %copy-start.4 = (f32[32,8,128]{2,1,0:T(8,128)S(1)}, f32[32,8,128]{2,1,0:T(8,128)}, u32[]{:S(2)}) copy-start(f32[32,8,128]{2,1,0:T(8,128)} %param.16) | copy-start | bytes 393220
  21.1 15.8 %copy-start.6 = (s32[32,8,128]{2,1,0:T(8,128)S(1)}, s32[32,8,128]{2,1,0:T(8,128)}, u32[]{:S(2)}) copy-start(s32[32,8,128]{2,1,0:T(8,128)} %param.17) | copy-start | bytes 393220
  21.2 15.8 %copy-start.7 = (f32[32,8,128]{2,1,0:T(8,128)S(1)}, f32[32,8,128]{2,1,0:T(8,128)}, u32[]{:S(2)}) copy-start(f32[32,8,128]{2,1,0:T(8,128)} %param.18) | copy-start | bytes 393220
  26.3 5.0 %collective-permute-start.4 = (f32[24,128]{1,0:T(8,128)S(1)}, f32[24,128]{1,0:T(8,128)S(1)}, u32[]{:S(2)}, u32[]{:S(2)}) collective-permute-start(f32[24,128]{1,0:T(8,128)S(1)} %get-tuple-element.35), channel_id=1, source_target_pairs={{0,1},{1,2},{2,3},{3,0},{4,5},{5,6},{6,7},{7,4},{8,9},{9,10},{10,1... | collective-permute-start | bytes 36872 | tf_op jit(solution)/shard_map/ppermute | solution.py:373
  28.2 3.7 %collective-permute-start.5 = (f32[24,128]{1,0:T(8,128)S(1)}, f32[24,128]{1,0:T(8,128)S(1)}, u32[]{:S(2)}, u32[]{:S(2)}) collective-permute-start(f32[24,128]{1,0:T(8,128)S(1)} %get-tuple-element.37), channel_id=1, source_target_pairs={{1,0},{2,1},{3,2},{0,3},{5,4},{6,5},{7,6},{4,7},{9,8},{10,9},{11,1... | collective-permute-start | bytes 36872 | tf_op jit(solution)/shard_map/ppermute | solution.py:378
  31.9 6.4 %collective-permute-start.6 = (f32[24,128]{1,0:T(8,128)S(1)}, f32[24,128]{1,0:T(8,128)S(1)}, u32[]{:S(2)}, u32[]{:S(2)}) collective-permute-start(f32[24,128]{1,0:T(8,128)S(1)} %pad_maximum_fusion.4), channel_id=1, source_target_pairs={{0,4},{4,8},{8,12},{12,16},{16,20},{20,24},{24,28},{28,32},{32,36}... | collective-permute-start | bytes 36872 | tf_op jit(solution)/shard_map/ppermute | solution.py:373
  31.9 6.5 %collective-permute-start.7 = (f32[24,128]{1,0:T(8,128)S(1)}, f32[24,128]{1,0:T(8,128)S(1)}, u32[]{:S(2)}, u32[]{:S(2)}) collective-permute-start(f32[24,128]{1,0:T(8,128)S(1)} %pad_maximum_fusion.5), channel_id=1, source_target_pairs={{4,0},{8,4},{12,8},{16,12},{20,16},{24,20},{28,24},{32,28},{36,32}... | collective-permute-start | bytes 36872 | tf_op jit(solution)/shard_map/ppermute | solution.py:378
  44.2 7.0 %collective-permute-start.8 = (f32[112,128]{1,0:T(8,128)S(1)}, f32[112,128]{1,0:T(8,128)S(1)}, u32[]{:S(2)}, u32[]{:S(2)}) collective-permute-start(f32[112,128]{1,0:T(8,128)S(1)} %get-tuple-element.41), channel_id=1, source_target_pairs={{0,4},{4,8},{8,12},{12,16},{16,20},{20,24},{24,28},{28,32},{32,36}... | collective-permute-start | bytes 172040 | tf_op jit(solution)/shard_map/ppermute | solution.py:373
  44.3 6.9 %collective-permute-start.9 = (f32[112,128]{1,0:T(8,128)S(1)}, f32[112,128]{1,0:T(8,128)S(1)}, u32[]{:S(2)}, u32[]{:S(2)}) collective-permute-start(f32[112,128]{1,0:T(8,128)S(1)} %get-tuple-element.43), channel_id=1, source_target_pairs={{4,0},{8,4},{12,8},{16,12},{20,16},{24,20},{28,24},{32,28},{36,32}... | collective-permute-start | bytes 172040 | tf_op jit(solution)/shard_map/ppermute | solution.py:378
  51.2 5.1 %collective-permute-start.10 = (f32[56,128]{1,0:T(8,128)S(1)}, f32[56,128]{1,0:T(8,128)S(1)}, u32[]{:S(2)}, u32[]{:S(2)}) collective-permute-start(f32[56,128]{1,0:T(8,128)S(1)} %pad_maximum_fusion.2), channel_id=1, source_target_pairs={{0,1},{1,2},{2,3},{3,0},{4,5},{5,6},{6,7},{7,4},{8,9},{9,10},{10,1... | collective-permute-start | bytes 86024 | tf_op jit(solution)/shard_map/ppermute | solution.py:373
  52.9 3.9 %collective-permute-start.11 = (f32[56,128]{1,0:T(8,128)S(1)}, f32[56,128]{1,0:T(8,128)S(1)}, u32[]{:S(2)}, u32[]{:S(2)}) collective-permute-start(f32[56,128]{1,0:T(8,128)S(1)} %pad_maximum_fusion.3), channel_id=1, source_target_pairs={{1,0},{2,1},{3,2},{0,3},{5,4},{6,5},{7,6},{4,7},{9,8},{10,9},{11,1... | collective-permute-start | bytes 86024 | tf_op jit(solution)/shard_map/ppermute | solution.py:378
  61.6 5.0 %collective-permute-start.12 = (f32[24,128]{1,0:T(8,128)S(1)}, f32[24,128]{1,0:T(8,128)S(1)}, u32[]{:S(2)}, u32[]{:S(2)}) collective-permute-start(f32[24,128]{1,0:T(8,128)S(1)} %get-tuple-element.46), channel_id=1, source_target_pairs={{0,1},{1,2},{2,3},{3,0},{4,5},{5,6},{6,7},{7,4},{8,9},{9,10},{10,1... | collective-permute-start | bytes 36872 | tf_op jit(solution)/shard_map/ppermute | solution.py:373
  63.4 3.7 %collective-permute-start.13 = (f32[24,128]{1,0:T(8,128)S(1)}, f32[24,128]{1,0:T(8,128)S(1)}, u32[]{:S(2)}, u32[]{:S(2)}) collective-permute-start(f32[24,128]{1,0:T(8,128)S(1)} %get-tuple-element.48), channel_id=1, source_target_pairs={{1,0},{2,1},{3,2},{0,3},{5,4},{6,5},{7,6},{4,7},{9,8},{10,9},{11,1... | collective-permute-start | bytes 36872 | tf_op jit(solution)/shard_map/ppermute | solution.py:378
  67.1 6.4 %collective-permute-start.14 = (f32[24,128]{1,0:T(8,128)S(1)}, f32[24,128]{1,0:T(8,128)S(1)}, u32[]{:S(2)}, u32[]{:S(2)}) collective-permute-start(f32[24,128]{1,0:T(8,128)S(1)} %pad_maximum_fusion.6), channel_id=1, source_target_pairs={{0,4},{4,8},{8,12},{12,16},{16,20},{20,24},{24,28},{28,32},{32,36}... | collective-permute-start | bytes 36872 | tf_op jit(solution)/shard_map/ppermute | solution.py:373
  67.1 6.5 %collective-permute-start.15 = (f32[24,128]{1,0:T(8,128)S(1)}, f32[24,128]{1,0:T(8,128)S(1)}, u32[]{:S(2)}, u32[]{:S(2)}) collective-permute-start(f32[24,128]{1,0:T(8,128)S(1)} %pad_maximum_fusion.7), channel_id=1, source_target_pairs={{4,0},{8,4},{12,8},{16,12},{20,16},{24,20},{28,24},{32,28},{36,32}... | collective-permute-start | bytes 36872 | tf_op jit(solution)/shard_map/ppermute | solution.py:378
  (8 other events, 6.5 us)

commit v3 on v2

--- a/solution.py
+++ b/solution.py
@@ -44,7 +44,13 @@
     return SPAN_THETA * factor * slope + STORAGE
 
 
-def lay_cells(head, cond, weight, minus, plus, edge_minus, edge_plus):
+def x_places():
+    odd = lax.rem(lax.axis_index("gx"), 2)
+    return (2 - 2 * odd, 2 * odd)
+
+
+def lay_cells(head, cond, weight, chip, cross, edge_minus, edge_plus):
+    even = x_places()[0] == 2
     for field, ref in enumerate((head, cond)):
         for half in range(2):
             turned = ref[half * 128 : half * 128 + 128, :].T
@@ -53,83 +59,70 @@
             hi, lo = split(turned)
             weight[field * 128 : field * 128 + 128, half * 128 : half * 128 + 128] = hi
             weight[field * 128 : field * 128 + 128, 256 + half * 128 : 384 + half * 128] = lo
-        minus[48 + 32 * field : 80 + 32 * field, :] = ref[pl.ds(0, LAYERS, stride=8), :]
-        plus[48 + 32 * field : 80 + 32 * field, :] = ref[pl.ds(7, LAYERS, stride=8), :]
+        first = ref[pl.ds(0, LAYERS, stride=8), :]
+        last = ref[pl.ds(7, LAYERS, stride=8), :]
+        chip[48 + 32 * field : 80 + 32 * field, :] = jnp.where(even, last, first)
+        cross[48 + 32 * field : 80 + 32 * field, :] = jnp.where(even, first, last)
     edge_minus[4:8, :] = jnp.zeros((4, LANES), F32)
     edge_plus[4:8, :] = jnp.zeros((4, LANES), F32)
+
+
+def eight(ref, at):
+    return ref[pl.ds(pl.multiple_of(at, 8), 8), :]
 
 
 def gather_cells(row, col, weight, outs):
     cells = lax.broadcasted_iota(I32, (CELLS, LANES), 0).astype(F32).astype(BF16)
     columns = lax.broadcasted_iota(I32, (LANES, LANES), 0)
     one, zero = (jnp.ones((), BF16), jnp.zeros((), BF16))
-    for j in range(0, SLOTS, 2):
-        out = outs[j // 24]
-        if out is None:
-            continue
-        picks = []
-        for i in (j, j + 1):
-            wanted = jnp.broadcast_to(row[i : i + 1, :].astype(F32).astype(BF16), (CELLS, LANES))
-            picks.append(jnp.where(cells == wanted, one, zero))
-        pick = jnp.concatenate(picks, 1)
-        got = lax.dot_general(
-            weight[...],
-            jnp.concatenate([pick, pick], 0),
-            (((1,), (0,)), ((), ())),
-            preferred_element_type=F32,
-        )
-        for n, i in enumerate((j, j + 1)):
-            k, chunk = divmod(i, 8)
-            mask = columns == col[i : i + 1, :]
-            for field in range(2):
-                part = got[field * 128 : field * 128 + 128, n * 128 : n * 128 + 128]
-                at = k % 3 * 16 + field * 8 + chunk
-                out[at : at + 1, :] = jnp.sum(jnp.where(mask, part, 0.0), 0, keepdims=True)
-
-
-def here_kernel(row, col, weight, here):
-    gather_cells(row, col, weight, (None, here, None))
-
-
-def start_kernel(
-    head_in, sat_in, alpha_in, wet_in, row_in, col_in,
-    cond, row, col, minus, plus, edge_minus, edge_plus, weight,
-    head, sat, alpha_dry, wet, send_row, send_col, arrived,
-):
-    loads = [
-        pltpu.make_async_copy(source, target, arrived.at[i])
-        for i, (source, target) in enumerate(
-            (
-                (row_in, send_row), (col_in, send_col), (head_in, head), (alpha_in, alpha_dry), (wet_in, wet),
-                (sat_in, sat),
-            )
-        )
-    ]
-    for load in loads:
-        load.start()
-    loads[0].wait()
-    loads[1].wait()
-    for k in range(9):
-        for chunk in range(8):
-            at = k * 8 + chunk
-            row[at : at + 1, :] = send_row[0, k : k + 1, chunk * 128 : chunk * 128 + 128]
-            col[at : at + 1, :] = send_col[0, k : k + 1, chunk * 128 : chunk * 128 + 128]
-    for load in loads[2:]:
-        load.wait()
-    for layer in range(LAYERS):
-        at = slice(layer * 8, layer * 8 + 8)
-        cond[at, :] = conduct(head[at, :], sat[at, :], alpha_dry[at, :] * (1.0 + wet[at, :].astype(F32)))
-    lay_cells(head, cond, weight, minus, plus, edge_minus, edge_plus)
-    gather_cells(row, col, weight, (minus, None, plus))
+    for out, place in outs:
+        for dy in range(3):
+            rows8, cols8 = (eight(x, (place * 3 + dy) * 8) for x in (row, col))
+            for chunk in range(0, 8, 2):
+                picks = []
+                for i in (chunk, chunk + 1):
+                    wanted = rows8[i : i + 1].astype(F32).astype(BF16)
+                    wanted = jnp.broadcast_to(wanted, (CELLS, LANES))
+                    picks.append(jnp.where(cells == wanted, one, zero))
+                pick = jnp.concatenate(picks, 1)
+                got = lax.dot_general(
+                    weight[...],
+                    jnp.concatenate([pick, pick], 0),
+                    (((1,), (0,)), ((), ())),
+                    preferred_element_type=F32,
+                )
+                for n, i in enumerate((chunk, chunk + 1)):
+                    mask = columns == cols8[i : i + 1]
+                    for field in range(2):
+                        part = got[field * 128 : field * 128 + 128, n * 128 : n * 128 + 128]
+                        at = dy * 16 + field * 8 + i
+                        out[at : at + 1, :] = jnp.sum(jnp.where(mask, part, 0.0), 0, keepdims=True)
+
+
+def here_kernel(row, col, weight, _, here):
+    gather_cells(row, col, weight, ((here, 1),))
+
+
+def gather_far(head, cond, row, col, weight, chip, cross, edge_minus, edge_plus):
+    lay_cells(head, cond, weight, chip, cross, edge_minus, edge_plus)
+    chip_place, cross_place = x_places()
+    gather_cells(row, col, weight, ((chip, chip_place), (cross, cross_place)))
+
+
+def start_kernel(head, cond, row, col, chip, cross, edge_minus, edge_plus, weight):
+    gather_far(head, cond, row, col, weight, chip, cross, edge_minus, edge_plus)
 
 
 def terms_kernel(
-    head, cond, head_old, alpha_dry, wet, reversal, from_minus, from_plus, side_minus, side_plus,
+    head, cond, head_old, alpha_dry, wet, reversal, chip, cross, side_minus, side_plus,
     back_minus, back_here, back_plus, row, col,
     numerator, denominator, halo,
 ):
-    pieces = {3 + dy: (x, 8) for dy, x in enumerate((back_minus, back_here, back_plus))}
+    pieces = [(x, 8, 3 + dy) for dy, x in enumerate((back_minus, back_here, back_plus))]
     sink = SINK_GAIN * sink_of(pieces, row, col)
+    even = x_places()[0] == 2
+    from_plus = jnp.where(even, chip[48:112, :], cross[48:112, :])
+    from_minus = jnp.where(even, cross[48:112, :], chip[48:112, :])
     halo[...] = jnp.zeros_like(halo)
     turned = []
     for i in range(4):
@@ -155,13 +148,13 @@
 
         num, den = add(
             num, den,
-            beside(pltpu.roll(h, 7, 0), from_plus[48 + layer : 49 + layer, :], 7),
-            beside(pltpu.roll(c, 7, 0), from_plus[80 + layer : 81 + layer, :], 7),
+            beside(pltpu.roll(h, 7, 0), from_plus[layer : layer + 1], 7),
+            beside(pltpu.roll(c, 7, 0), from_plus[32 + layer : 33 + layer], 7),
         )
         num, den = add(
             num, den,
-            beside(pltpu.roll(h, 1, 0), from_minus[48 + layer : 49 + layer, :], 0),
-            beside(pltpu.roll(c, 1, 0), from_minus[80 + layer : 81 + layer, :], 0),
+            beside(pltpu.roll(h, 1, 0), from_minus[layer : layer + 1], 0),
+            beside(pltpu.roll(c, 1, 0), from_minus[32 + layer : 33 + layer], 0),
         )
         num, den = add(
             num, den,
@@ -187,18 +180,20 @@
 
 
 def root_kernel(
-    demand, from_minus, here, from_plus, side_minus, side_plus, code, radial_in, axial, stem, entry,
-    out_minus, out_here, out_plus, collar_out, weight, table, seg_head, seg_cond, uptake,
+    chip, here, cross, side_minus, side_plus, code, radial_in, axial, lines,
+    out_minus, out_here, out_plus, collar_out, weight, table, seg_head, seg_cond, uptake, summed,
 ):
-    for dx in range(3):
+    cross_place, chip_place = x_places()
+    places = (chip_place, 1, cross_place)
+    for n, place in enumerate(places):
         for dy in range(3):
             if dy == 1:
-                source, at = ((from_plus, here, from_minus)[dx], 16)
+                source, at = ((chip, here, cross)[n], 16)
             else:
-                source, at = ((side_plus, None, side_minus)[dy], (2 - dx) * 16)
+                source, at = ((side_plus, None, side_minus)[dy], n * 16)
             for field in range(2):
-                to = field * 72 + (dx * 3 + dy) * 8
-                table[to : to + 8, :] = source[at + field * 8 : at + field * 8 + 8, :]
+                to = pl.multiple_of(field * 72 + (place * 3 + dy) * 8, 8)
+                table[pl.ds(to, 8), :] = source[at + field * 8 : at + field * 8 + 8, :]
     weight[:, 0:128], weight[:, 128:256] = split(table[...])
     columns = lax.broadcasted_iota(I32, (128, LANES), 0).astype(F32).astype(BF16)
     rows = lax.broadcasted_iota(I32, (SLOTS, LANES), 0)
@@ -228,13 +223,13 @@
         at = slice(g * group, g * group + group)
         sub = lax.broadcasted_iota(I32, (group, LANES), 0) + g * group
         own = sub == lane
-        stem_col = jnp.sum(jnp.where(own, stem[...], 0.0), 1, keepdims=True)
-        entry_col = jnp.sum(jnp.where(own, entry[...], 0), 1, keepdims=True)
+        stem_col = jnp.sum(jnp.where(own, lines[0:1, :], 0.0), 1, keepdims=True)
+        entry_col = jnp.sum(jnp.where(own, lines[1:2, :], 0.0), 1, keepdims=True)
         hs, ks, rr = (seg_head[at, :], seg_cond[at, :], radial_in[at, :])
         radial = rr * ks / (rr + ks)
         right = jnp.where(lane == 127, 0.0, axial[at, :])
         left = pltpu.roll(right, 1, 1)
-        second = jnp.where(lane == entry_col, stem_col, 0.0)
+        second = jnp.where(lane.astype(F32) == entry_col, stem_col, 0.0)
         first = radial * hs
         diagonal = radial + second + left + right
         lower, upper = (-left, -right)
@@ -257,20 +252,18 @@
         def per_plant(x):
             return jnp.sum(jnp.sum(x.reshape(group // 8, 8, LANES), 1), 1, keepdims=True)
 
-        need = jnp.zeros((group // 8, 1), F32)
-        for p in range(group // 8):
-            need = jnp.where(plant_row == p, demand[g * (group // 8) + p], need)
+        mine = lax.broadcasted_iota(I32, (group // 8, LANES), 1) == plant_row + g * (group // 8)
+        need = jnp.sum(jnp.where(mine, lines[2:3, :], 0.0), 1, keepdims=True)
         head = (per_plant(radial * (hs - free)) - need) / per_plant(radial * collar)
         spread = jnp.broadcast_to(head[:, None, :], (group // 8, 8, LANES)).reshape(group, LANES)
         uptake[at, :] = radial * (hs - (free + spread * collar))
-        mine = lax.broadcasted_iota(I32, (group // 8, LANES), 1) == plant_row + g * (group // 8)
         collar_line = collar_line + jnp.sum(jnp.where(mine, head, 0.0), 0, keepdims=True)
-    collar_out[...] = collar_line
+    collar_out[...] = collar_line[:, 0:PLANTS]
     slot_rows = lax.broadcasted_iota(I32, (80, LANES), 0).astype(F32).astype(BF16)
     slot_cols = columns
     total = jnp.zeros((160, LANES), F32)
     for start in range(0, BLOCKS, 8):
-        values, places = ([], [])
+        values, spots = ([], [])
         for i in range(start, start + 8):
             where = code[i : i + 1, :]
             hi, lo = split(uptake[i : i + 1, :])
@@ -281,18 +274,17 @@
                 )
             )
             wanted = jnp.broadcast_to((where & 127).astype(F32).astype(BF16), (128, LANES))
-            places.append(jnp.where(slot_cols == wanted, one, zero))
+            spots.append(jnp.where(slot_cols == wanted, one, zero))
         total = total + lax.dot_general(
             jnp.concatenate(values, 1),
-            jnp.concatenate(places, 1),
+            jnp.concatenate(spots, 1),
             (((1,), (1,)), ((), ())),
             preferred_element_type=F32,
         )
-    summed = total[0:72] + total[80:152]
-    for dx in range(3):
+    summed[...] = total[0:72] + total[80:152]
+    for n, place in enumerate(places):
         for dy, out in enumerate((out_minus, out_here, out_plus)):
-            k = dx * 3 + dy
-            out[dx * 8 : dx * 8 + 8, :] = summed[k * 8 : k * 8 + 8]
+            out[n * 8 : n * 8 + 8, :] = eight(summed, (place * 3 + dy) * 8)
 
 
 def sink_of(pieces, row, col):
@@ -300,11 +292,11 @@
     places_of = lax.broadcasted_iota(I32, (256, LANES), 0).astype(F32).astype(BF16)
     one, zero = (jnp.ones((), BF16), jnp.zeros((), BF16))
     total = jnp.zeros((256, 256), F32)
-    for k, (source, base) in pieces.items():
+    for source, base, k in pieces:
         values, places = ([], [])
+        rows8, cols8 = (eight(x, k * 8) for x in (row, col))
         for chunk in range(8):
-            i = k * 8 + chunk
-            r, c = (row[i : i + 1, :], col[i : i + 1, :])
+            r, c = (rows8[chunk : chunk + 1], cols8[chunk : chunk + 1])
             hi, lo = split(source[base + chunk : base + chunk + 1, :])
             mask = low_rows == jnp.broadcast_to((r & 127).astype(F32).astype(BF16), (128, LANES))
             values.append(
@@ -323,11 +315,13 @@
     return total[0:128] + total[128:256]
 
 
-def new_head(from_minus, from_plus, row, col, numerator, denominator, head_new):
-    pieces = {}
-    for dx, source in ((0, from_minus), (2, from_plus)):
-        for dy in range(3):
-            pieces[dx * 3 + dy] = (source, dy * 8)
+def new_head(chip, cross, row, col, numerator, denominator, head_new):
+    places = x_places()
+    pieces = [
+        (source, dy * 8, places[n] * 3 + dy)
+        for n, source in enumerate((chip, cross))
+        for dy in range(3)
+    ]
     sink = sink_of(pieces, row, col)
     for half in range(2):
         at = slice(half * 128, half * 128 + 128)
@@ -335,19 +329,18 @@
 
 
 def next_kernel(
-    from_minus, from_plus, row, col, numerator, denominator, sat, alpha_dry, wet,
-    head, cond, minus, plus, edge_minus, edge_plus, weight,
+    chip_in, cross_in, row, col, numerator, denominator, sat, alpha_dry, wet,
+    head, cond, chip, cross, edge_minus, edge_plus, weight,
 ):
-    new_head(from_minus, from_plus, row, col, numerator, denominator, head)
+    new_head(chip_in, cross_in, row, col, numerator, denominator, head)
     for layer in range(LAYERS):
         at = slice(layer * 8, layer * 8 + 8)
         cond[at, :] = conduct(head[at, :], sat[at, :], alpha_dry[at, :] * (1.0 + wet[at, :].astype(F32)))
-    lay_cells(head, cond, weight, minus, plus, edge_minus, edge_plus)
-    gather_cells(row, col, weight, (minus, None, plus))
-
-
-def last_kernel(from_minus, from_plus, row, col, numerator, denominator, head):
-    new_head(from_minus, from_plus, row, col, numerator, denominator, head)
+    gather_far(head, cond, row, col, weight, chip, cross, edge_minus, edge_plus)
+
+
+def last_kernel(chip, cross, row, col, numerator, denominator, head):
+    new_head(chip, cross, row, col, numerator, denominator, head)
 
 
 def call(kernel, outs, scratch=(), specs=None, micros=1):
@@ -378,25 +371,27 @@
     return lax.ppermute(x, axis, [((i + 1) % size, i) for i in range(size)])
 
 
-def spread(row, col, minus, plus, edge_minus, edge_plus, weight):
-    from_minus = up(plus, "gx")
-    from_plus = down(minus, "gx")
-    (here,) = call(here_kernel, [((48, 128), F32)])(row, col, weight)
-    side_minus = up(
-        jnp.concatenate([from_minus[32:48], here[32:48], from_plus[32:48], edge_plus], 0), "gy"
-    )
-    side_plus = down(
-        jnp.concatenate([from_minus[0:16], here[0:16], from_plus[0:16], edge_minus], 0), "gy"
-    )
-    return (from_minus, here, from_plus, side_minus, side_plus)
+def swap(x, axis, first):
+    size = lax.axis_size(axis)
+    pairs = [((first + i) % size, (first + i + 1) % size) for i in range(0, size, 2)]
+    return lax.ppermute(x, axis, [p for i, j in pairs for p in ((i, j), (j, i))])
+
+
+def spread(row, col, chip, cross, edge_minus, edge_plus, weight):
+    from_cross = swap(cross, "gx", 1)
+    from_chip = swap(chip, "gx", 0)
+    (here,) = call(here_kernel, [((48, 128), F32)])(row, col, weight, from_chip)
+    parts = (from_chip, here, from_cross)
+    side_minus = up(jnp.concatenate([x[32:48] for x in parts] + [edge_plus], 0), "gy")
+    side_plus = down(jnp.concatenate([x[0:16] for x in parts] + [edge_minus], 0), "gy")
+    return (*parts, side_minus, side_plus)
 
 
 def give_back(minus, here, plus):
-    back_minus = up(minus, "gy")
-    back_plus = down(plus, "gy")
-    from_minus = up(jnp.concatenate([x[0:8] for x in (back_minus, here, back_plus)], 0), "gx")
-    from_plus = down(jnp.concatenate([x[16:24] for x in (back_minus, here, back_plus)], 0), "gx")
-    return ((back_minus, here, back_plus), (from_minus, from_plus))
+    back = (up(minus, "gy"), here, down(plus, "gy"))
+    from_cross = swap(jnp.concatenate([x[16:24] for x in back], 0), "gx", 1)
+    from_chip = swap(jnp.concatenate([x[0:8] for x in back], 0), "gx", 0)
+    return (back, (from_chip, from_cross))
 
 
 def on_device(
@@ -425,27 +420,21 @@
         lax.axis_index("gy") - source_dev % cols_gy + 1
     ) % cols_gy
     code = offset_k * send_row.shape[2] + source_slot
-    stem, entry = (stem_link.reshape(1, BLOCKS), entry_seg.reshape(1, BLOCKS))
+    lines = jnp.stack(
+        (stem_link, entry_seg.astype(F32), jnp.pad(demand, (0, BLOCKS - demand.shape[0])))
+    )
+    row, col = (x.reshape(SLOTS, LANES) for x in (send_row, send_col))
     head_old = head
-    far = pl.BlockSpec(memory_space=pltpu.HBM)
-    tile_scratch = [((CELLS, LANES), F32)] * 3 + [((CELLS, LANES), I32)] + [(send_row.shape, I32)] * 2
-    cond, row, col, *messages = call(
-        start_kernel,
-        [((CELLS, LANES), F32), ((SLOTS, LANES), I32), ((SLOTS, LANES), I32)] + MESSAGES,
-        tile_scratch + [pltpu.SemaphoreType.DMA((6,))],
-        specs=[far] * 6,
-        micros=4,
-    )(head, sat, alpha, wet, send_row, send_col)
-    smem = [pl.BlockSpec(memory_space=pltpu.SMEM)] + [pl.BlockSpec(memory_space=pltpu.VMEM)] * 10
+    cond = conduct(head, sat, alpha * (1.0 + wet.astype(F32)))
+    messages = call(start_kernel, MESSAGES, micros=3)(head, cond, row, col)
     for iteration in range(PICARD):
         got = spread(row, col, *messages)
         *sums, collar = call(
             root_kernel,
-            [((24, 128), F32)] * 3 + [((1, 128), F32)],
-            [((144, 256), BF16), ((144, 128), F32)] + [((128, 128), F32)] * 3,
-            specs=smem,
+            [((24, 128), F32)] * 3 + [((1, PLANTS), F32)],
+            [((144, 256), BF16), ((144, 128), F32)] + [((128, 128), F32)] * 3 + [((72, 128), F32)],
             micros=6,
-        )(demand, *got, code, root_radial, root_axial, stem, entry)
+        )(*got, code, root_radial, root_axial, lines)
         near, far_back = give_back(*sums)
         numerator, denominator = call(
             terms_kernel,
@@ -460,7 +449,7 @@
             (head,) = call(last_kernel, [((CELLS, LANES), F32)])(
                 *far_back, row, col, numerator, denominator
             )
-    return (head.reshape(tile), collar[0, :PLANTS])
+    return (head.reshape(tile), collar.reshape(-1))
 
 
 def solution(mesh):

time: 75.7 us -> 70.2 us (0.927)
  starting transfers between devices: 34.7 us -> 23.9 us
  waiting for transfers between devices: 11.2 us -> 20.7 us
  local copies, waits for them, and re-layouts: 4.85 us -> 1.27 us
  Pallas kernels: 23.5 us -> 21.7 us
  other arithmetic: 0.16 us -> 1.47 us
    ppermute x8 -> x4, starting transfers between devices: 27.5 us -> 7.29 us  [down(): return lax.ppermute(x, axis, [((i + 1) % size, i) for i in range(size)])]
    ppermute x0 -> x8, waiting for transfers between devices: none -> 12.8 us  [swap(): lax.ppermute(x, axis, [p for i, j in pairs for p in ((i, j), (j, i))])]
    ppermute x0 -> x8, starting transfers between devices: none -> 9.92 us  [swap(): lax.ppermute(x, axis, [p for i, j in pairs for p in ((i, j), (j, i))])]
    unnamed x34 -> x28, local copies, waits for them, and re-layouts: 4.31 us -> 1.23 us
    ppermute x8 -> x4, waiting for transfers between devices: 9.58 us -> 6.88 us  [up(): return lax.ppermute(x, axis, [(i, (i + 1) % size) for i in range(size)])]
    pallas_call x5, Pallas kernels: 15.2 us -> 13.4 us  [the longest x2 9.17 us: on_device(): call(root_kernel, [((24, 128), F32)] * 3 + [((1, PLANTS), F32)], [((144,...]
    mul x0 -> x1, other arithmetic: none -> 1.29 us  [conduct(): return sat_conduct * root * inner * inner]
    ppermute x8 -> x4, waiting for transfers between devices: 1.65 us -> 1.01 us  [down(): return lax.ppermute(x, axis, [((i + 1) % size, i) for i in range(size)])]
  transfers between devices with their start and end apart: 16 -> 16, of which waited for: 11 -> 11; matrix products, arithmetic and copies ran while one was open for 1% -> 0% of each run, Pallas kernels for 4% -> 6%
where the time goes in v3:
time: 70.2 us; the launch traced here: 70 us
  starting transfers between devices  23.9 us (34%)
  Pallas kernels  21.7 us (31%)
  waiting for transfers between devices  20.7 us (29%)
  other arithmetic  1.47 us (2%)
  local copies, waits for them, and re-layouts  1.27 us (2%)
  between operations  0.94 us (1%)
    ppermute x8, waiting for transfers between devices, swap(): lax.ppermute(x, axis, [p for i, j in pairs for p in ((i, j), (j, i))])  12.8 us
    ppermute x8, starting transfers between devices, swap(): lax.ppermute(x, axis, [p for i, j in pairs for p in ((i, j), (j, i))])  9.92 us
    pallas_call x2, Pallas kernels, on_device(): call(root_kernel, [((24, 128), F32)] * 3 + [((1, PLANTS), F32)], [((144,...  9.17 us
    ppermute x4, starting transfers between devices, down(): return lax.ppermute(x, axis, [((i + 1) % size, i) for i in range(size)])  7.29 us
    ppermute x4, waiting for transfers between devices, up(): return lax.ppermute(x, axis, [(i, (i + 1) % size) for i in range(size)])  6.88 us
    ppermute x4, starting transfers between devices, up(): return lax.ppermute(x, axis, [(i, (i + 1) % size) for i in range(size)])  6.69 us
    pallas_call x1, Pallas kernels, on_device(): call(next_kernel, [((CELLS, LANES), F32)] * 2 + MESSAGES, micros=5)  4.73 us
    pallas_call x2, Pallas kernels, spread(): here, = call(here_kernel, [((48, 128), F32)])(row, col, weight, from_chip)  2.21 us
  transfers between devices with their start and end apart: 16, of which 11 were waited for; matrix products, arithmetic and copies ran while one was open for 0% of the time, Pallas kernels for 6%

profile of v3, /device:TPU:0, one launch (start us, length us, event | category | flops | bytes accessed | tf_op | source)
XLA Modules:
  0.0 70.0 jit_solution(5610992954955780861)
XLA Ops:
  0.7 1.3 %multiply_multiply_fusion.cond = f32[256,128]{1,0:T(8,128)S(1)} fusion(s32[32,8,128]{2,1,0:T(8,128)} %param.17, f32[32,8,128]{2,1,0:T(8,128)} %param.16, f32[32,8,128]{2,1,0:T(8,128)} %param.15, f32[32,8,128]{2,1,0:T(8,128)} %param.14), kind=kLoop, calls=%fused_computation | loop fusion | flops 491520 | bytes 655360 | tf_op jit(solution)/shard_map/mul | solution.py:29
  2.0 2.0 %shard_map.149 = (f32[112,128]{1,0:T(8,128)S(1)}, f32[112,128]{1,0:T(8,128)S(1)}, f32[8,128]{1,0:T(8,128)S(1)}, f32[8,128]{1,0:T(8,128)S(1)}, bf16[256,512]{1,0:T(8,128)(2,1)S(1)}) custom-call(f32[256,128]{1,0:T(8,128)S(1)} %bitcast.19, f32[256,128]{1,0:T(8,128)S(1)} %multiply_multiply_fusion.cond, s32[72,128]{1,0:T(8,128)S(1)} %bitcast.31, ...), custom_call_target="tpu_custom_call" | custom-call | flops 3000000000 | bytes 9000000 | tf_op jit(solution)/shard_map/pallas_call | solution.py:429
  4.2 5.4 %collective-permute-start.1 = (f32[112,128]{1,0:T(8,128)S(1)}, f32[112,128]{1,0:T(8,128)S(1)}, u32[]{:S(2)}, u32[]{:S(2)}) collective-permute-start(f32[112,128]{1,0:T(8,128)S(1)} %get-tuple-element.27), channel_id=1, source_target_pairs={{4,8},{8,4},{12,16},{16,12},{20,24},{24,20},{28,32},{32,28},{36,40... | collective-permute-start | bytes 172040 | tf_op jit(solution)/shard_map/ppermute | solution.py:377
  12.1 2.0 %collective-permute-start.2 = (f32[56,128]{1,0:T(8,128)S(1)}, f32[56,128]{1,0:T(8,128)S(1)}, u32[]{:S(2)}, u32[]{:S(2)}) collective-permute-start(f32[56,128]{1,0:T(8,128)S(1)} %pad_maximum_fusion), channel_id=1, source_target_pairs={{0,1},{1,2},{2,3},{3,0},{4,5},{5,6},{6,7},{7,4},{8,9},{9,10},{10,1... | collective-permute-start | bytes 86024 | tf_op jit(solution)/shard_map/ppermute | solution.py:366
  14.1 2.2 %collective-permute-start.3 = (f32[56,128]{1,0:T(8,128)S(1)}, f32[56,128]{1,0:T(8,128)S(1)}, u32[]{:S(2)}, u32[]{:S(2)}) collective-permute-start(f32[56,128]{1,0:T(8,128)S(1)} %pad_maximum_fusion.1), channel_id=1, source_target_pairs={{1,0},{2,1},{3,2},{0,3},{5,4},{6,5},{7,6},{4,7},{9,8},{10,9},{11,1... | collective-permute-start | bytes 86024 | tf_op jit(solution)/shard_map/ppermute | solution.py:371
  16.3 1.7 %collective-permute-done.2.side_minus = f32[56,128]{1,0:T(8,128)S(1)} collective-permute-done((f32[56,128]{1,0:T(8,128)S(1)}, f32[56,128]{1,0:T(8,128)S(1)}, u32[]{:S(2)}, u32[]{:S(2)}) %collective-permute-start.2) | collective-permute-done | bytes 28704 | tf_op jit(solution)/shard_map/ppermute | solution.py:366
  18.0 4.6 %shard_map.151 = (f32[24,128]{1,0:T(8,128)S(1)}, f32[24,128]{1,0:T(8,128)S(1)}, f32[24,128]{1,0:T(8,128)S(1)}, f32[1,16]{1,0:T(1,128)}) custom-call(f32[112,128]{1,0:T(8,128)S(1)} %collective-permute-done._.chip, f32[48,128]{1,0:T(8,128)S(1)} %shard_map.150.here, f32[112,128]{1,0:T(8,128)S(1)} %collective-permute-done.1.cross, ...), custom_call_target="tpu_custom_call" | custom-call | flops 6000000000 | bytes 18000000 | tf_op jit(solution)/shard_map/pallas_call | solution.py:432
  22.6 1.8 %collective-permute-start.4 = (f32[24,128]{1,0:T(8,128)S(1)}, f32[24,128]{1,0:T(8,128)S(1)}, u32[]{:S(2)}, u32[]{:S(2)}) collective-permute-start(f32[24,128]{1,0:T(8,128)S(1)} %get-tuple-element.30), channel_id=1, source_target_pairs={{0,1},{1,2},{2,3},{3,0},{4,5},{5,6},{6,7},{7,4},{8,9},{9,10},{10,1... | collective-permute-start | bytes 36872 | tf_op jit(solution)/shard_map/ppermute | solution.py:366
  24.4 1.5 %collective-permute-start.5 = (f32[24,128]{1,0:T(8,128)S(1)}, f32[24,128]{1,0:T(8,128)S(1)}, u32[]{:S(2)}, u32[]{:S(2)}) collective-permute-start(f32[24,128]{1,0:T(8,128)S(1)} %get-tuple-element.32), channel_id=1, source_target_pairs={{1,0},{2,1},{3,2},{0,3},{5,4},{6,5},{7,6},{4,7},{9,8},{10,9},{11,1... | collective-permute-start | bytes 36872 | tf_op jit(solution)/shard_map/ppermute | solution.py:371
  25.9 1.7 %collective-permute-done.4.back_minus = f32[24,128]{1,0:T(8,128)S(1)} collective-permute-done((f32[24,128]{1,0:T(8,128)S(1)}, f32[24,128]{1,0:T(8,128)S(1)}, u32[]{:S(2)}, u32[]{:S(2)}) %collective-permute-start.4) | collective-permute-done | bytes 12320 | tf_op jit(solution)/shard_map/ppermute | solution.py:366
  28.1 2.2 %collective-permute-start.7 = (f32[24,128]{1,0:T(8,128)S(1)}, f32[24,128]{1,0:T(8,128)S(1)}, u32[]{:S(2)}, u32[]{:S(2)}) collective-permute-start(f32[24,128]{1,0:T(8,128)S(1)} %pad_maximum_fusion.5), channel_id=1, source_target_pairs={{4,8},{8,4},{12,16},{16,12},{20,24},{24,20},{28,32},{32,28},{36,40... | collective-permute-start | bytes 36872 | tf_op jit(solution)/shard_map/ppermute | solution.py:377
  31.3 3.5 %collective-permute-done.7.cross_in = f32[24,128]{1,0:T(8,128)S(1)} collective-permute-done((f32[24,128]{1,0:T(8,128)S(1)}, f32[24,128]{1,0:T(8,128)S(1)}, u32[]{:S(2)}, u32[]{:S(2)}) %collective-permute-start.7) | collective-permute-done | bytes 12320 | tf_op jit(solution)/shard_map/ppermute | solution.py:377
  34.9 4.7 %shard_map.153 = (f32[256,128]{1,0:T(8,128)S(1)}, f32[256,128]{1,0:T(8,128)S(1)}, f32[112,128]{1,0:T(8,128)S(1)}, f32[112,128]{1,0:T(8,128)S(1)}, f32[8,128]{1,0...) custom-call(f32[24,128]{1,0:T(8,128)S(1)} %collective-permute-done.6.chip_in, ...), custom_call_target="tpu_custom_call" | custom-call | flops 5000000000 | bytes 15000000 | tf_op jit(solution)/shard_map/pallas_call | solution.py:445
  39.7 2.0 %collective-permute-start.9 = (f32[112,128]{1,0:T(8,128)S(1)}, f32[112,128]{1,0:T(8,128)S(1)}, u32[]{:S(2)}, u32[]{:S(2)}) collective-permute-start(f32[112,128]{1,0:T(8,128)S(1)} %get-tuple-element.37), channel_id=1, source_target_pairs={{4,8},{8,4},{12,16},{16,12},{20,24},{24,20},{28,32},{32,28},{36,40... | collective-permute-start | bytes 172040 | tf_op jit(solution)/shard_map/ppermute | solution.py:377
  42.9 3.8 %collective-permute-done.9.cross = f32[112,128]{1,0:T(8,128)S(1)} collective-permute-done((f32[112,128]{1,0:T(8,128)S(1)}, f32[112,128]{1,0:T(8,128)S(1)}, u32[]{:S(2)}, u32[]{:S(2)}) %collective-permute-start.9) | collective-permute-done | bytes 57376 | tf_op jit(solution)/shard_map/ppermute | solution.py:377
  46.7 1.6 %collective-permute-start.10 = (f32[56,128]{1,0:T(8,128)S(1)}, f32[56,128]{1,0:T(8,128)S(1)}, u32[]{:S(2)}, u32[]{:S(2)}) collective-permute-start(f32[56,128]{1,0:T(8,128)S(1)} %pad_maximum_fusion.2), channel_id=1, source_target_pairs={{0,1},{1,2},{2,3},{3,0},{4,5},{5,6},{6,7},{7,4},{8,9},{9,10},{10,1... | collective-permute-start | bytes 86024 | tf_op jit(solution)/shard_map/ppermute | solution.py:366
  48.3 1.6 %collective-permute-start.11 = (f32[56,128]{1,0:T(8,128)S(1)}, f32[56,128]{1,0:T(8,128)S(1)}, u32[]{:S(2)}, u32[]{:S(2)}) collective-permute-start(f32[56,128]{1,0:T(8,128)S(1)} %pad_maximum_fusion.3), channel_id=1, source_target_pairs={{1,0},{2,1},{3,2},{0,3},{5,4},{6,5},{7,6},{4,7},{9,8},{10,9},{11,1... | collective-permute-start | bytes 86024 | tf_op jit(solution)/shard_map/ppermute | solution.py:371
  49.9 1.8 %collective-permute-done.10.side_minus = f32[56,128]{1,0:T(8,128)S(1)} collective-permute-done((f32[56,128]{1,0:T(8,128)S(1)}, f32[56,128]{1,0:T(8,128)S(1)}, u32[]{:S(2)}, u32[]{:S(2)}) %collective-permute-start.10) | collective-permute-done | bytes 28704 | tf_op jit(solution)/shard_map/ppermute | solution.py:366
  52.2 4.6 %shard_map.155 = (f32[24,128]{1,0:T(8,128)S(1)}, f32[24,128]{1,0:T(8,128)S(1)}, f32[24,128]{1,0:T(8,128)S(1)}, f32[1,16]{1,0:T(1,128)}) custom-call(f32[112,128]{1,0:T(8,128)S(1)} %collective-permute-done.8._.chip, f32[48,128]{1,0:T(8,128)S(1)} %shard_map.154.here, f32[112,128]{1,0:T(8,128)S(1)} %collective-permute-done.9.cross, ...), custom_call_target="tpu_custom_call" | custom-call | flops 6000000000 | bytes 18000000 | tf_op jit(solution)/shard_map/pallas_call | solution.py:432
  56.8 1.3 %collective-permute-start.12 = (f32[24,128]{1,0:T(8,128)S(1)}, f32[24,128]{1,0:T(8,128)S(1)}, u32[]{:S(2)}, u32[]{:S(2)}) collective-permute-start(f32[24,128]{1,0:T(8,128)S(1)} %get-tuple-element.40), channel_id=1, source_target_pairs={{0,1},{1,2},{2,3},{3,0},{4,5},{5,6},{6,7},{7,4},{8,9},{9,10},{10,1... | collective-permute-start | bytes 36872 | tf_op jit(solution)/shard_map/ppermute | solution.py:366
  58.0 2.0 %collective-permute-start.13 = (f32[24,128]{1,0:T(8,128)S(1)}, f32[24,128]{1,0:T(8,128)S(1)}, u32[]{:S(2)}, u32[]{:S(2)}) collective-permute-start(f32[24,128]{1,0:T(8,128)S(1)} %get-tuple-element.42), channel_id=1, source_target_pairs={{1,0},{2,1},{3,2},{0,3},{5,4},{6,5},{7,6},{4,7},{9,8},{10,9},{11,1... | collective-permute-start | bytes 36872 | tf_op jit(solution)/shard_map/ppermute | solution.py:371
  60.0 1.7 %collective-permute-done.12.back_minus = f32[24,128]{1,0:T(8,128)S(1)} collective-permute-done((f32[24,128]{1,0:T(8,128)S(1)}, f32[24,128]{1,0:T(8,128)S(1)}, u32[]{:S(2)}, u32[]{:S(2)}) %collective-permute-start.12) | collective-permute-done | bytes 12320 | tf_op jit(solution)/shard_map/ppermute | solution.py:366
  62.9 5.4 %collective-permute-done.15.cross = f32[24,128]{1,0:T(8,128)S(1)} collective-permute-done((f32[24,128]{1,0:T(8,128)S(1)}, f32[24,128]{1,0:T(8,128)S(1)}, u32[]{:S(2)}, u32[]{:S(2)}) %collective-permute-start.15) | collective-permute-done | bytes 12320 | tf_op jit(solution)/shard_map/ppermute | solution.py:377
  68.3 1.7 %shard_map.157 = f32[256,128]{1,0:T(8,128)} custom-call(f32[24,128]{1,0:T(8,128)S(1)} %collective-permute-done.14.chip, f32[24,128]{1,0:T(8,128)S(1)} %collective-permute-done.15.cross, s32[72,128]{1,0:T(8,128)S(1)} %bitcast.37, s32[72,128]{1,0:T(8,128)S(1)} %bitcast.44, f32[256,128]{1,0:T(8,128)S(1)} %get-tuple-element.45.numerator, ...), custom_call_target="tpu_custom_call" | custom-call | flops 1000000000 | bytes 3000000 | tf_op jit(solution)/shard_map/pallas_call | solution.py:449
  (69 shorter events, 6.9 us)
Async XLA Ops:
  2.0 8.2 %copy-start.9 = (s32[128,128]{1,0:T(8,128)S(1)}, s32[128,128]{1,0:T(8,128)}, u32[]{:S(2)}) copy-start(s32[128,128]{1,0:T(8,128)} %param.26) | copy-start | bytes 196612
  2.0 8.2 %copy-start.10 = (s32[128,128]{1,0:T(8,128)S(1)}, s32[128,128]{1,0:T(8,128)}, u32[]{:S(2)}) copy-start(s32[128,128]{1,0:T(8,128)} %param.25) | copy-start | bytes 196612
  4.1 6.8 %collective-permute-start = (f32[112,128]{1,0:T(8,128)S(1)}, f32[112,128]{1,0:T(8,128)S(1)}, u32[]{:S(2)}, u32[]{:S(2)}) collective-permute-start(f32[112,128]{1,0:T(8,128)S(1)} %get-tuple-element.25), channel_id=1, source_target_pairs={{0,4},{4,0},{8,12},{12,8},{16,20},{20,16},{24,28},{28,24},{32,36},... | collective-permute-start | bytes 172040 | tf_op jit(solution)/shard_map/ppermute | solution.py:377
  4.2 7.9 %collective-permute-start.1 = (f32[112,128]{1,0:T(8,128)S(1)}, f32[112,128]{1,0:T(8,128)S(1)}, u32[]{:S(2)}, u32[]{:S(2)}) collective-permute-start(f32[112,128]{1,0:T(8,128)S(1)} %get-tuple-element.27), channel_id=1, source_target_pairs={{4,8},{8,4},{12,16},{16,12},{20,24},{24,20},{28,32},{32,28},{36,40... | collective-permute-start | bytes 172040 | tf_op jit(solution)/shard_map/ppermute | solution.py:377
  12.0 6.0 %copy-start.5 = (f32[128,128]{1,0:T(8,128)S(1)}, f32[128,128]{1,0:T(8,128)}, u32[]{:S(2)}) copy-start(f32[128,128]{1,0:T(8,128)} %radial_in.3) | copy-start | bytes 196612
  12.0 6.0 %copy-start.6 = (f32[128,128]{1,0:T(8,128)S(1)}, f32[128,128]{1,0:T(8,128)}, u32[]{:S(2)}) copy-start(f32[128,128]{1,0:T(8,128)} %axial.3) | copy-start | bytes 196612
  12.1 6.0 %collective-permute-start.2 = (f32[56,128]{1,0:T(8,128)S(1)}, f32[56,128]{1,0:T(8,128)S(1)}, u32[]{:S(2)}, u32[]{:S(2)}) collective-permute-start(f32[56,128]{1,0:T(8,128)S(1)} %pad_maximum_fusion), channel_id=1, source_target_pairs={{0,1},{1,2},{2,3},{3,0},{4,5},{5,6},{6,7},{7,4},{8,9},{9,10},{10,1... | collective-permute-start | bytes 86024 | tf_op jit(solution)/shard_map/ppermute | solution.py:366
  14.1 4.0 %collective-permute-start.3 = (f32[56,128]{1,0:T(8,128)S(1)}, f32[56,128]{1,0:T(8,128)S(1)}, u32[]{:S(2)}, u32[]{:S(2)}) collective-permute-start(f32[56,128]{1,0:T(8,128)S(1)} %pad_maximum_fusion.1), channel_id=1, source_target_pairs={{1,0},{2,1},{3,2},{0,3},{5,4},{6,5},{7,6},{4,7},{9,8},{10,9},{11,1... | collective-permute-start | bytes 86024 | tf_op jit(solution)/shard_map/ppermute | solution.py:371
  16.3 14.1 %copy-start.2 = (s32[32,8,128]{2,1,0:T(8,128)S(1)}, s32[32,8,128]{2,1,0:T(8,128)}, u32[]{:S(2)}) copy-start(s32[32,8,128]{2,1,0:T(8,128)} %param.17) | copy-start | bytes 393220
  16.3 14.1 %copy-start.3 = (f32[32,8,128]{2,1,0:T(8,128)S(1)}, f32[32,8,128]{2,1,0:T(8,128)}, u32[]{:S(2)}) copy-start(f32[32,8,128]{2,1,0:T(8,128)} %param.16) | copy-start | bytes 393220
  16.3 14.1 %copy-start.4 = (f32[32,8,128]{2,1,0:T(8,128)S(1)}, f32[32,8,128]{2,1,0:T(8,128)}, u32[]{:S(2)}) copy-start(f32[32,8,128]{2,1,0:T(8,128)} %param.18) | copy-start | bytes 393220
  22.6 5.0 %collective-permute-start.4 = (f32[24,128]{1,0:T(8,128)S(1)}, f32[24,128]{1,0:T(8,128)S(1)}, u32[]{:S(2)}, u32[]{:S(2)}) collective-permute-start(f32[24,128]{1,0:T(8,128)S(1)} %get-tuple-element.30), channel_id=1, source_target_pairs={{0,1},{1,2},{2,3},{3,0},{4,5},{5,6},{6,7},{7,4},{8,9},{9,10},{10,1... | collective-permute-start | bytes 36872 | tf_op jit(solution)/shard_map/ppermute | solution.py:366
  24.4 3.7 %collective-permute-start.5 = (f32[24,128]{1,0:T(8,128)S(1)}, f32[24,128]{1,0:T(8,128)S(1)}, u32[]{:S(2)}, u32[]{:S(2)}) collective-permute-start(f32[24,128]{1,0:T(8,128)S(1)} %get-tuple-element.32), channel_id=1, source_target_pairs={{1,0},{2,1},{3,2},{0,3},{5,4},{6,5},{7,6},{4,7},{9,8},{10,9},{11,1... | collective-permute-start | bytes 36872 | tf_op jit(solution)/shard_map/ppermute | solution.py:371
  28.1 3.2 %collective-permute-start.6 = (f32[24,128]{1,0:T(8,128)S(1)}, f32[24,128]{1,0:T(8,128)S(1)}, u32[]{:S(2)}, u32[]{:S(2)}) collective-permute-start(f32[24,128]{1,0:T(8,128)S(1)} %pad_maximum_fusion.4), channel_id=1, source_target_pairs={{0,4},{4,0},{8,12},{12,8},{16,20},{20,16},{24,28},{28,24},{32,36},... | collective-permute-start | bytes 36872 | tf_op jit(solution)/shard_map/ppermute | solution.py:377
  28.1 6.7 %collective-permute-start.7 = (f32[24,128]{1,0:T(8,128)S(1)}, f32[24,128]{1,0:T(8,128)S(1)}, u32[]{:S(2)}, u32[]{:S(2)}) collective-permute-start(f32[24,128]{1,0:T(8,128)S(1)} %pad_maximum_fusion.5), channel_id=1, source_target_pairs={{4,8},{8,4},{12,16},{16,12},{20,24},{24,20},{28,32},{32,28},{36,40... | collective-permute-start | bytes 36872 | tf_op jit(solution)/shard_map/ppermute | solution.py:377
  30.4 4.5 %copy-start = (f32[32,8,128]{2,1,0:T(8,128)S(1)}, f32[32,8,128]{2,1,0:T(8,128)}, u32[]{:S(2)}) copy-start(f32[32,8,128]{2,1,0:T(8,128)} %param.15) | copy-start | bytes 393220
  39.6 2.1 %collective-permute-start.8 = (f32[112,128]{1,0:T(8,128)S(1)}, f32[112,128]{1,0:T(8,128)S(1)}, u32[]{:S(2)}, u32[]{:S(2)}) collective-permute-start(f32[112,128]{1,0:T(8,128)S(1)} %get-tuple-element.35), channel_id=1, source_target_pairs={{0,4},{4,0},{8,12},{12,8},{16,20},{20,16},{24,28},{28,24},{32,36},... | collective-permute-start | bytes 172040 | tf_op jit(solution)/shard_map/ppermute | solution.py:377
  39.7 7.0 %collective-permute-start.9 = (f32[112,128]{1,0:T(8,128)S(1)}, f32[112,128]{1,0:T(8,128)S(1)}, u32[]{:S(2)}, u32[]{:S(2)}) collective-permute-start(f32[112,128]{1,0:T(8,128)S(1)} %get-tuple-element.37), channel_id=1, source_target_pairs={{4,8},{8,4},{12,16},{16,12},{20,24},{24,20},{28,32},{32,28},{36,40... | collective-permute-start | bytes 172040 | tf_op jit(solution)/shard_map/ppermute | solution.py:377
  46.7 5.1 %collective-permute-start.10 = (f32[56,128]{1,0:T(8,128)S(1)}, f32[56,128]{1,0:T(8,128)S(1)}, u32[]{:S(2)}, u32[]{:S(2)}) collective-permute-start(f32[56,128]{1,0:T(8,128)S(1)} %pad_maximum_fusion.2), channel_id=1, source_target_pairs={{0,1},{1,2},{2,3},{3,0},{4,5},{5,6},{6,7},{7,4},{8,9},{9,10},{10,1... | collective-permute-start | bytes 86024 | tf_op jit(solution)/shard_map/ppermute | solution.py:366
  48.3 3.9 %collective-permute-start.11 = (f32[56,128]{1,0:T(8,128)S(1)}, f32[56,128]{1,0:T(8,128)S(1)}, u32[]{:S(2)}, u32[]{:S(2)}) collective-permute-start(f32[56,128]{1,0:T(8,128)S(1)} %pad_maximum_fusion.3), channel_id=1, source_target_pairs={{1,0},{2,1},{3,2},{0,3},{5,4},{6,5},{7,6},{4,7},{9,8},{10,9},{11,1... | collective-permute-start | bytes 86024 | tf_op jit(solution)/shard_map/ppermute | solution.py:371
  56.8 4.9 %collective-permute-start.12 = (f32[24,128]{1,0:T(8,128)S(1)}, f32[24,128]{1,0:T(8,128)S(1)}, u32[]{:S(2)}, u32[]{:S(2)}) collective-permute-start(f32[24,128]{1,0:T(8,128)S(1)} %get-tuple-element.40), channel_id=1, source_target_pairs={{0,1},{1,2},{2,3},{3,0},{4,5},{5,6},{6,7},{7,4},{8,9},{9,10},{10,1... | collective-permute-start | bytes 36872 | tf_op jit(solution)/shard_map/ppermute | solution.py:366
  58.0 3.7 %collective-permute-start.13 = (f32[24,128]{1,0:T(8,128)S(1)}, f32[24,128]{1,0:T(8,128)S(1)}, u32[]{:S(2)}, u32[]{:S(2)}) collective-permute-start(f32[24,128]{1,0:T(8,128)S(1)} %get-tuple-element.42), channel_id=1, source_target_pairs={{1,0},{2,1},{3,2},{0,3},{5,4},{6,5},{7,6},{4,7},{9,8},{10,9},{11,1... | collective-permute-start | bytes 36872 | tf_op jit(solution)/shard_map/ppermute | solution.py:371
  61.8 1.2 %collective-permute-start.14 = (f32[24,128]{1,0:T(8,128)S(1)}, f32[24,128]{1,0:T(8,128)S(1)}, u32[]{:S(2)}, u32[]{:S(2)}) collective-permute-start(f32[24,128]{1,0:T(8,128)S(1)} %pad_maximum_fusion.6), channel_id=1, source_target_pairs={{0,4},{4,0},{8,12},{12,8},{16,20},{20,16},{24,28},{28,24},{32,36},... | collective-permute-start | bytes 36872 | tf_op jit(solution)/shard_map/ppermute | solution.py:377
  61.8 6.5 %collective-permute-start.15 = (f32[24,128]{1,0:T(8,128)S(1)}, f32[24,128]{1,0:T(8,128)S(1)}, u32[]{:S(2)}, u32[]{:S(2)}) collective-permute-start(f32[24,128]{1,0:T(8,128)S(1)} %pad_maximum_fusion.7), channel_id=1, source_target_pairs={{4,8},{8,4},{12,16},{16,12},{20,24},{24,20},{28,32},{32,28},{36,40... | collective-permute-start | bytes 36872 | tf_op jit(solution)/shard_map/ppermute | solution.py:377
  (6 other events, 9.6 us)

commit v4 on v3

--- a/solution.py
+++ b/solution.py
@@ -61,8 +61,9 @@
             weight[field * 128 : field * 128 + 128, 256 + half * 128 : 384 + half * 128] = lo
         first = ref[pl.ds(0, LAYERS, stride=8), :]
         last = ref[pl.ds(7, LAYERS, stride=8), :]
-        chip[48 + 32 * field : 80 + 32 * field, :] = jnp.where(even, last, first)
-        cross[48 + 32 * field : 80 + 32 * field, :] = jnp.where(even, first, last)
+        at = chip.shape[0] - 64 + 32 * field
+        chip[at : at + 32, :] = jnp.where(even, last, first)
+        cross[at : at + 32, :] = jnp.where(even, first, last)
     edge_minus[4:8, :] = jnp.zeros((4, LANES), F32)
     edge_plus[4:8, :] = jnp.zeros((4, LANES), F32)
 
@@ -99,26 +100,42 @@
                         out[at : at + 1, :] = jnp.sum(jnp.where(mask, part, 0.0), 0, keepdims=True)
 
 
+def gather_far(row, col, weight, chip, cross):
+    chip_place, cross_place = x_places()
+    gather_cells(row, col, weight, ((cross, cross_place), (chip, chip_place)))
+
+
+def start_kernel(head, cond, row, col, chip, cross, edge_minus, edge_plus, weight):
+    lay_cells(head, cond, weight, chip, cross, edge_minus, edge_plus)
+    gather_far(row, col, weight, chip, cross)
+
+
+def far_kernel(row, col, weight, chip_edge, cross_edge, chip, cross):
+    gather_far(row, col, weight, chip, cross)
+    chip[48:112, :] = chip_edge[...]
+    cross[48:112, :] = cross_edge[...]
+
+
 def here_kernel(row, col, weight, _, here):
     gather_cells(row, col, weight, ((here, 1),))
 
 
-def gather_far(head, cond, row, col, weight, chip, cross, edge_minus, edge_plus):
-    lay_cells(head, cond, weight, chip, cross, edge_minus, edge_plus)
-    chip_place, cross_place = x_places()
-    gather_cells(row, col, weight, ((chip, chip_place), (cross, cross_place)))
-
-
-def start_kernel(head, cond, row, col, chip, cross, edge_minus, edge_plus, weight):
-    gather_far(head, cond, row, col, weight, chip, cross, edge_minus, edge_plus)
+def collar_kernel(lines, second):
+    sub = lax.broadcasted_iota(I32, (BLOCKS, LANES), 0)
+    lane = lax.broadcasted_iota(I32, (BLOCKS, LANES), 1)
+    own = sub == lane
+    stem = jnp.sum(jnp.where(own, lines[0:1, :], 0.0), 1, keepdims=True)
+    entry = jnp.sum(jnp.where(own, lines[1:2, :], 0.0), 1, keepdims=True)
+    second[...] = jnp.where(lane.astype(F32) == entry, stem, 0.0)
 
 
 def terms_kernel(
     head, cond, head_old, alpha_dry, wet, reversal, chip, cross, side_minus, side_plus,
-    back_minus, back_here, back_plus, row, col,
+    back_minus, back_here, back_plus, back_chip, row, col,
     numerator, denominator, halo,
 ):
     pieces = [(x, 8, 3 + dy) for dy, x in enumerate((back_minus, back_here, back_plus))]
+    pieces += [(back_chip, dy * 8, x_places()[0] * 3 + dy) for dy in range(3)]
     sink = SINK_GAIN * sink_of(pieces, row, col)
     even = x_places()[0] == 2
     from_plus = jnp.where(even, chip[48:112, :], cross[48:112, :])
@@ -180,7 +197,7 @@
 
 
 def root_kernel(
-    chip, here, cross, side_minus, side_plus, code, radial_in, axial, lines,
+    chip, here, cross, side_minus, side_plus, code, radial_in, axial, lines, collar_link,
     out_minus, out_here, out_plus, collar_out, weight, table, seg_head, seg_cond, uptake, summed,
 ):
     cross_place, chip_place = x_places()
@@ -198,9 +215,9 @@
     columns = lax.broadcasted_iota(I32, (128, LANES), 0).astype(F32).astype(BF16)
     rows = lax.broadcasted_iota(I32, (SLOTS, LANES), 0)
     one, zero = (jnp.ones((), BF16), jnp.zeros((), BF16))
-    for j in range(0, BLOCKS, 2):
+    for j in range(0, BLOCKS, 8):
         picks = []
-        for i in (j, j + 1):
+        for i in range(j, j + 8):
             wanted = jnp.broadcast_to((code[i : i + 1, :] & 127).astype(F32).astype(BF16), (128, LANES))
             picks.append(jnp.where(columns == wanted, one, zero))
         pick = jnp.concatenate(picks, 1)
@@ -210,7 +227,7 @@
             (((1,), (0,)), ((), ())),
             preferred_element_type=F32,
         )
-        for n, i in enumerate((j, j + 1)):
+        for n, i in enumerate(range(j, j + 8)):
             mask = rows == (code[i : i + 1, :] >> 7)
             for field, ref in enumerate((seg_head, seg_cond)):
                 part = got[field * 72 : field * 72 + 72, n * 128 : n * 128 + 128]
@@ -221,15 +238,11 @@
     collar_line = jnp.zeros((1, LANES), F32)
     for g in range(BLOCKS // group):
         at = slice(g * group, g * group + group)
-        sub = lax.broadcasted_iota(I32, (group, LANES), 0) + g * group
-        own = sub == lane
-        stem_col = jnp.sum(jnp.where(own, lines[0:1, :], 0.0), 1, keepdims=True)
-        entry_col = jnp.sum(jnp.where(own, lines[1:2, :], 0.0), 1, keepdims=True)
         hs, ks, rr = (seg_head[at, :], seg_cond[at, :], radial_in[at, :])
         radial = rr * ks / (rr + ks)
         right = jnp.where(lane == 127, 0.0, axial[at, :])
         left = pltpu.roll(right, 1, 1)
-        second = jnp.where(lane.astype(F32) == entry_col, stem_col, 0.0)
+        second = collar_link[at, :]
         first = radial * hs
         diagonal = radial + second + left + right
         lower, upper = (-left, -right)
@@ -315,32 +328,27 @@
     return total[0:128] + total[128:256]
 
 
-def new_head(chip, cross, row, col, numerator, denominator, head_new):
-    places = x_places()
-    pieces = [
-        (source, dy * 8, places[n] * 3 + dy)
-        for n, source in enumerate((chip, cross))
-        for dy in range(3)
-    ]
-    sink = sink_of(pieces, row, col)
+def new_head(cross, row, col, numerator, denominator, head_new):
+    place = x_places()[1]
+    sink = sink_of([(cross, dy * 8, place * 3 + dy) for dy in range(3)], row, col)
     for half in range(2):
         at = slice(half * 128, half * 128 + 128)
         head_new[at, :] = (numerator[at, :] - SINK_GAIN * sink[:, at]) / denominator[at, :]
 
 
 def next_kernel(
-    chip_in, cross_in, row, col, numerator, denominator, sat, alpha_dry, wet,
-    head, cond, chip, cross, edge_minus, edge_plus, weight,
+    cross, row, col, numerator, denominator, sat, alpha_dry, wet,
+    head, cond, chip_edge, cross_edge, edge_minus, edge_plus, weight,
 ):
-    new_head(chip_in, cross_in, row, col, numerator, denominator, head)
+    new_head(cross, row, col, numerator, denominator, head)
     for layer in range(LAYERS):
         at = slice(layer * 8, layer * 8 + 8)
         cond[at, :] = conduct(head[at, :], sat[at, :], alpha_dry[at, :] * (1.0 + wet[at, :].astype(F32)))
-    gather_far(head, cond, row, col, weight, chip, cross, edge_minus, edge_plus)
-
-
-def last_kernel(chip, cross, row, col, numerator, denominator, head):
-    new_head(chip, cross, row, col, numerator, denominator, head)
+    lay_cells(head, cond, weight, chip_edge, cross_edge, edge_minus, edge_plus)
+
+
+def last_kernel(cross, row, col, numerator, denominator, head):
+    new_head(cross, row, col, numerator, denominator, head)
 
 
 def call(kernel, outs, scratch=(), specs=None, micros=1):
@@ -357,8 +365,9 @@
     )
 
 
-WEIGHT = ((256, 512), BF16)
-MESSAGES = [((112, 128), F32), ((112, 128), F32), ((8, 128), F32), ((8, 128), F32), WEIGHT]
+MESSAGE = ((112, 128), F32)
+EDGE = ((64, 128), F32)
+SIDES = [((8, 128), F32)] * 2 + [((256, 512), BF16)]
 
 
 def up(x, axis):
@@ -426,7 +435,8 @@
     row, col = (x.reshape(SLOTS, LANES) for x in (send_row, send_col))
     head_old = head
     cond = conduct(head, sat, alpha * (1.0 + wet.astype(F32)))
-    messages = call(start_kernel, MESSAGES, micros=3)(head, cond, row, col)
+    messages = call(start_kernel, [MESSAGE] * 2 + SIDES, micros=2)(head, cond, row, col)
+    (collar_link,) = call(collar_kernel, [((BLOCKS, LANES), F32)])(lines)
     for iteration in range(PICARD):
         got = spread(row, col, *messages)
         *sums, collar = call(
@@ -434,20 +444,25 @@
             [((24, 128), F32)] * 3 + [((1, PLANTS), F32)],
             [((144, 256), BF16), ((144, 128), F32)] + [((128, 128), F32)] * 3 + [((72, 128), F32)],
             micros=6,
-        )(*got, code, root_radial, root_axial, lines)
-        near, far_back = give_back(*sums)
+        )(*got, code, root_radial, root_axial, lines, collar_link)
+        near, (from_chip, from_cross) = give_back(*sums)
         numerator, denominator = call(
             terms_kernel,
             [((CELLS, LANES), F32)] * 2,
             [((128, 128), F32)],
-        )(head, cond, head_old, alpha, wet, reversal, got[0], got[2], got[3], got[4], *near, row, col)
+        )(
+            head, cond, head_old, alpha, wet, reversal, got[0], got[2], got[3], got[4],
+            *near, from_chip, row, col,
+        )
         if iteration < PICARD - 1:
-            head, cond, *messages = call(
-                next_kernel, [((CELLS, LANES), F32)] * 2 + MESSAGES, micros=5
-            )(*far_back, row, col, numerator, denominator, sat, alpha, wet)
+            head, cond, *edges, side_minus, side_plus, weight = call(
+                next_kernel, [((CELLS, LANES), F32)] * 2 + [EDGE] * 2 + SIDES, micros=2
+            )(from_cross, row, col, numerator, denominator, sat, alpha, wet)
+            far = call(far_kernel, [MESSAGE] * 2, micros=2)(row, col, weight, *edges)
+            messages = (*far, side_minus, side_plus, weight)
         else:
             (head,) = call(last_kernel, [((CELLS, LANES), F32)])(
-                *far_back, row, col, numerator, denominator
+                from_cross, row, col, numerator, denominator
             )
     return (head.reshape(tile), collar.reshape(-1))
 

time: 70.2 us -> 68.7 us (0.979)
  starting transfers between devices: 23.9 us -> 22.2 us
  Pallas kernels: 21.7 us -> 20.3 us
  waiting for transfers between devices: 20.7 us -> 21.6 us
  local copies, waits for them, and re-layouts: 1.27 us -> 2.05 us
    ppermute x8, starting transfers between devices: 9.92 us -> 8.2 us  [swap(): lax.ppermute(x, axis, [p for i, j in pairs for p in ((i, j), (j, i))])]
    pallas_call x2 -> x4, Pallas kernels: 6.78 us -> 5.09 us  [the longest x1 2.1 us: on_device(): far = call(far_kernel, [MESSAGE] * 2, micros=2)(row, col, weight, *edges)]
    ppermute x8, waiting for transfers between devices: 12.8 us -> 13.8 us  [swap(): lax.ppermute(x, axis, [p for i, j in pairs for p in ((i, j), (j, i))])]
    unnamed x28, local copies, waits for them, and re-layouts: 1.23 us -> 2.01 us
    pallas_call x2, Pallas kernels: 1.88 us -> 2.64 us  [on_device(): call(terms_kernel, [((CELLS, LANES), F32)] * 2, [((128, 128), F32)])]
  transfers between devices with their start and end apart: 16 -> 16, of which waited for: 11 -> 11; matrix products, arithmetic and copies ran while one was open for 0% -> 0% of each run, Pallas kernels for 6% -> 7%
where the time goes in v4:
time: 68.7 us; the launch traced here: 68.6 us
  starting transfers between devices  22.2 us (32%)
  waiting for transfers between devices  21.6 us (31%)
  Pallas kernels  20.3 us (30%)
  local copies, waits for them, and re-layouts  2.05 us (3%)
  other arithmetic  1.47 us (2%)
  between operations  0.94 us (1%)
    ppermute x8, waiting for transfers between devices, swap(): lax.ppermute(x, axis, [p for i, j in pairs for p in ((i, j), (j, i))])  13.8 us
    pallas_call x2, Pallas kernels, on_device(): call(root_kernel, [((24, 128), F32)] * 3 + [((1, PLANTS), F32)], [((144,...  9.05 us
    ppermute x8, starting transfers between devices, swap(): lax.ppermute(x, axis, [p for i, j in pairs for p in ((i, j), (j, i))])  8.2 us
    ppermute x4, starting transfers between devices, down(): return lax.ppermute(x, axis, [((i + 1) % size, i) for i in range(size)])  7.29 us
    ppermute x4, waiting for transfers between devices, up(): return lax.ppermute(x, axis, [(i, (i + 1) % size) for i in range(size)])  6.75 us
    ppermute x4, starting transfers between devices, up(): return lax.ppermute(x, axis, [(i, (i + 1) % size) for i in range(size)])  6.75 us
    pallas_call x2, Pallas kernels, on_device(): call(terms_kernel, [((CELLS, LANES), F32)] * 2, [((128, 128), F32)])  2.64 us
    pallas_call x2, Pallas kernels, spread(): here, = call(here_kernel, [((48, 128), F32)])(row, col, weight, from_chip)  2.21 us
  transfers between devices with their start and end apart: 16, of which 11 were waited for; matrix products, arithmetic and copies ran while one was open for 0% of the time, Pallas kernels for 7%

profile of v4, /device:TPU:0, one launch (start us, length us, event | category | flops | bytes accessed | tf_op | source)
XLA Modules:
  0.0 68.6 jit_solution(12182633493118046803)
XLA Ops:
  0.7 1.3 %multiply_multiply_fusion.cond = f32[256,128]{1,0:T(8,128)S(1)} fusion(s32[32,8,128]{2,1,0:T(8,128)} %param.17, f32[32,8,128]{2,1,0:T(8,128)} %param.16, f32[32,8,128]{2,1,0:T(8,128)} %param.15, f32[32,8,128]{2,1,0:T(8,128)} %param.14), kind=kLoop, calls=%fused_computation | loop fusion | flops 491520 | bytes 655360 | tf_op jit(solution)/shard_map/mul | solution.py:29
  2.0 2.1 %shard_map.149 = (f32[112,128]{1,0:T(8,128)S(1)}, f32[112,128]{1,0:T(8,128)S(1)}, f32[8,128]{1,0:T(8,128)S(1)}, f32[8,128]{1,0:T(8,128)S(1)}, bf16[256,512]{1,0:T(8,128)(2,1)S(1)}) custom-call(f32[256,128]{1,0:T(8,128)S(1)} %bitcast.19, f32[256,128]{1,0:T(8,128)S(1)} %multiply_multiply_fusion.cond, s32[72,128]{1,0:T(8,128)S(1)} %bitcast.31, ...), custom_call_target="tpu_custom_call" | custom-call | flops 2000000000 | bytes 6000000 | tf_op jit(solution)/shard_map/pallas_call | solution.py:438
  4.2 5.4 %collective-permute-start.1 = (f32[112,128]{1,0:T(8,128)S(1)}, f32[112,128]{1,0:T(8,128)S(1)}, u32[]{:S(2)}, u32[]{:S(2)}) collective-permute-start(f32[112,128]{1,0:T(8,128)S(1)} %get-tuple-element.29), channel_id=1, source_target_pairs={{4,8},{8,4},{12,16},{16,12},{20,24},{24,20},{28,32},{32,28},{36,40... | collective-permute-start | bytes 172040 | tf_op jit(solution)/shard_map/ppermute | solution.py:386
  12.8 2.0 %collective-permute-start.2 = (f32[56,128]{1,0:T(8,128)S(1)}, f32[56,128]{1,0:T(8,128)S(1)}, u32[]{:S(2)}, u32[]{:S(2)}) collective-permute-start(f32[56,128]{1,0:T(8,128)S(1)} %pad_maximum_fusion), channel_id=1, source_target_pairs={{0,1},{1,2},{2,3},{3,0},{4,5},{5,6},{6,7},{7,4},{8,9},{9,10},{10,1... | collective-permute-start | bytes 86024 | tf_op jit(solution)/shard_map/ppermute | solution.py:375
  14.8 2.2 %collective-permute-start.3 = (f32[56,128]{1,0:T(8,128)S(1)}, f32[56,128]{1,0:T(8,128)S(1)}, u32[]{:S(2)}, u32[]{:S(2)}) collective-permute-start(f32[56,128]{1,0:T(8,128)S(1)} %pad_maximum_fusion.1), channel_id=1, source_target_pairs={{1,0},{2,1},{3,2},{0,3},{5,4},{6,5},{7,6},{4,7},{9,8},{10,9},{11,1... | collective-permute-start | bytes 86024 | tf_op jit(solution)/shard_map/ppermute | solution.py:380
  17.2 1.6 %collective-permute-done.2.side_minus = f32[56,128]{1,0:T(8,128)S(1)} collective-permute-done((f32[56,128]{1,0:T(8,128)S(1)}, f32[56,128]{1,0:T(8,128)S(1)}, u32[]{:S(2)}, u32[]{:S(2)}) %collective-permute-start.2) | collective-permute-done | bytes 28704 | tf_op jit(solution)/shard_map/ppermute | solution.py:375
  18.8 4.5 %shard_map.152 = (f32[24,128]{1,0:T(8,128)S(1)}, f32[24,128]{1,0:T(8,128)S(1)}, f32[24,128]{1,0:T(8,128)S(1)}, f32[1,16]{1,0:T(1,128)}) custom-call(f32[112,128]{1,0:T(8,128)S(1)} %collective-permute-done._.chip, f32[48,128]{1,0:T(8,128)S(1)} %shard_map.150.here, f32[112,128]{1,0:T(8,128)S(1)} %collective-permute-done.1.cross, ...), custom_call_target="tpu_custom_call" | custom-call | flops 6000000000 | bytes 18000000 | tf_op jit(solution)/shard_map/pallas_call | solution.py:442
  23.3 1.9 %collective-permute-start.4 = (f32[24,128]{1,0:T(8,128)S(1)}, f32[24,128]{1,0:T(8,128)S(1)}, u32[]{:S(2)}, u32[]{:S(2)}) collective-permute-start(f32[24,128]{1,0:T(8,128)S(1)} %get-tuple-element.32), channel_id=1, source_target_pairs={{0,1},{1,2},{2,3},{3,0},{4,5},{5,6},{6,7},{7,4},{8,9},{9,10},{10,1... | collective-permute-start | bytes 36872 | tf_op jit(solution)/shard_map/ppermute | solution.py:375
  25.2 1.4 %collective-permute-start.5 = (f32[24,128]{1,0:T(8,128)S(1)}, f32[24,128]{1,0:T(8,128)S(1)}, u32[]{:S(2)}, u32[]{:S(2)}) collective-permute-start(f32[24,128]{1,0:T(8,128)S(1)} %get-tuple-element.34), channel_id=1, source_target_pairs={{1,0},{2,1},{3,2},{0,3},{5,4},{6,5},{7,6},{4,7},{9,8},{10,9},{11,1... | collective-permute-start | bytes 36872 | tf_op jit(solution)/shard_map/ppermute | solution.py:380
  26.7 1.7 %collective-permute-done.4.back_minus = f32[24,128]{1,0:T(8,128)S(1)} collective-permute-done((f32[24,128]{1,0:T(8,128)S(1)}, f32[24,128]{1,0:T(8,128)S(1)}, u32[]{:S(2)}, u32[]{:S(2)}) %collective-permute-start.4) | collective-permute-done | bytes 12320 | tf_op jit(solution)/shard_map/ppermute | solution.py:375
  28.9 1.3 %collective-permute-start.6 = (f32[24,128]{1,0:T(8,128)S(1)}, f32[24,128]{1,0:T(8,128)S(1)}, u32[]{:S(2)}, u32[]{:S(2)}) collective-permute-start(f32[24,128]{1,0:T(8,128)S(1)} %pad_maximum_fusion.4), channel_id=1, source_target_pairs={{4,8},{8,4},{12,16},{16,12},{20,24},{24,20},{28,32},{32,28},{36,40... | collective-permute-start | bytes 36872 | tf_op jit(solution)/shard_map/ppermute | solution.py:386
  30.3 1.3 %shard_map.153 = (f32[256,128]{1,0:T(8,128)S(1)}, f32[256,128]{1,0:T(8,128)S(1)}) custom-call(f32[256,128]{1,0:T(8,128)S(1)} %bitcast.20, f32[256,128]{1,0:T(8,128)S(1)} %multiply_multiply_fusion.cond, f32[256,128]{1,0:T(8,128)S(1)} %bitcast.21, f32[256,128]{1,0:T(8,128)S(1)} %bitcast.26, s32[256,128]{1,0:T(8,128)S(1)} %bitcast.23, f32[256,128]{1,0:T(8,128)S(1)} %bitcast.29, ...), custom_call_target="tpu_custom_call" | custom-call | flops 1000000000 | bytes 3000000 | tf_op jit(solution)/shard_map/pallas_call | solution.py:449
  31.6 4.0 %collective-permute-done.6.cross = f32[24,128]{1,0:T(8,128)S(1)} collective-permute-done((f32[24,128]{1,0:T(8,128)S(1)}, f32[24,128]{1,0:T(8,128)S(1)}, u32[]{:S(2)}, u32[]{:S(2)}) %collective-permute-start.6) | collective-permute-done | bytes 12320 | tf_op jit(solution)/shard_map/ppermute | solution.py:386
  36.5 2.1 %shard_map.155 = (f32[112,128]{1,0:T(8,128)S(1)}, f32[112,128]{1,0:T(8,128)S(1)}) custom-call(s32[72,128]{1,0:T(8,128)S(1)} %bitcast.35, s32[72,128]{1,0:T(8,128)S(1)} %bitcast.43, bf16[256,512]{1,0:T(8,128)(2,1)S(1)} %get-tuple-element.37.weight, f32[64,128]{1,0:T(8,128)S(1)} %get-tuple-element.38.chip_edge, f32[64,128]{1,0:T(8,128)S(1)} %get-tuple-element.39.cross_edge), custom_call_target="tpu_custom_call" | custom-call | flops 2000000000 | bytes 6000000 | tf_op jit(solution)/shard_map/pallas_call | solution.py:461
  41.1 4.6 %collective-permute-done.9.cross = f32[112,128]{1,0:T(8,128)S(1)} collective-permute-done((f32[112,128]{1,0:T(8,128)S(1)}, f32[112,128]{1,0:T(8,128)S(1)}, u32[]{:S(2)}, u32[]{:S(2)}) %collective-permute-start.9) | collective-permute-done | bytes 57376 | tf_op jit(solution)/shard_map/ppermute | solution.py:386
  45.7 1.6 %collective-permute-start.10 = (f32[56,128]{1,0:T(8,128)S(1)}, f32[56,128]{1,0:T(8,128)S(1)}, u32[]{:S(2)}, u32[]{:S(2)}) collective-permute-start(f32[56,128]{1,0:T(8,128)S(1)} %pad_maximum_fusion.2), channel_id=1, source_target_pairs={{0,1},{1,2},{2,3},{3,0},{4,5},{5,6},{6,7},{7,4},{8,9},{9,10},{10,1... | collective-permute-start | bytes 86024 | tf_op jit(solution)/shard_map/ppermute | solution.py:375
  47.3 1.6 %collective-permute-start.11 = (f32[56,128]{1,0:T(8,128)S(1)}, f32[56,128]{1,0:T(8,128)S(1)}, u32[]{:S(2)}, u32[]{:S(2)}) collective-permute-start(f32[56,128]{1,0:T(8,128)S(1)} %pad_maximum_fusion.3), channel_id=1, source_target_pairs={{1,0},{2,1},{3,2},{0,3},{5,4},{6,5},{7,6},{4,7},{9,8},{10,9},{11,1... | collective-permute-start | bytes 86024 | tf_op jit(solution)/shard_map/ppermute | solution.py:380
  48.9 1.8 %collective-permute-done.10.side_minus = f32[56,128]{1,0:T(8,128)S(1)} collective-permute-done((f32[56,128]{1,0:T(8,128)S(1)}, f32[56,128]{1,0:T(8,128)S(1)}, u32[]{:S(2)}, u32[]{:S(2)}) %collective-permute-start.10) | collective-permute-done | bytes 28704 | tf_op jit(solution)/shard_map/ppermute | solution.py:375
  51.2 4.5 %shard_map.157 = (f32[24,128]{1,0:T(8,128)S(1)}, f32[24,128]{1,0:T(8,128)S(1)}, f32[24,128]{1,0:T(8,128)S(1)}, f32[1,16]{1,0:T(1,128)}) custom-call(f32[112,128]{1,0:T(8,128)S(1)} %collective-permute-done.8._.chip, f32[48,128]{1,0:T(8,128)S(1)} %shard_map.156.here, f32[112,128]{1,0:T(8,128)S(1)} %collective-permute-done.9.cross, ...), custom_call_target="tpu_custom_call" | custom-call | flops 6000000000 | bytes 18000000 | tf_op jit(solution)/shard_map/pallas_call | solution.py:442
  57.0 2.0 %collective-permute-start.13 = (f32[24,128]{1,0:T(8,128)S(1)}, f32[24,128]{1,0:T(8,128)S(1)}, u32[]{:S(2)}, u32[]{:S(2)}) collective-permute-start(f32[24,128]{1,0:T(8,128)S(1)} %get-tuple-element.46), channel_id=1, source_target_pairs={{1,0},{2,1},{3,2},{0,3},{5,4},{6,5},{7,6},{4,7},{9,8},{10,9},{11,1... | collective-permute-start | bytes 36872 | tf_op jit(solution)/shard_map/ppermute | solution.py:380
  59.0 1.7 %collective-permute-done.12.back_minus = f32[24,128]{1,0:T(8,128)S(1)} collective-permute-done((f32[24,128]{1,0:T(8,128)S(1)}, f32[24,128]{1,0:T(8,128)S(1)}, u32[]{:S(2)}, u32[]{:S(2)}) %collective-permute-start.12) | collective-permute-done | bytes 12320 | tf_op jit(solution)/shard_map/ppermute | solution.py:375
  61.9 1.3 %shard_map.158 = (f32[256,128]{1,0:T(8,128)S(1)}, f32[256,128]{1,0:T(8,128)S(1)}) custom-call(f32[256,128]{1,0:T(8,128)S(1)} %get-tuple-element.47.head, f32[256,128]{1,0:T(8,128)S(1)} %get-tuple-element.48.cond, f32[256,128]{1,0:T(8,128)S(1)} %bitcast.22, f32[256,128]{1,0:T(8,128)S(1)} %bitcast.28, s32[256,128]{1,0:T(8,128)S(1)} %bitcast.25, ...), custom_call_target="tpu_custom_call" | custom-call | flops 1000000000 | bytes 3000000 | tf_op jit(solution)/shard_map/pallas_call | solution.py:449
  63.2 4.0 %collective-permute-done.14.cross = f32[24,128]{1,0:T(8,128)S(1)} collective-permute-done((f32[24,128]{1,0:T(8,128)S(1)}, f32[24,128]{1,0:T(8,128)S(1)}, u32[]{:S(2)}, u32[]{:S(2)}) %collective-permute-start.14) | collective-permute-done | bytes 12320 | tf_op jit(solution)/shard_map/ppermute | solution.py:386
  67.3 1.3 %shard_map.159 = f32[256,128]{1,0:T(8,128)} custom-call(f32[24,128]{1,0:T(8,128)S(1)} %collective-permute-done.14.cross, s32[72,128]{1,0:T(8,128)S(1)} %bitcast.38, s32[72,128]{1,0:T(8,128)S(1)} %bitcast.46, f32[256,128]{1,0:T(8,128)S(1)} %get-tuple-element.49.numerator, f32[256,128]{1,0:T(8,128)S(1)} %get-tuple-element.50.denominator), custom_call_target="tpu_custom_call" | custom-call | flops 1000000000 | bytes 3000000 | tf_op jit(solution)/shard_map/pallas_call | solution.py:464
  (71 shorter events, 10.3 us)
Async XLA Ops:
  2.0 8.9 %copy-start.9 = (s32[128,128]{1,0:T(8,128)S(1)}, s32[128,128]{1,0:T(8,128)}, u32[]{:S(2)}) copy-start(s32[128,128]{1,0:T(8,128)} %param.26) | copy-start | bytes 196612
  2.0 8.9 %copy-start.10 = (s32[128,128]{1,0:T(8,128)S(1)}, s32[128,128]{1,0:T(8,128)}, u32[]{:S(2)}) copy-start(s32[128,128]{1,0:T(8,128)} %param.25) | copy-start | bytes 196612
  4.1 7.6 %collective-permute-start = (f32[112,128]{1,0:T(8,128)S(1)}, f32[112,128]{1,0:T(8,128)S(1)}, u32[]{:S(2)}, u32[]{:S(2)}) collective-permute-start(f32[112,128]{1,0:T(8,128)S(1)} %get-tuple-element.27), channel_id=1, source_target_pairs={{0,4},{4,0},{8,12},{12,8},{16,20},{20,16},{24,28},{28,24},{32,36},... | collective-permute-start | bytes 172040 | tf_op jit(solution)/shard_map/ppermute | solution.py:386
  4.2 8.6 %collective-permute-start.1 = (f32[112,128]{1,0:T(8,128)S(1)}, f32[112,128]{1,0:T(8,128)S(1)}, u32[]{:S(2)}, u32[]{:S(2)}) collective-permute-start(f32[112,128]{1,0:T(8,128)S(1)} %get-tuple-element.29), channel_id=1, source_target_pairs={{4,8},{8,4},{12,16},{16,12},{20,24},{24,20},{28,32},{32,28},{36,40... | collective-permute-start | bytes 172040 | tf_op jit(solution)/shard_map/ppermute | solution.py:386
  12.8 6.0 %collective-permute-start.2 = (f32[56,128]{1,0:T(8,128)S(1)}, f32[56,128]{1,0:T(8,128)S(1)}, u32[]{:S(2)}, u32[]{:S(2)}) collective-permute-start(f32[56,128]{1,0:T(8,128)S(1)} %pad_maximum_fusion), channel_id=1, source_target_pairs={{0,1},{1,2},{2,3},{3,0},{4,5},{5,6},{6,7},{7,4},{8,9},{9,10},{10,1... | collective-permute-start | bytes 86024 | tf_op jit(solution)/shard_map/ppermute | solution.py:375
  14.8 4.0 %copy-start.5 = (f32[128,128]{1,0:T(8,128)S(1)}, f32[128,128]{1,0:T(8,128)}, u32[]{:S(2)}) copy-start(f32[128,128]{1,0:T(8,128)} %radial_in.3) | copy-start | bytes 196612
  14.8 4.0 %copy-start.6 = (f32[128,128]{1,0:T(8,128)S(1)}, f32[128,128]{1,0:T(8,128)}, u32[]{:S(2)}) copy-start(f32[128,128]{1,0:T(8,128)} %axial.3) | copy-start | bytes 196612
  14.8 4.0 %collective-permute-start.3 = (f32[56,128]{1,0:T(8,128)S(1)}, f32[56,128]{1,0:T(8,128)S(1)}, u32[]{:S(2)}, u32[]{:S(2)}) collective-permute-start(f32[56,128]{1,0:T(8,128)S(1)} %pad_maximum_fusion.1), channel_id=1, source_target_pairs={{1,0},{2,1},{3,2},{0,3},{5,4},{6,5},{7,6},{4,7},{9,8},{10,9},{11,1... | collective-permute-start | bytes 86024 | tf_op jit(solution)/shard_map/ppermute | solution.py:380
  17.2 13.1 %copy-start.2 = (s32[32,8,128]{2,1,0:T(8,128)S(1)}, s32[32,8,128]{2,1,0:T(8,128)}, u32[]{:S(2)}) copy-start(s32[32,8,128]{2,1,0:T(8,128)} %param.17) | copy-start | bytes 393220
  17.2 13.1 %copy-start.3 = (f32[32,8,128]{2,1,0:T(8,128)S(1)}, f32[32,8,128]{2,1,0:T(8,128)}, u32[]{:S(2)}) copy-start(f32[32,8,128]{2,1,0:T(8,128)} %param.16) | copy-start | bytes 393220
  17.2 13.1 %copy-start.4 = (f32[32,8,128]{2,1,0:T(8,128)S(1)}, f32[32,8,128]{2,1,0:T(8,128)}, u32[]{:S(2)}) copy-start(f32[32,8,128]{2,1,0:T(8,128)} %param.18) | copy-start | bytes 393220
  23.3 5.0 %collective-permute-start.4 = (f32[24,128]{1,0:T(8,128)S(1)}, f32[24,128]{1,0:T(8,128)S(1)}, u32[]{:S(2)}, u32[]{:S(2)}) collective-permute-start(f32[24,128]{1,0:T(8,128)S(1)} %get-tuple-element.32), channel_id=1, source_target_pairs={{0,1},{1,2},{2,3},{3,0},{4,5},{5,6},{6,7},{7,4},{8,9},{9,10},{10,1... | collective-permute-start | bytes 36872 | tf_op jit(solution)/shard_map/ppermute | solution.py:375
  25.2 3.7 %collective-permute-start.5 = (f32[24,128]{1,0:T(8,128)S(1)}, f32[24,128]{1,0:T(8,128)S(1)}, u32[]{:S(2)}, u32[]{:S(2)}) collective-permute-start(f32[24,128]{1,0:T(8,128)S(1)} %get-tuple-element.34), channel_id=1, source_target_pairs={{1,0},{2,1},{3,2},{0,3},{5,4},{6,5},{7,6},{4,7},{9,8},{10,9},{11,1... | collective-permute-start | bytes 36872 | tf_op jit(solution)/shard_map/ppermute | solution.py:380
  28.9 1.4 %collective-permute-start.7 = (f32[24,128]{1,0:T(8,128)S(1)}, f32[24,128]{1,0:T(8,128)S(1)}, u32[]{:S(2)}, u32[]{:S(2)}) collective-permute-start(f32[24,128]{1,0:T(8,128)S(1)} %pad_maximum_fusion.5), channel_id=1, source_target_pairs={{0,4},{4,0},{8,12},{12,8},{16,20},{20,16},{24,28},{28,24},{32,36},... | collective-permute-start | bytes 36872 | tf_op jit(solution)/shard_map/ppermute | solution.py:386
  28.9 6.7 %collective-permute-start.6 = (f32[24,128]{1,0:T(8,128)S(1)}, f32[24,128]{1,0:T(8,128)S(1)}, u32[]{:S(2)}, u32[]{:S(2)}) collective-permute-start(f32[24,128]{1,0:T(8,128)S(1)} %pad_maximum_fusion.4), channel_id=1, source_target_pairs={{4,8},{8,4},{12,16},{16,12},{20,24},{24,20},{28,32},{32,28},{36,40... | collective-permute-start | bytes 36872 | tf_op jit(solution)/shard_map/ppermute | solution.py:386
  30.3 5.3 %copy-start = (f32[32,8,128]{2,1,0:T(8,128)S(1)}, f32[32,8,128]{2,1,0:T(8,128)}, u32[]{:S(2)}) copy-start(f32[32,8,128]{2,1,0:T(8,128)} %param.15) | copy-start | bytes 393220
  38.6 1.3 %collective-permute-start.8 = (f32[112,128]{1,0:T(8,128)S(1)}, f32[112,128]{1,0:T(8,128)S(1)}, u32[]{:S(2)}, u32[]{:S(2)}) collective-permute-start(f32[112,128]{1,0:T(8,128)S(1)} %get-tuple-element.40), channel_id=1, source_target_pairs={{0,4},{4,0},{8,12},{12,8},{16,20},{20,16},{24,28},{28,24},{32,36},... | collective-permute-start | bytes 172040 | tf_op jit(solution)/shard_map/ppermute | solution.py:386
  38.7 7.0 %collective-permute-start.9 = (f32[112,128]{1,0:T(8,128)S(1)}, f32[112,128]{1,0:T(8,128)S(1)}, u32[]{:S(2)}, u32[]{:S(2)}) collective-permute-start(f32[112,128]{1,0:T(8,128)S(1)} %get-tuple-element.41), channel_id=1, source_target_pairs={{4,8},{8,4},{12,16},{16,12},{20,24},{24,20},{28,32},{32,28},{36,40... | collective-permute-start | bytes 172040 | tf_op jit(solution)/shard_map/ppermute | solution.py:386
  45.7 5.1 %collective-permute-start.10 = (f32[56,128]{1,0:T(8,128)S(1)}, f32[56,128]{1,0:T(8,128)S(1)}, u32[]{:S(2)}, u32[]{:S(2)}) collective-permute-start(f32[56,128]{1,0:T(8,128)S(1)} %pad_maximum_fusion.2), channel_id=1, source_target_pairs={{0,1},{1,2},{2,3},{3,0},{4,5},{5,6},{6,7},{7,4},{8,9},{9,10},{10,1... | collective-permute-start | bytes 86024 | tf_op jit(solution)/shard_map/ppermute | solution.py:375
  47.3 3.9 %collective-permute-start.11 = (f32[56,128]{1,0:T(8,128)S(1)}, f32[56,128]{1,0:T(8,128)S(1)}, u32[]{:S(2)}, u32[]{:S(2)}) collective-permute-start(f32[56,128]{1,0:T(8,128)S(1)} %pad_maximum_fusion.3), channel_id=1, source_target_pairs={{1,0},{2,1},{3,2},{0,3},{5,4},{6,5},{7,6},{4,7},{9,8},{10,9},{11,1... | collective-permute-start | bytes 86024 | tf_op jit(solution)/shard_map/ppermute | solution.py:380
  55.7 4.9 %collective-permute-start.12 = (f32[24,128]{1,0:T(8,128)S(1)}, f32[24,128]{1,0:T(8,128)S(1)}, u32[]{:S(2)}, u32[]{:S(2)}) collective-permute-start(f32[24,128]{1,0:T(8,128)S(1)} %get-tuple-element.44), channel_id=1, source_target_pairs={{0,1},{1,2},{2,3},{3,0},{4,5},{5,6},{6,7},{7,4},{8,9},{9,10},{10,1... | collective-permute-start | bytes 36872 | tf_op jit(solution)/shard_map/ppermute | solution.py:375
  57.0 3.7 %collective-permute-start.13 = (f32[24,128]{1,0:T(8,128)S(1)}, f32[24,128]{1,0:T(8,128)S(1)}, u32[]{:S(2)}, u32[]{:S(2)}) collective-permute-start(f32[24,128]{1,0:T(8,128)S(1)} %get-tuple-element.46), channel_id=1, source_target_pairs={{1,0},{2,1},{3,2},{0,3},{5,4},{6,5},{7,6},{4,7},{9,8},{10,9},{11,1... | collective-permute-start | bytes 36872 | tf_op jit(solution)/shard_map/ppermute | solution.py:380
  60.7 1.2 %collective-permute-start.15 = (f32[24,128]{1,0:T(8,128)S(1)}, f32[24,128]{1,0:T(8,128)S(1)}, u32[]{:S(2)}, u32[]{:S(2)}) collective-permute-start(f32[24,128]{1,0:T(8,128)S(1)} %pad_maximum_fusion.7), channel_id=1, source_target_pairs={{0,4},{4,0},{8,12},{12,8},{16,20},{20,16},{24,28},{28,24},{32,36},... | collective-permute-start | bytes 36872 | tf_op jit(solution)/shard_map/ppermute | solution.py:386
  60.8 6.5 %collective-permute-start.14 = (f32[24,128]{1,0:T(8,128)S(1)}, f32[24,128]{1,0:T(8,128)S(1)}, u32[]{:S(2)}, u32[]{:S(2)}) collective-permute-start(f32[24,128]{1,0:T(8,128)S(1)} %pad_maximum_fusion.6), channel_id=1, source_target_pairs={{4,8},{8,4},{12,16},{16,12},{20,24},{24,20},{28,32},{32,28},{36,40... | collective-permute-start | bytes 36872 | tf_op jit(solution)/shard_map/ppermute | solution.py:386
  (6 other events, 5.9 us)

commit v5 on v4

--- a/solution.py
+++ b/solution.py
@@ -49,7 +49,7 @@
     return (2 - 2 * odd, 2 * odd)
 
 
-def lay_cells(head, cond, weight, chip, cross, edge_minus, edge_plus):
+def lay_cells(head, cond, weight, chip_edge, cross, edge_minus, edge_plus):
     even = x_places()[0] == 2
     for field, ref in enumerate((head, cond)):
         for half in range(2):
@@ -61,8 +61,8 @@
             weight[field * 128 : field * 128 + 128, 256 + half * 128 : 384 + half * 128] = lo
         first = ref[pl.ds(0, LAYERS, stride=8), :]
         last = ref[pl.ds(7, LAYERS, stride=8), :]
-        at = chip.shape[0] - 64 + 32 * field
-        chip[at : at + 32, :] = jnp.where(even, last, first)
+        chip_edge[32 * field : 32 * field + 32, :] = jnp.where(even, last, first)
+        at = cross.shape[0] - 64 + 32 * field
         cross[at : at + 32, :] = jnp.where(even, first, last)
     edge_minus[4:8, :] = jnp.zeros((4, LANES), F32)
     edge_plus[4:8, :] = jnp.zeros((4, LANES), F32)
@@ -100,37 +100,33 @@
                         out[at : at + 1, :] = jnp.sum(jnp.where(mask, part, 0.0), 0, keepdims=True)
 
 
-def gather_far(row, col, weight, chip, cross):
-    chip_place, cross_place = x_places()
-    gather_cells(row, col, weight, ((cross, cross_place), (chip, chip_place)))
-
-
-def start_kernel(head, cond, row, col, chip, cross, edge_minus, edge_plus, weight):
-    lay_cells(head, cond, weight, chip, cross, edge_minus, edge_plus)
-    gather_far(row, col, weight, chip, cross)
-
-
-def far_kernel(row, col, weight, chip_edge, cross_edge, chip, cross):
-    gather_far(row, col, weight, chip, cross)
-    chip[48:112, :] = chip_edge[...]
+def start_kernel(head, cond, row, col, chip_edge, cross, edge_minus, edge_plus, weight):
+    lay_cells(head, cond, weight, chip_edge, cross, edge_minus, edge_plus)
+    gather_cells(row, col, weight, ((cross, x_places()[1]),))
+
+
+def cross_kernel(row, col, weight, cross_edge, cross):
+    gather_cells(row, col, weight, ((cross, x_places()[1]),))
     cross[48:112, :] = cross_edge[...]
 
 
-def here_kernel(row, col, weight, _, here):
-    gather_cells(row, col, weight, ((here, 1),))
-
-
-def collar_kernel(lines, second):
+def rest_kernel(row, col, weight, _, chip, here):
+    gather_cells(row, col, weight, ((chip, x_places()[0]), (here, 1)))
+
+
+def collar_kernel(stem, entry, demand, second, need):
     sub = lax.broadcasted_iota(I32, (BLOCKS, LANES), 0)
     lane = lax.broadcasted_iota(I32, (BLOCKS, LANES), 1)
     own = sub == lane
-    stem = jnp.sum(jnp.where(own, lines[0:1, :], 0.0), 1, keepdims=True)
-    entry = jnp.sum(jnp.where(own, lines[1:2, :], 0.0), 1, keepdims=True)
-    second[...] = jnp.where(lane.astype(F32) == entry, stem, 0.0)
+    stem_col = jnp.sum(jnp.where(own, stem[...], 0.0), 1, keepdims=True)
+    entry_col = jnp.sum(jnp.where(own, entry[...].astype(F32), 0.0), 1, keepdims=True)
+    second[...] = jnp.where(lane.astype(F32) == entry_col, stem_col, 0.0)
+    need[...] = jnp.zeros((1, LANES), F32)
+    need[:, 0:PLANTS] = demand[...]
 
 
 def terms_kernel(
-    head, cond, head_old, alpha_dry, wet, reversal, chip, cross, side_minus, side_plus,
+    head, cond, head_old, alpha_dry, wet, reversal, chip_edges, cross, side_minus, side_plus,
     back_minus, back_here, back_plus, back_chip, row, col,
     numerator, denominator, halo,
 ):
@@ -138,8 +134,8 @@
     pieces += [(back_chip, dy * 8, x_places()[0] * 3 + dy) for dy in range(3)]
     sink = SINK_GAIN * sink_of(pieces, row, col)
     even = x_places()[0] == 2
-    from_plus = jnp.where(even, chip[48:112, :], cross[48:112, :])
-    from_minus = jnp.where(even, cross[48:112, :], chip[48:112, :])
+    from_plus = jnp.where(even, chip_edges[...], cross[48:112, :])
+    from_minus = jnp.where(even, cross[48:112, :], chip_edges[...])
     halo[...] = jnp.zeros_like(halo)
     turned = []
     for i in range(4):
@@ -197,7 +193,7 @@
 
 
 def root_kernel(
-    chip, here, cross, side_minus, side_plus, code, radial_in, axial, lines, collar_link,
+    chip, here, cross, side_minus, side_plus, code, radial_in, axial, collar_link, demand,
     out_minus, out_here, out_plus, collar_out, weight, table, seg_head, seg_cond, uptake, summed,
 ):
     cross_place, chip_place = x_places()
@@ -266,7 +262,7 @@
             return jnp.sum(jnp.sum(x.reshape(group // 8, 8, LANES), 1), 1, keepdims=True)
 
         mine = lax.broadcasted_iota(I32, (group // 8, LANES), 1) == plant_row + g * (group // 8)
-        need = jnp.sum(jnp.where(mine, lines[2:3, :], 0.0), 1, keepdims=True)
+        need = jnp.sum(jnp.where(mine, demand[...], 0.0), 1, keepdims=True)
         head = (per_plant(radial * (hs - free)) - need) / per_plant(radial * collar)
         spread = jnp.broadcast_to(head[:, None, :], (group // 8, 8, LANES)).reshape(group, LANES)
         uptake[at, :] = radial * (hs - (free + spread * collar))
@@ -367,6 +363,7 @@
 
 MESSAGE = ((112, 128), F32)
 EDGE = ((64, 128), F32)
+SLOT = ((48, 128), F32)
 SIDES = [((8, 128), F32)] * 2 + [((256, 512), BF16)]
 
 
@@ -386,14 +383,15 @@
     return lax.ppermute(x, axis, [p for i, j in pairs for p in ((i, j), (j, i))])
 
 
-def spread(row, col, chip, cross, edge_minus, edge_plus, weight):
+def spread(row, col, chip_edge, cross, edge_minus, edge_plus, weight):
     from_cross = swap(cross, "gx", 1)
+    chip_edges = swap(chip_edge, "gx", 0)
+    chip, here = call(rest_kernel, [SLOT] * 2, micros=2)(row, col, weight, chip_edges)
     from_chip = swap(chip, "gx", 0)
-    (here,) = call(here_kernel, [((48, 128), F32)])(row, col, weight, from_chip)
     parts = (from_chip, here, from_cross)
     side_minus = up(jnp.concatenate([x[32:48] for x in parts] + [edge_plus], 0), "gy")
     side_plus = down(jnp.concatenate([x[0:16] for x in parts] + [edge_minus], 0), "gy")
-    return (*parts, side_minus, side_plus)
+    return (*parts, side_minus, side_plus), chip_edges
 
 
 def give_back(minus, here, plus):
@@ -429,37 +427,36 @@
         lax.axis_index("gy") - source_dev % cols_gy + 1
     ) % cols_gy
     code = offset_k * send_row.shape[2] + source_slot
-    lines = jnp.stack(
-        (stem_link, entry_seg.astype(F32), jnp.pad(demand, (0, BLOCKS - demand.shape[0])))
-    )
     row, col = (x.reshape(SLOTS, LANES) for x in (send_row, send_col))
     head_old = head
     cond = conduct(head, sat, alpha * (1.0 + wet.astype(F32)))
-    messages = call(start_kernel, [MESSAGE] * 2 + SIDES, micros=2)(head, cond, row, col)
-    (collar_link,) = call(collar_kernel, [((BLOCKS, LANES), F32)])(lines)
+    messages = call(start_kernel, [EDGE, MESSAGE] + SIDES, micros=2)(head, cond, row, col)
+    collar_link, need = call(collar_kernel, [((BLOCKS, LANES), F32), ((1, LANES), F32)])(
+        stem_link.reshape(1, BLOCKS), entry_seg.reshape(1, BLOCKS), demand.reshape(1, PLANTS)
+    )
     for iteration in range(PICARD):
-        got = spread(row, col, *messages)
+        got, chip_edges = spread(row, col, *messages)
         *sums, collar = call(
             root_kernel,
             [((24, 128), F32)] * 3 + [((1, PLANTS), F32)],
             [((144, 256), BF16), ((144, 128), F32)] + [((128, 128), F32)] * 3 + [((72, 128), F32)],
             micros=6,
-        )(*got, code, root_radial, root_axial, lines, collar_link)
+        )(*got, code, root_radial, root_axial, collar_link, need)
         near, (from_chip, from_cross) = give_back(*sums)
         numerator, denominator = call(
             terms_kernel,
             [((CELLS, LANES), F32)] * 2,
             [((128, 128), F32)],
         )(
-            head, cond, head_old, alpha, wet, reversal, got[0], got[2], got[3], got[4],
+            head, cond, head_old, alpha, wet, reversal, chip_edges, got[2], got[3], got[4],
             *near, from_chip, row, col,
         )
         if iteration < PICARD - 1:
-            head, cond, *edges, side_minus, side_plus, weight = call(
+            head, cond, chip_edge, cross_edge, *sides, weight = call(
                 next_kernel, [((CELLS, LANES), F32)] * 2 + [EDGE] * 2 + SIDES, micros=2
             )(from_cross, row, col, numerator, denominator, sat, alpha, wet)
-            far = call(far_kernel, [MESSAGE] * 2, micros=2)(row, col, weight, *edges)
-            messages = (*far, side_minus, side_plus, weight)
+            (cross,) = call(cross_kernel, [MESSAGE])(row, col, weight, cross_edge)
+            messages = (chip_edge, cross, *sides, weight)
         else:
             (head,) = call(last_kernel, [((CELLS, LANES), F32)])(
                 from_cross, row, col, numerator, denominator

time: 68.7 us -> 67 us (0.975)
  waiting for transfers between devices: 21.6 us -> 19.2 us
  starting transfers between devices: 22.2 us -> 24.2 us
  local copies, waits for them, and re-layouts: 2.05 us -> 0.77 us
    ppermute x8 -> x10, starting transfers between devices: 8.2 us -> 10.2 us  [swap(): lax.ppermute(x, axis, [p for i, j in pairs for p in ((i, j), (j, i))])]
    ppermute x8 -> x10, waiting for transfers between devices: 13.8 us -> 12.1 us  [swap(): lax.ppermute(x, axis, [p for i, j in pairs for p in ((i, j), (j, i))])]
    unnamed x28, local copies, waits for them, and re-layouts: 2.01 us -> 0.74 us
  transfers between devices with their start and end apart: 16 -> 18, of which waited for: 11 -> 12; matrix products, arithmetic and copies ran while one was open for 0% -> 0% of each run, Pallas kernels for 7% -> 12%
where the time goes in v5:
time: 67 us; the launch traced here: 66.8 us
  starting transfers between devices  24.2 us (36%)
  Pallas kernels  20.3 us (30%)
  waiting for transfers between devices  19.2 us (29%)
  other arithmetic  1.45 us (2%)
  between operations  0.93 us (1%)
  local copies, waits for them, and re-layouts  0.77 us (1%)
    ppermute x10, waiting for transfers between devices, swap(): lax.ppermute(x, axis, [p for i, j in pairs for p in ((i, j), (j, i))])  12.1 us
    ppermute x10, starting transfers between devices, swap(): lax.ppermute(x, axis, [p for i, j in pairs for p in ((i, j), (j, i))])  10.2 us
    pallas_call x2, Pallas kernels, on_device(): call(root_kernel, [((24, 128), F32)] * 3 + [((1, PLANTS), F32)], [((144,...  9.05 us
    ppermute x4, starting transfers between devices, down(): return lax.ppermute(x, axis, [((i + 1) % size, i) for i in range(size)])  7.27 us
    ppermute x4, starting transfers between devices, up(): return lax.ppermute(x, axis, [(i, (i + 1) % size) for i in range(size)])  6.71 us
    ppermute x4, waiting for transfers between devices, up(): return lax.ppermute(x, axis, [(i, (i + 1) % size) for i in range(size)])  6.12 us
    pallas_call x2, Pallas kernels, spread(): call(rest_kernel, [SLOT] * 2, micros=2)(row, col, weight, chip_edges)  4.13 us
    pallas_call x2, Pallas kernels, on_device(): call(terms_kernel, [((CELLS, LANES), F32)] * 2, [((128, 128), F32)])  2.64 us
  transfers between devices with their start and end apart: 18, of which 12 were waited for; matrix products, arithmetic and copies ran while one was open for 0% of the time, Pallas kernels for 12%

profile of v5, /device:TPU:0, one launch (start us, length us, event | category | flops | bytes accessed | tf_op | source)
XLA Modules:
  0.0 66.8 jit_solution(10706541676189297143)
XLA Ops:
  0.7 1.3 %multiply_multiply_fusion.cond = f32[256,128]{1,0:T(8,128)S(1)} fusion(s32[32,8,128]{2,1,0:T(8,128)} %param.17, f32[32,8,128]{2,1,0:T(8,128)} %param.16, f32[32,8,128]{2,1,0:T(8,128)} %param.15, f32[32,8,128]{2,1,0:T(8,128)} %param.14), kind=kLoop, calls=%fused_computation | loop fusion | flops 491520 | bytes 655360 | tf_op jit(solution)/shard_map/mul | solution.py:29
  3.2 5.4 %collective-permute-start.2 = (f32[112,128]{1,0:T(8,128)S(1)}, f32[112,128]{1,0:T(8,128)S(1)}, u32[]{:S(2)}, u32[]{:S(2)}) collective-permute-start(f32[112,128]{1,0:T(8,128)S(1)} %get-tuple-element.35), channel_id=1, source_target_pairs={{4,8},{8,4},{12,16},{16,12},{20,24},{24,20},{28,32},{32,28},{36,40... | collective-permute-start | bytes 172040 | tf_op jit(solution)/shard_map/ppermute | solution.py:383
  8.8 2.0 %shard_map.150 = (f32[48,128]{1,0:T(8,128)S(1)}, f32[48,128]{1,0:T(8,128)S(1)}) custom-call(s32[72,128]{1,0:T(8,128)S(1)} %bitcast.30, s32[72,128]{1,0:T(8,128)S(1)} %bitcast.38, bf16[256,512]{1,0:T(8,128)(2,1)S(1)} %get-tuple-element.31.weight, f32[64,128]{1,0:T(8,128)S(1)} %collective-permute-done._.chip_edges), custom_call_target="tpu_custom_call" | custom-call | flops 2000000000 | bytes 6000000 | tf_op jit(solution)/shard_map/pallas_call | solution.py:389
  12.1 2.0 %collective-permute-start.3 = (f32[56,128]{1,0:T(8,128)S(1)}, f32[56,128]{1,0:T(8,128)S(1)}, u32[]{:S(2)}, u32[]{:S(2)}) collective-permute-start(f32[56,128]{1,0:T(8,128)S(1)} %pad_maximum_fusion), channel_id=1, source_target_pairs={{0,1},{1,2},{2,3},{3,0},{4,5},{5,6},{6,7},{7,4},{8,9},{9,10},{10,1... | collective-permute-start | bytes 86024 | tf_op jit(solution)/shard_map/ppermute | solution.py:372
  14.1 2.2 %collective-permute-start.4 = (f32[56,128]{1,0:T(8,128)S(1)}, f32[56,128]{1,0:T(8,128)S(1)}, u32[]{:S(2)}, u32[]{:S(2)}) collective-permute-start(f32[56,128]{1,0:T(8,128)S(1)} %pad_maximum_fusion.1), channel_id=1, source_target_pairs={{1,0},{2,1},{3,2},{0,3},{5,4},{6,5},{7,6},{4,7},{9,8},{10,9},{11,1... | collective-permute-start | bytes 86024 | tf_op jit(solution)/shard_map/ppermute | solution.py:377
  18.1 4.5 %shard_map.152 = (f32[24,128]{1,0:T(8,128)S(1)}, f32[24,128]{1,0:T(8,128)S(1)}, f32[24,128]{1,0:T(8,128)S(1)}, f32[1,16]{1,0:T(1,128)}) custom-call(f32[48,128]{1,0:T(8,128)S(1)} %collective-permute-done.1.chip, f32[48,128]{1,0:T(8,128)S(1)} %get-tuple-element.34.here, f32[112,128]{1,0:T(8,128)S(1)} %collective-permute-done.2.cross, ...), custom_call_target="tpu_custom_call" | custom-call | flops 6000000000 | bytes 18000000 | tf_op jit(solution)/shard_map/pallas_call | solution.py:439
  22.7 1.8 %collective-permute-start.5 = (f32[24,128]{1,0:T(8,128)S(1)}, f32[24,128]{1,0:T(8,128)S(1)}, u32[]{:S(2)}, u32[]{:S(2)}) collective-permute-start(f32[24,128]{1,0:T(8,128)S(1)} %get-tuple-element.40), channel_id=1, source_target_pairs={{0,1},{1,2},{2,3},{3,0},{4,5},{5,6},{6,7},{7,4},{8,9},{9,10},{10,1... | collective-permute-start | bytes 36872 | tf_op jit(solution)/shard_map/ppermute | solution.py:372
  24.5 1.5 %collective-permute-start.6 = (f32[24,128]{1,0:T(8,128)S(1)}, f32[24,128]{1,0:T(8,128)S(1)}, u32[]{:S(2)}, u32[]{:S(2)}) collective-permute-start(f32[24,128]{1,0:T(8,128)S(1)} %get-tuple-element.42), channel_id=1, source_target_pairs={{1,0},{2,1},{3,2},{0,3},{5,4},{6,5},{7,6},{4,7},{9,8},{10,9},{11,1... | collective-permute-start | bytes 36872 | tf_op jit(solution)/shard_map/ppermute | solution.py:377
  26.0 1.7 %collective-permute-done.5.back_minus = f32[24,128]{1,0:T(8,128)S(1)} collective-permute-done((f32[24,128]{1,0:T(8,128)S(1)}, f32[24,128]{1,0:T(8,128)S(1)}, u32[]{:S(2)}, u32[]{:S(2)}) %collective-permute-start.5) | collective-permute-done | bytes 12320 | tf_op jit(solution)/shard_map/ppermute | solution.py:372
  29.5 1.3 %shard_map.153 = (f32[256,128]{1,0:T(8,128)S(1)}, f32[256,128]{1,0:T(8,128)S(1)}) custom-call(f32[256,128]{1,0:T(8,128)S(1)} %bitcast.18, f32[256,128]{1,0:T(8,128)S(1)} %multiply_multiply_fusion.cond, f32[256,128]{1,0:T(8,128)S(1)} %bitcast.19, f32[256,128]{1,0:T(8,128)S(1)} %bitcast.24, s32[256,128]{1,0:T(8,128)S(1)} %bitcast.21, f32[256,128]{1,0:T(8,128)S(1)} %bitcast.27, ...), custom_call_target="tpu_custom_call" | custom-call | flops 1000000000 | bytes 3000000 | tf_op jit(solution)/shard_map/pallas_call | solution.py:446
  30.8 3.9 %collective-permute-done.7.cross = f32[24,128]{1,0:T(8,128)S(1)} collective-permute-done((f32[24,128]{1,0:T(8,128)S(1)}, f32[24,128]{1,0:T(8,128)S(1)}, u32[]{:S(2)}, u32[]{:S(2)}) %collective-permute-start.7) | collective-permute-done | bytes 12320 | tf_op jit(solution)/shard_map/ppermute | solution.py:383
  38.2 2.1 %shard_map.155 = (f32[48,128]{1,0:T(8,128)S(1)}, f32[48,128]{1,0:T(8,128)S(1)}) custom-call(s32[72,128]{1,0:T(8,128)S(1)} %bitcast.34, s32[72,128]{1,0:T(8,128)S(1)} %bitcast.42, bf16[256,512]{1,0:T(8,128)(2,1)S(1)} %get-tuple-element.45.weight, f32[64,128]{1,0:T(8,128)S(1)} %collective-permute-done.9._.chip_edges), custom_call_target="tpu_custom_call" | custom-call | flops 2000000000 | bytes 6000000 | tf_op jit(solution)/shard_map/pallas_call | solution.py:389
  41.6 2.4 %collective-permute-done.11.cross = f32[112,128]{1,0:T(8,128)S(1)} collective-permute-done((f32[112,128]{1,0:T(8,128)S(1)}, f32[112,128]{1,0:T(8,128)S(1)}, u32[]{:S(2)}, u32[]{:S(2)}) %collective-permute-start.11) | collective-permute-done | bytes 57376 | tf_op jit(solution)/shard_map/ppermute | solution.py:383
  44.0 1.6 %collective-permute-start.12 = (f32[56,128]{1,0:T(8,128)S(1)}, f32[56,128]{1,0:T(8,128)S(1)}, u32[]{:S(2)}, u32[]{:S(2)}) collective-permute-start(f32[56,128]{1,0:T(8,128)S(1)} %pad_maximum_fusion.2), channel_id=1, source_target_pairs={{0,1},{1,2},{2,3},{3,0},{4,5},{5,6},{6,7},{7,4},{8,9},{9,10},{10,1... | collective-permute-start | bytes 86024 | tf_op jit(solution)/shard_map/ppermute | solution.py:372
  45.6 1.6 %collective-permute-start.13 = (f32[56,128]{1,0:T(8,128)S(1)}, f32[56,128]{1,0:T(8,128)S(1)}, u32[]{:S(2)}, u32[]{:S(2)}) collective-permute-start(f32[56,128]{1,0:T(8,128)S(1)} %pad_maximum_fusion.3), channel_id=1, source_target_pairs={{1,0},{2,1},{3,2},{0,3},{5,4},{6,5},{7,6},{4,7},{9,8},{10,9},{11,1... | collective-permute-start | bytes 86024 | tf_op jit(solution)/shard_map/ppermute | solution.py:377
  47.2 1.8 %collective-permute-done.12.side_minus = f32[56,128]{1,0:T(8,128)S(1)} collective-permute-done((f32[56,128]{1,0:T(8,128)S(1)}, f32[56,128]{1,0:T(8,128)S(1)}, u32[]{:S(2)}, u32[]{:S(2)}) %collective-permute-start.12) | collective-permute-done | bytes 28704 | tf_op jit(solution)/shard_map/ppermute | solution.py:372
  49.5 4.5 %shard_map.157 = (f32[24,128]{1,0:T(8,128)S(1)}, f32[24,128]{1,0:T(8,128)S(1)}, f32[24,128]{1,0:T(8,128)S(1)}, f32[1,16]{1,0:T(1,128)}) custom-call(f32[48,128]{1,0:T(8,128)S(1)} %collective-permute-done.10.chip, f32[48,128]{1,0:T(8,128)S(1)} %get-tuple-element.48.here, f32[112,128]{1,0:T(8,128)S(1)} %collective-permute-done.11.cross, ...), custom_call_target="tpu_custom_call" | custom-call | flops 6000000000 | bytes 18000000 | tf_op jit(solution)/shard_map/pallas_call | solution.py:439
  54.0 1.3 %collective-permute-start.14 = (f32[24,128]{1,0:T(8,128)S(1)}, f32[24,128]{1,0:T(8,128)S(1)}, u32[]{:S(2)}, u32[]{:S(2)}) collective-permute-start(f32[24,128]{1,0:T(8,128)S(1)} %get-tuple-element.52), channel_id=1, source_target_pairs={{0,1},{1,2},{2,3},{3,0},{4,5},{5,6},{6,7},{7,4},{8,9},{9,10},{10,1... | collective-permute-start | bytes 36872 | tf_op jit(solution)/shard_map/ppermute | solution.py:372
  55.3 1.9 %collective-permute-start.15 = (f32[24,128]{1,0:T(8,128)S(1)}, f32[24,128]{1,0:T(8,128)S(1)}, u32[]{:S(2)}, u32[]{:S(2)}) collective-permute-start(f32[24,128]{1,0:T(8,128)S(1)} %get-tuple-element.54), channel_id=1, source_target_pairs={{1,0},{2,1},{3,2},{0,3},{5,4},{6,5},{7,6},{4,7},{9,8},{10,9},{11,1... | collective-permute-start | bytes 36872 | tf_op jit(solution)/shard_map/ppermute | solution.py:377
  57.2 1.7 %collective-permute-done.14.back_minus = f32[24,128]{1,0:T(8,128)S(1)} collective-permute-done((f32[24,128]{1,0:T(8,128)S(1)}, f32[24,128]{1,0:T(8,128)S(1)}, u32[]{:S(2)}, u32[]{:S(2)}) %collective-permute-start.14) | collective-permute-done | bytes 12320 | tf_op jit(solution)/shard_map/ppermute | solution.py:372
  59.0 1.7 %collective-permute-start.16 = (f32[24,128]{1,0:T(8,128)S(1)}, f32[24,128]{1,0:T(8,128)S(1)}, u32[]{:S(2)}, u32[]{:S(2)}) collective-permute-start(f32[24,128]{1,0:T(8,128)S(1)} %pad_maximum_fusion.6), channel_id=1, source_target_pairs={{4,8},{8,4},{12,16},{16,12},{20,24},{24,20},{28,32},{32,28},{36,40... | collective-permute-start | bytes 36872 | tf_op jit(solution)/shard_map/ppermute | solution.py:383
  60.8 1.3 %shard_map.158 = (f32[256,128]{1,0:T(8,128)S(1)}, f32[256,128]{1,0:T(8,128)S(1)}) custom-call(f32[256,128]{1,0:T(8,128)S(1)} %get-tuple-element.55.head, f32[256,128]{1,0:T(8,128)S(1)} %get-tuple-element.56.cond, f32[256,128]{1,0:T(8,128)S(1)} %bitcast.20, f32[256,128]{1,0:T(8,128)S(1)} %bitcast.26, s32[256,128]{1,0:T(8,128)S(1)} %bitcast.23, ...), custom_call_target="tpu_custom_call" | custom-call | flops 1000000000 | bytes 3000000 | tf_op jit(solution)/shard_map/pallas_call | solution.py:446
  62.1 3.4 %collective-permute-done.16.cross = f32[24,128]{1,0:T(8,128)S(1)} collective-permute-done((f32[24,128]{1,0:T(8,128)S(1)}, f32[24,128]{1,0:T(8,128)S(1)}, u32[]{:S(2)}, u32[]{:S(2)}) %collective-permute-start.16) | collective-permute-done | bytes 12320 | tf_op jit(solution)/shard_map/ppermute | solution.py:383
  65.5 1.3 %shard_map.159 = f32[256,128]{1,0:T(8,128)} custom-call(f32[24,128]{1,0:T(8,128)S(1)} %collective-permute-done.16.cross, s32[72,128]{1,0:T(8,128)S(1)} %bitcast.36, s32[72,128]{1,0:T(8,128)S(1)} %bitcast.44, f32[256,128]{1,0:T(8,128)S(1)} %get-tuple-element.57.numerator, f32[256,128]{1,0:T(8,128)S(1)} %get-tuple-element.58.denominator), custom_call_target="tpu_custom_call" | custom-call | flops 1000000000 | bytes 3000000 | tf_op jit(solution)/shard_map/pallas_call | solution.py:461
  (73 shorter events, 11.5 us)
Async XLA Ops:
  2.0 6.7 %copy-start.12 = (s32[128,128]{1,0:T(8,128)S(1)}, s32[128,128]{1,0:T(8,128)}, u32[]{:S(2)}) copy-start(s32[128,128]{1,0:T(8,128)} %param.26) | copy-start | bytes 196612
  2.0 6.6 %copy-start.13 = (s32[128,128]{1,0:T(8,128)S(1)}, s32[128,128]{1,0:T(8,128)}, u32[]{:S(2)}) copy-start(s32[128,128]{1,0:T(8,128)} %param.25) | copy-start | bytes 196612
  3.1 5.6 %collective-permute-start = (f32[64,128]{1,0:T(8,128)S(1)}, f32[64,128]{1,0:T(8,128)S(1)}, u32[]{:S(2)}, u32[]{:S(2)}) collective-permute-start(f32[64,128]{1,0:T(8,128)S(1)} %get-tuple-element.32), channel_id=1, source_target_pairs={{0,4},{4,0},{8,12},{12,8},{16,20},{20,16},{24,28},{28,24},{32,36},... | collective-permute-start | bytes 98312 | tf_op jit(solution)/shard_map/ppermute | solution.py:383
  3.2 8.9 %collective-permute-start.2 = (f32[112,128]{1,0:T(8,128)S(1)}, f32[112,128]{1,0:T(8,128)S(1)}, u32[]{:S(2)}, u32[]{:S(2)}) collective-permute-start(f32[112,128]{1,0:T(8,128)S(1)} %get-tuple-element.35), channel_id=1, source_target_pairs={{4,8},{8,4},{12,16},{16,12},{20,24},{24,20},{28,32},{32,28},{36,40... | collective-permute-start | bytes 172040 | tf_op jit(solution)/shard_map/ppermute | solution.py:383
  10.8 1.3 %collective-permute-start.1 = (f32[48,128]{1,0:T(8,128)S(1)}, f32[48,128]{1,0:T(8,128)S(1)}, u32[]{:S(2)}, u32[]{:S(2)}) collective-permute-start(f32[48,128]{1,0:T(8,128)S(1)} %get-tuple-element.33), channel_id=1, source_target_pairs={{0,4},{4,0},{8,12},{12,8},{16,20},{20,16},{24,28},{28,24},{32,36},... | collective-permute-start | bytes 73736 | tf_op jit(solution)/shard_map/ppermute | solution.py:383
  12.1 6.0 %collective-permute-start.3 = (f32[56,128]{1,0:T(8,128)S(1)}, f32[56,128]{1,0:T(8,128)S(1)}, u32[]{:S(2)}, u32[]{:S(2)}) collective-permute-start(f32[56,128]{1,0:T(8,128)S(1)} %pad_maximum_fusion), channel_id=1, source_target_pairs={{0,1},{1,2},{2,3},{3,0},{4,5},{5,6},{6,7},{7,4},{8,9},{9,10},{10,1... | collective-permute-start | bytes 86024 | tf_op jit(solution)/shard_map/ppermute | solution.py:372
  14.1 4.0 %collective-permute-start.4 = (f32[56,128]{1,0:T(8,128)S(1)}, f32[56,128]{1,0:T(8,128)S(1)}, u32[]{:S(2)}, u32[]{:S(2)}) collective-permute-start(f32[56,128]{1,0:T(8,128)S(1)} %pad_maximum_fusion.1), channel_id=1, source_target_pairs={{1,0},{2,1},{3,2},{0,3},{5,4},{6,5},{7,6},{4,7},{9,8},{10,9},{11,1... | collective-permute-start | bytes 86024 | tf_op jit(solution)/shard_map/ppermute | solution.py:377
  18.1 11.4 %copy-start.2 = (s32[32,8,128]{2,1,0:T(8,128)S(1)}, s32[32,8,128]{2,1,0:T(8,128)}, u32[]{:S(2)}) copy-start(s32[32,8,128]{2,1,0:T(8,128)} %param.17) | copy-start | bytes 393220
  18.1 11.3 %copy-start.3 = (f32[32,8,128]{2,1,0:T(8,128)S(1)}, f32[32,8,128]{2,1,0:T(8,128)}, u32[]{:S(2)}) copy-start(f32[32,8,128]{2,1,0:T(8,128)} %param.16) | copy-start | bytes 393220
  18.1 11.3 %copy-start.4 = (f32[32,8,128]{2,1,0:T(8,128)S(1)}, f32[32,8,128]{2,1,0:T(8,128)}, u32[]{:S(2)}) copy-start(f32[32,8,128]{2,1,0:T(8,128)} %param.18) | copy-start | bytes 393220
  22.7 5.0 %collective-permute-start.5 = (f32[24,128]{1,0:T(8,128)S(1)}, f32[24,128]{1,0:T(8,128)S(1)}, u32[]{:S(2)}, u32[]{:S(2)}) collective-permute-start(f32[24,128]{1,0:T(8,128)S(1)} %get-tuple-element.40), channel_id=1, source_target_pairs={{0,1},{1,2},{2,3},{3,0},{4,5},{5,6},{6,7},{7,4},{8,9},{9,10},{10,1... | collective-permute-start | bytes 36872 | tf_op jit(solution)/shard_map/ppermute | solution.py:372
  24.5 3.7 %collective-permute-start.6 = (f32[24,128]{1,0:T(8,128)S(1)}, f32[24,128]{1,0:T(8,128)S(1)}, u32[]{:S(2)}, u32[]{:S(2)}) collective-permute-start(f32[24,128]{1,0:T(8,128)S(1)} %get-tuple-element.42), channel_id=1, source_target_pairs={{1,0},{2,1},{3,2},{0,3},{5,4},{6,5},{7,6},{4,7},{9,8},{10,9},{11,1... | collective-permute-start | bytes 36872 | tf_op jit(solution)/shard_map/ppermute | solution.py:377
  28.2 1.3 %collective-permute-start.8 = (f32[24,128]{1,0:T(8,128)S(1)}, f32[24,128]{1,0:T(8,128)S(1)}, u32[]{:S(2)}, u32[]{:S(2)}) collective-permute-start(f32[24,128]{1,0:T(8,128)S(1)} %pad_maximum_fusion.5), channel_id=1, source_target_pairs={{0,4},{4,0},{8,12},{12,8},{16,20},{20,16},{24,28},{28,24},{32,36},... | collective-permute-start | bytes 36872 | tf_op jit(solution)/shard_map/ppermute | solution.py:383
  28.2 6.5 %collective-permute-start.7 = (f32[24,128]{1,0:T(8,128)S(1)}, f32[24,128]{1,0:T(8,128)S(1)}, u32[]{:S(2)}, u32[]{:S(2)}) collective-permute-start(f32[24,128]{1,0:T(8,128)S(1)} %pad_maximum_fusion.4), channel_id=1, source_target_pairs={{4,8},{8,4},{12,16},{16,12},{20,24},{24,20},{28,32},{32,28},{36,40... | collective-permute-start | bytes 36872 | tf_op jit(solution)/shard_map/ppermute | solution.py:383
  29.5 5.2 %copy-start = (f32[32,8,128]{2,1,0:T(8,128)S(1)}, f32[32,8,128]{2,1,0:T(8,128)}, u32[]{:S(2)}) copy-start(f32[32,8,128]{2,1,0:T(8,128)} %param.15) | copy-start | bytes 393220
  35.6 2.7 %collective-permute-start.9 = (f32[64,128]{1,0:T(8,128)S(1)}, f32[64,128]{1,0:T(8,128)S(1)}, u32[]{:S(2)}, u32[]{:S(2)}) collective-permute-start(f32[64,128]{1,0:T(8,128)S(1)} %get-tuple-element.46), channel_id=1, source_target_pairs={{0,4},{4,0},{8,12},{12,8},{16,20},{20,16},{24,28},{28,24},{32,36},... | collective-permute-start | bytes 98312 | tf_op jit(solution)/shard_map/ppermute | solution.py:383
  37.0 7.0 %collective-permute-start.11 = (f32[112,128]{1,0:T(8,128)S(1)}, f32[112,128]{1,0:T(8,128)S(1)}, u32[]{:S(2)}, u32[]{:S(2)}) collective-permute-start(f32[112,128]{1,0:T(8,128)S(1)} %shard_map.156), channel_id=1, source_target_pairs={{4,8},{8,4},{12,16},{16,12},{20,24},{24,20},{28,32},{32,28},{36,40... | collective-permute-start | bytes 172040 | tf_op jit(solution)/shard_map/ppermute | solution.py:383
  40.3 1.3 %collective-permute-start.10 = (f32[48,128]{1,0:T(8,128)S(1)}, f32[48,128]{1,0:T(8,128)S(1)}, u32[]{:S(2)}, u32[]{:S(2)}) collective-permute-start(f32[48,128]{1,0:T(8,128)S(1)} %get-tuple-element.47), channel_id=1, source_target_pairs={{0,4},{4,0},{8,12},{12,8},{16,20},{20,16},{24,28},{28,24},{32,36},... | collective-permute-start | bytes 73736 | tf_op jit(solution)/shard_map/ppermute | solution.py:383
  44.0 5.1 %collective-permute-start.12 = (f32[56,128]{1,0:T(8,128)S(1)}, f32[56,128]{1,0:T(8,128)S(1)}, u32[]{:S(2)}, u32[]{:S(2)}) collective-permute-start(f32[56,128]{1,0:T(8,128)S(1)} %pad_maximum_fusion.2), channel_id=1, source_target_pairs={{0,1},{1,2},{2,3},{3,0},{4,5},{5,6},{6,7},{7,4},{8,9},{9,10},{10,1... | collective-permute-start | bytes 86024 | tf_op jit(solution)/shard_map/ppermute | solution.py:372
  45.6 3.9 %collective-permute-start.13 = (f32[56,128]{1,0:T(8,128)S(1)}, f32[56,128]{1,0:T(8,128)S(1)}, u32[]{:S(2)}, u32[]{:S(2)}) collective-permute-start(f32[56,128]{1,0:T(8,128)S(1)} %pad_maximum_fusion.3), channel_id=1, source_target_pairs={{1,0},{2,1},{3,2},{0,3},{5,4},{6,5},{7,6},{4,7},{9,8},{10,9},{11,1... | collective-permute-start | bytes 86024 | tf_op jit(solution)/shard_map/ppermute | solution.py:377
  54.0 4.9 %collective-permute-start.14 = (f32[24,128]{1,0:T(8,128)S(1)}, f32[24,128]{1,0:T(8,128)S(1)}, u32[]{:S(2)}, u32[]{:S(2)}) collective-permute-start(f32[24,128]{1,0:T(8,128)S(1)} %get-tuple-element.52), channel_id=1, source_target_pairs={{0,1},{1,2},{2,3},{3,0},{4,5},{5,6},{6,7},{7,4},{8,9},{9,10},{10,1... | collective-permute-start | bytes 36872 | tf_op jit(solution)/shard_map/ppermute | solution.py:372
  55.3 3.7 %collective-permute-start.15 = (f32[24,128]{1,0:T(8,128)S(1)}, f32[24,128]{1,0:T(8,128)S(1)}, u32[]{:S(2)}, u32[]{:S(2)}) collective-permute-start(f32[24,128]{1,0:T(8,128)S(1)} %get-tuple-element.54), channel_id=1, source_target_pairs={{1,0},{2,1},{3,2},{0,3},{5,4},{6,5},{7,6},{4,7},{9,8},{10,9},{11,1... | collective-permute-start | bytes 36872 | tf_op jit(solution)/shard_map/ppermute | solution.py:377
  59.0 1.8 %collective-permute-start.17 = (f32[24,128]{1,0:T(8,128)S(1)}, f32[24,128]{1,0:T(8,128)S(1)}, u32[]{:S(2)}, u32[]{:S(2)}) collective-permute-start(f32[24,128]{1,0:T(8,128)S(1)} %pad_maximum_fusion.7), channel_id=1, source_target_pairs={{0,4},{4,0},{8,12},{12,8},{16,20},{20,16},{24,28},{28,24},{32,36},... | collective-permute-start | bytes 36872 | tf_op jit(solution)/shard_map/ppermute | solution.py:383
  59.0 6.5 %collective-permute-start.16 = (f32[24,128]{1,0:T(8,128)S(1)}, f32[24,128]{1,0:T(8,128)S(1)}, u32[]{:S(2)}, u32[]{:S(2)}) collective-permute-start(f32[24,128]{1,0:T(8,128)S(1)} %pad_maximum_fusion.6), channel_id=1, source_target_pairs={{4,8},{8,4},{12,16},{16,12},{20,24},{24,20},{28,32},{32,28},{36,40... | collective-permute-start | bytes 36872 | tf_op jit(solution)/shard_map/ppermute | solution.py:383
  (8 other events, 8.1 us)

commit v6 on v5

--- a/solution.py
+++ b/solution.py
@@ -100,9 +100,30 @@
                         out[at : at + 1, :] = jnp.sum(jnp.where(mask, part, 0.0), 0, keepdims=True)
 
 
-def start_kernel(head, cond, row, col, chip_edge, cross, edge_minus, edge_plus, weight):
+def leads():
+    return lax.axis_index("gx") == 0
+
+
+def start_kernel(
+    head, cond, row, col, chip_edge, cross, edge_minus, edge_plus, weight, chip, here
+):
     lay_cells(head, cond, weight, chip_edge, cross, edge_minus, edge_plus)
     gather_cells(row, col, weight, ((cross, x_places()[1]),))
+
+    @pl.when(leads())
+    def _():
+        gather_cells(row, col, weight, ((chip, x_places()[0]), (here, 1)))
+
+
+def first_rest_kernel(row, col, weight, _, chip_in, here_in, chip, here):
+    @pl.when(leads())
+    def _():
+        chip[...] = chip_in[...]
+        here[...] = here_in[...]
+
+    @pl.when(jnp.logical_not(leads()))
+    def _():
+        gather_cells(row, col, weight, ((chip, x_places()[0]), (here, 1)))
 
 
 def cross_kernel(row, col, weight, cross_edge, cross):
@@ -383,10 +404,12 @@
     return lax.ppermute(x, axis, [p for i, j in pairs for p in ((i, j), (j, i))])
 
 
-def spread(row, col, chip_edge, cross, edge_minus, edge_plus, weight):
+def spread(row, col, chip_edge, cross, edge_minus, edge_plus, weight, *early):
     from_cross = swap(cross, "gx", 1)
     chip_edges = swap(chip_edge, "gx", 0)
-    chip, here = call(rest_kernel, [SLOT] * 2, micros=2)(row, col, weight, chip_edges)
+    chip, here = call(first_rest_kernel if early else rest_kernel, [SLOT] * 2, micros=2)(
+        row, col, weight, chip_edges, *early
+    )
     from_chip = swap(chip, "gx", 0)
     parts = (from_chip, here, from_cross)
     side_minus = up(jnp.concatenate([x[32:48] for x in parts] + [edge_plus], 0), "gy")
@@ -430,7 +453,7 @@
     row, col = (x.reshape(SLOTS, LANES) for x in (send_row, send_col))
     head_old = head
     cond = conduct(head, sat, alpha * (1.0 + wet.astype(F32)))
-    messages = call(start_kernel, [EDGE, MESSAGE] + SIDES, micros=2)(head, cond, row, col)
+    messages = call(start_kernel, [EDGE, MESSAGE] + SIDES + [SLOT] * 2, micros=2)(head, cond, row, col)
     collar_link, need = call(collar_kernel, [((BLOCKS, LANES), F32), ((1, LANES), F32)])(
         stem_link.reshape(1, BLOCKS), entry_seg.reshape(1, BLOCKS), demand.reshape(1, PLANTS)
     )

time: 67 us -> 67.2 us (level)
  waiting for transfers between devices: 19.2 us -> 20.6 us
  starting transfers between devices: 24.2 us -> 23 us
    ppermute x10, waiting for transfers between devices: 12.1 us -> 13.4 us  [swap(): lax.ppermute(x, axis, [p for i, j in pairs for p in ((i, j), (j, i))])]
    ppermute x10, starting transfers between devices: 10.2 us -> 8.98 us  [swap(): lax.ppermute(x, axis, [p for i, j in pairs for p in ((i, j), (j, i))])]
  transfers between devices with their start and end apart: 18 -> 18, of which waited for: 12 -> 13; matrix products, arithmetic and copies ran while one was open for 0% -> 0% of each run, Pallas kernels for 12% -> 9%
where the time goes in v6:
time: 67.2 us; the launch traced here: 67 us
  starting transfers between devices  23 us (34%)
  waiting for transfers between devices  20.6 us (31%)
  Pallas kernels  20.3 us (30%)
  other arithmetic  1.46 us (2%)
  between operations  0.92 us (1%)
  local copies, waits for them, and re-layouts  0.77 us (1%)
    ppermute x10, waiting for transfers between devices, swap(): lax.ppermute(x, axis, [p for i, j in pairs for p in ((i, j), (j, i))])  13.4 us
    pallas_call x2, Pallas kernels, on_device(): call(root_kernel, [((24, 128), F32)] * 3 + [((1, PLANTS), F32)], [((144,...  9.05 us
    ppermute x10, starting transfers between devices, swap(): lax.ppermute(x, axis, [p for i, j in pairs for p in ((i, j), (j, i))])  8.98 us
    ppermute x4, starting transfers between devices, down(): return lax.ppermute(x, axis, [((i + 1) % size, i) for i in range(size)])  7.26 us
    ppermute x4, starting transfers between devices, up(): return lax.ppermute(x, axis, [(i, (i + 1) % size) for i in range(size)])  6.73 us
    ppermute x4, waiting for transfers between devices, up(): return lax.ppermute(x, axis, [(i, (i + 1) % size) for i in range(size)])  6.13 us
    pallas_call x1, Pallas kernels, on_device(): call(start_kernel, [EDGE, MESSAGE] + SIDES + [SLOT] * 2, micros=2)  3.19 us
    pallas_call x2, Pallas kernels, on_device(): call(terms_kernel, [((CELLS, LANES), F32)] * 2, [((128, 128), F32)])  2.64 us
  transfers between devices with their start and end apart: 18, of which 13 were waited for; matrix products, arithmetic and copies ran while one was open for 0% of the time, Pallas kernels for 9%

profile of v6, /device:TPU:0, one launch (start us, length us, event | category | flops | bytes accessed | tf_op | source)
XLA Modules:
  0.0 67.0 jit_solution(304984666887645858)
XLA Ops:
  2.0 3.2 %shard_map.149 = (f32[64,128]{1,0:T(8,128)S(1)}, f32[112,128]{1,0:T(8,128)S(1)}, f32[8,128]{1,0:T(8,128)S(1)}, f32[8,128]{1,0:T(8,128)S(1)}, bf16[256,512]{1,0:T...) custom-call(f32[256,128]{1,0:T(8,128)S(1)} %bitcast.17, f32[256,128]{1,0:T(8,128)S(1)} %multiply_multiply_fusion.cond, ...), custom_call_target="tpu_custom_call" | custom-call | flops 2000000000 | bytes 6000000 | tf_op jit(solution)/shard_map/pallas_call | solution.py:456
  5.3 3.3 %collective-permute-start.2 = (f32[112,128]{1,0:T(8,128)S(1)}, f32[112,128]{1,0:T(8,128)S(1)}, u32[]{:S(2)}, u32[]{:S(2)}) collective-permute-start(f32[112,128]{1,0:T(8,128)S(1)} %get-tuple-element.39), channel_id=1, source_target_pairs={{4,8},{8,4},{12,16},{16,12},{20,24},{24,20},{28,32},{32,28},{36,40... | collective-permute-start | bytes 172040 | tf_op jit(solution)/shard_map/ppermute | solution.py:404
  10.1 2.2 %collective-permute-done.2.cross = f32[112,128]{1,0:T(8,128)S(1)} collective-permute-done((f32[112,128]{1,0:T(8,128)S(1)}, f32[112,128]{1,0:T(8,128)S(1)}, u32[]{:S(2)}, u32[]{:S(2)}) %collective-permute-start.2) | collective-permute-done | bytes 57376 | tf_op jit(solution)/shard_map/ppermute | solution.py:404
  12.3 2.0 %collective-permute-start.3 = (f32[56,128]{1,0:T(8,128)S(1)}, f32[56,128]{1,0:T(8,128)S(1)}, u32[]{:S(2)}, u32[]{:S(2)}) collective-permute-start(f32[56,128]{1,0:T(8,128)S(1)} %pad_maximum_fusion), channel_id=1, source_target_pairs={{0,1},{1,2},{2,3},{3,0},{4,5},{5,6},{6,7},{7,4},{8,9},{9,10},{10,1... | collective-permute-start | bytes 86024 | tf_op jit(solution)/shard_map/ppermute | solution.py:393
  14.3 2.2 %collective-permute-start.4 = (f32[56,128]{1,0:T(8,128)S(1)}, f32[56,128]{1,0:T(8,128)S(1)}, u32[]{:S(2)}, u32[]{:S(2)}) collective-permute-start(f32[56,128]{1,0:T(8,128)S(1)} %pad_maximum_fusion.1), channel_id=1, source_target_pairs={{1,0},{2,1},{3,2},{0,3},{5,4},{6,5},{7,6},{4,7},{9,8},{10,9},{11,1... | collective-permute-start | bytes 86024 | tf_op jit(solution)/shard_map/ppermute | solution.py:398
  18.3 4.5 %shard_map.152 = (f32[24,128]{1,0:T(8,128)S(1)}, f32[24,128]{1,0:T(8,128)S(1)}, f32[24,128]{1,0:T(8,128)S(1)}, f32[1,16]{1,0:T(1,128)}) custom-call(f32[48,128]{1,0:T(8,128)S(1)} %collective-permute-done.1.chip, f32[48,128]{1,0:T(8,128)S(1)} %get-tuple-element.38.here, f32[112,128]{1,0:T(8,128)S(1)} %collective-permute-done.2.cross, ...), custom_call_target="tpu_custom_call" | custom-call | flops 6000000000 | bytes 18000000 | tf_op jit(solution)/shard_map/pallas_call | solution.py:462
  22.8 1.8 %collective-permute-start.5 = (f32[24,128]{1,0:T(8,128)S(1)}, f32[24,128]{1,0:T(8,128)S(1)}, u32[]{:S(2)}, u32[]{:S(2)}) collective-permute-start(f32[24,128]{1,0:T(8,128)S(1)} %get-tuple-element.44), channel_id=1, source_target_pairs={{0,1},{1,2},{2,3},{3,0},{4,5},{5,6},{6,7},{7,4},{8,9},{9,10},{10,1... | collective-permute-start | bytes 36872 | tf_op jit(solution)/shard_map/ppermute | solution.py:393
  24.7 1.5 %collective-permute-start.6 = (f32[24,128]{1,0:T(8,128)S(1)}, f32[24,128]{1,0:T(8,128)S(1)}, u32[]{:S(2)}, u32[]{:S(2)}) collective-permute-start(f32[24,128]{1,0:T(8,128)S(1)} %get-tuple-element.46), channel_id=1, source_target_pairs={{1,0},{2,1},{3,2},{0,3},{5,4},{6,5},{7,6},{4,7},{9,8},{10,9},{11,1... | collective-permute-start | bytes 36872 | tf_op jit(solution)/shard_map/ppermute | solution.py:398
  26.2 1.7 %collective-permute-done.5.back_minus = f32[24,128]{1,0:T(8,128)S(1)} collective-permute-done((f32[24,128]{1,0:T(8,128)S(1)}, f32[24,128]{1,0:T(8,128)S(1)}, u32[]{:S(2)}, u32[]{:S(2)}) %collective-permute-start.5) | collective-permute-done | bytes 12320 | tf_op jit(solution)/shard_map/ppermute | solution.py:393
  28.4 1.8 %collective-permute-start.7 = (f32[24,128]{1,0:T(8,128)S(1)}, f32[24,128]{1,0:T(8,128)S(1)}, u32[]{:S(2)}, u32[]{:S(2)}) collective-permute-start(f32[24,128]{1,0:T(8,128)S(1)} %pad_maximum_fusion.4), channel_id=1, source_target_pairs={{4,8},{8,4},{12,16},{16,12},{20,24},{24,20},{28,32},{32,28},{36,40... | collective-permute-start | bytes 36872 | tf_op jit(solution)/shard_map/ppermute | solution.py:404
  30.3 1.3 %shard_map.153 = (f32[256,128]{1,0:T(8,128)S(1)}, f32[256,128]{1,0:T(8,128)S(1)}) custom-call(f32[256,128]{1,0:T(8,128)S(1)} %bitcast.18, f32[256,128]{1,0:T(8,128)S(1)} %multiply_multiply_fusion.cond, f32[256,128]{1,0:T(8,128)S(1)} %bitcast.19, f32[256,128]{1,0:T(8,128)S(1)} %bitcast.24, s32[256,128]{1,0:T(8,128)S(1)} %bitcast.21, f32[256,128]{1,0:T(8,128)S(1)} %bitcast.27, ...), custom_call_target="tpu_custom_call" | custom-call | flops 1000000000 | bytes 3000000 | tf_op jit(solution)/shard_map/pallas_call | solution.py:469
  31.6 3.5 %collective-permute-done.7.cross = f32[24,128]{1,0:T(8,128)S(1)} collective-permute-done((f32[24,128]{1,0:T(8,128)S(1)}, f32[24,128]{1,0:T(8,128)S(1)}, u32[]{:S(2)}, u32[]{:S(2)}) %collective-permute-start.7) | collective-permute-done | bytes 12320 | tf_op jit(solution)/shard_map/ppermute | solution.py:404
  37.1 1.7 %collective-permute-start.11 = (f32[112,128]{1,0:T(8,128)S(1)}, f32[112,128]{1,0:T(8,128)S(1)}, u32[]{:S(2)}, u32[]{:S(2)}) collective-permute-start(f32[112,128]{1,0:T(8,128)S(1)} %shard_map.156), channel_id=1, source_target_pairs={{4,8},{8,4},{12,16},{16,12},{20,24},{24,20},{28,32},{32,28},{36,40... | collective-permute-start | bytes 172040 | tf_op jit(solution)/shard_map/ppermute | solution.py:404
  38.8 2.1 %shard_map.155 = (f32[48,128]{1,0:T(8,128)S(1)}, f32[48,128]{1,0:T(8,128)S(1)}) custom-call(s32[72,128]{1,0:T(8,128)S(1)} %bitcast.34, s32[72,128]{1,0:T(8,128)S(1)} %bitcast.42, bf16[256,512]{1,0:T(8,128)(2,1)S(1)} %get-tuple-element.49.weight, f32[64,128]{1,0:T(8,128)S(1)} %collective-permute-done.9._.chip_edges), custom_call_target="tpu_custom_call" | custom-call | flops 2000000000 | bytes 6000000 | tf_op jit(solution)/shard_map/pallas_call | solution.py:410
  42.2 2.0 %collective-permute-done.11.cross = f32[112,128]{1,0:T(8,128)S(1)} collective-permute-done((f32[112,128]{1,0:T(8,128)S(1)}, f32[112,128]{1,0:T(8,128)S(1)}, u32[]{:S(2)}, u32[]{:S(2)}) %collective-permute-start.11) | collective-permute-done | bytes 57376 | tf_op jit(solution)/shard_map/ppermute | solution.py:404
  44.1 1.6 %collective-permute-start.12 = (f32[56,128]{1,0:T(8,128)S(1)}, f32[56,128]{1,0:T(8,128)S(1)}, u32[]{:S(2)}, u32[]{:S(2)}) collective-permute-start(f32[56,128]{1,0:T(8,128)S(1)} %pad_maximum_fusion.2), channel_id=1, source_target_pairs={{0,1},{1,2},{2,3},{3,0},{4,5},{5,6},{6,7},{7,4},{8,9},{9,10},{10,1... | collective-permute-start | bytes 86024 | tf_op jit(solution)/shard_map/ppermute | solution.py:393
  45.8 1.6 %collective-permute-start.13 = (f32[56,128]{1,0:T(8,128)S(1)}, f32[56,128]{1,0:T(8,128)S(1)}, u32[]{:S(2)}, u32[]{:S(2)}) collective-permute-start(f32[56,128]{1,0:T(8,128)S(1)} %pad_maximum_fusion.3), channel_id=1, source_target_pairs={{1,0},{2,1},{3,2},{0,3},{5,4},{6,5},{7,6},{4,7},{9,8},{10,9},{11,1... | collective-permute-start | bytes 86024 | tf_op jit(solution)/shard_map/ppermute | solution.py:398
  47.4 1.8 %collective-permute-done.12.side_minus = f32[56,128]{1,0:T(8,128)S(1)} collective-permute-done((f32[56,128]{1,0:T(8,128)S(1)}, f32[56,128]{1,0:T(8,128)S(1)}, u32[]{:S(2)}, u32[]{:S(2)}) %collective-permute-start.12) | collective-permute-done | bytes 28704 | tf_op jit(solution)/shard_map/ppermute | solution.py:393
  49.7 4.5 %shard_map.157 = (f32[24,128]{1,0:T(8,128)S(1)}, f32[24,128]{1,0:T(8,128)S(1)}, f32[24,128]{1,0:T(8,128)S(1)}, f32[1,16]{1,0:T(1,128)}) custom-call(f32[48,128]{1,0:T(8,128)S(1)} %collective-permute-done.10.chip, f32[48,128]{1,0:T(8,128)S(1)} %get-tuple-element.52.here, f32[112,128]{1,0:T(8,128)S(1)} %collective-permute-done.11.cross, ...), custom_call_target="tpu_custom_call" | custom-call | flops 6000000000 | bytes 18000000 | tf_op jit(solution)/shard_map/pallas_call | solution.py:462
  55.5 1.9 %collective-permute-start.15 = (f32[24,128]{1,0:T(8,128)S(1)}, f32[24,128]{1,0:T(8,128)S(1)}, u32[]{:S(2)}, u32[]{:S(2)}) collective-permute-start(f32[24,128]{1,0:T(8,128)S(1)} %get-tuple-element.58), channel_id=1, source_target_pairs={{1,0},{2,1},{3,2},{0,3},{5,4},{6,5},{7,6},{4,7},{9,8},{10,9},{11,1... | collective-permute-start | bytes 36872 | tf_op jit(solution)/shard_map/ppermute | solution.py:398
  57.4 1.7 %collective-permute-done.14.back_minus = f32[24,128]{1,0:T(8,128)S(1)} collective-permute-done((f32[24,128]{1,0:T(8,128)S(1)}, f32[24,128]{1,0:T(8,128)S(1)}, u32[]{:S(2)}, u32[]{:S(2)}) %collective-permute-start.14) | collective-permute-done | bytes 12320 | tf_op jit(solution)/shard_map/ppermute | solution.py:393
  59.2 1.8 %collective-permute-start.16 = (f32[24,128]{1,0:T(8,128)S(1)}, f32[24,128]{1,0:T(8,128)S(1)}, u32[]{:S(2)}, u32[]{:S(2)}) collective-permute-start(f32[24,128]{1,0:T(8,128)S(1)} %pad_maximum_fusion.6), channel_id=1, source_target_pairs={{4,8},{8,4},{12,16},{16,12},{20,24},{24,20},{28,32},{32,28},{36,40... | collective-permute-start | bytes 36872 | tf_op jit(solution)/shard_map/ppermute | solution.py:404
  61.0 1.3 %shard_map.158 = (f32[256,128]{1,0:T(8,128)S(1)}, f32[256,128]{1,0:T(8,128)S(1)}) custom-call(f32[256,128]{1,0:T(8,128)S(1)} %get-tuple-element.59.head, f32[256,128]{1,0:T(8,128)S(1)} %get-tuple-element.60.cond, f32[256,128]{1,0:T(8,128)S(1)} %bitcast.20, f32[256,128]{1,0:T(8,128)S(1)} %bitcast.26, s32[256,128]{1,0:T(8,128)S(1)} %bitcast.23, ...), custom_call_target="tpu_custom_call" | custom-call | flops 1000000000 | bytes 3000000 | tf_op jit(solution)/shard_map/pallas_call | solution.py:469
  62.3 3.4 %collective-permute-done.16.cross = f32[24,128]{1,0:T(8,128)S(1)} collective-permute-done((f32[24,128]{1,0:T(8,128)S(1)}, f32[24,128]{1,0:T(8,128)S(1)}, u32[]{:S(2)}, u32[]{:S(2)}) %collective-permute-start.16) | collective-permute-done | bytes 12320 | tf_op jit(solution)/shard_map/ppermute | solution.py:404
  (73 shorter events, 11.6 us)
Async XLA Ops:
  2.0 6.7 %copy-start.12 = (s32[128,128]{1,0:T(8,128)S(1)}, s32[128,128]{1,0:T(8,128)}, u32[]{:S(2)}) copy-start(s32[128,128]{1,0:T(8,128)} %param.26) | copy-start | bytes 196612
  2.0 6.6 %copy-start.13 = (s32[128,128]{1,0:T(8,128)S(1)}, s32[128,128]{1,0:T(8,128)}, u32[]{:S(2)}) copy-start(s32[128,128]{1,0:T(8,128)} %param.25) | copy-start | bytes 196612
  5.2 3.6 %collective-permute-start = (f32[64,128]{1,0:T(8,128)S(1)}, f32[64,128]{1,0:T(8,128)S(1)}, u32[]{:S(2)}, u32[]{:S(2)}) collective-permute-start(f32[64,128]{1,0:T(8,128)S(1)} %get-tuple-element.34), channel_id=1, source_target_pairs={{0,4},{4,0},{8,12},{12,8},{16,20},{20,16},{24,28},{28,24},{32,36},... | collective-permute-start | bytes 98312 | tf_op jit(solution)/shard_map/ppermute | solution.py:404
  5.3 7.0 %collective-permute-start.2 = (f32[112,128]{1,0:T(8,128)S(1)}, f32[112,128]{1,0:T(8,128)S(1)}, u32[]{:S(2)}, u32[]{:S(2)}) collective-permute-start(f32[112,128]{1,0:T(8,128)S(1)} %get-tuple-element.39), channel_id=1, source_target_pairs={{4,8},{8,4},{12,16},{16,12},{20,24},{24,20},{28,32},{32,28},{36,40... | collective-permute-start | bytes 172040 | tf_op jit(solution)/shard_map/ppermute | solution.py:404
  8.8 1.3 %collective-permute-start.1 = (f32[48,128]{1,0:T(8,128)S(1)}, f32[48,128]{1,0:T(8,128)S(1)}, u32[]{:S(2)}, u32[]{:S(2)}) collective-permute-start(f32[48,128]{1,0:T(8,128)S(1)} %get-tuple-element.37), channel_id=1, source_target_pairs={{0,4},{4,0},{8,12},{12,8},{16,20},{20,16},{24,28},{28,24},{32,36},... | collective-permute-start | bytes 73736 | tf_op jit(solution)/shard_map/ppermute | solution.py:404
  12.3 6.0 %collective-permute-start.3 = (f32[56,128]{1,0:T(8,128)S(1)}, f32[56,128]{1,0:T(8,128)S(1)}, u32[]{:S(2)}, u32[]{:S(2)}) collective-permute-start(f32[56,128]{1,0:T(8,128)S(1)} %pad_maximum_fusion), channel_id=1, source_target_pairs={{0,1},{1,2},{2,3},{3,0},{4,5},{5,6},{6,7},{7,4},{8,9},{9,10},{10,1... | collective-permute-start | bytes 86024 | tf_op jit(solution)/shard_map/ppermute | solution.py:393
  14.3 4.0 %collective-permute-start.4 = (f32[56,128]{1,0:T(8,128)S(1)}, f32[56,128]{1,0:T(8,128)S(1)}, u32[]{:S(2)}, u32[]{:S(2)}) collective-permute-start(f32[56,128]{1,0:T(8,128)S(1)} %pad_maximum_fusion.1), channel_id=1, source_target_pairs={{1,0},{2,1},{3,2},{0,3},{5,4},{6,5},{7,6},{4,7},{9,8},{10,9},{11,1... | collective-permute-start | bytes 86024 | tf_op jit(solution)/shard_map/ppermute | solution.py:398
  18.3 11.9 %copy-start.2 = (s32[32,8,128]{2,1,0:T(8,128)S(1)}, s32[32,8,128]{2,1,0:T(8,128)}, u32[]{:S(2)}) copy-start(s32[32,8,128]{2,1,0:T(8,128)} %param.17) | copy-start | bytes 393220
  18.3 11.9 %copy-start.3 = (f32[32,8,128]{2,1,0:T(8,128)S(1)}, f32[32,8,128]{2,1,0:T(8,128)}, u32[]{:S(2)}) copy-start(f32[32,8,128]{2,1,0:T(8,128)} %param.16) | copy-start | bytes 393220
  18.3 11.9 %copy-start.4 = (f32[32,8,128]{2,1,0:T(8,128)S(1)}, f32[32,8,128]{2,1,0:T(8,128)}, u32[]{:S(2)}) copy-start(f32[32,8,128]{2,1,0:T(8,128)} %param.18) | copy-start | bytes 393220
  22.8 5.0 %collective-permute-start.5 = (f32[24,128]{1,0:T(8,128)S(1)}, f32[24,128]{1,0:T(8,128)S(1)}, u32[]{:S(2)}, u32[]{:S(2)}) collective-permute-start(f32[24,128]{1,0:T(8,128)S(1)} %get-tuple-element.44), channel_id=1, source_target_pairs={{0,1},{1,2},{2,3},{3,0},{4,5},{5,6},{6,7},{7,4},{8,9},{9,10},{10,1... | collective-permute-start | bytes 36872 | tf_op jit(solution)/shard_map/ppermute | solution.py:393
  24.7 3.7 %collective-permute-start.6 = (f32[24,128]{1,0:T(8,128)S(1)}, f32[24,128]{1,0:T(8,128)S(1)}, u32[]{:S(2)}, u32[]{:S(2)}) collective-permute-start(f32[24,128]{1,0:T(8,128)S(1)} %get-tuple-element.46), channel_id=1, source_target_pairs={{1,0},{2,1},{3,2},{0,3},{5,4},{6,5},{7,6},{4,7},{9,8},{10,9},{11,1... | collective-permute-start | bytes 36872 | tf_op jit(solution)/shard_map/ppermute | solution.py:398
  28.4 1.9 %collective-permute-start.8 = (f32[24,128]{1,0:T(8,128)S(1)}, f32[24,128]{1,0:T(8,128)S(1)}, u32[]{:S(2)}, u32[]{:S(2)}) collective-permute-start(f32[24,128]{1,0:T(8,128)S(1)} %pad_maximum_fusion.5), channel_id=1, source_target_pairs={{0,4},{4,0},{8,12},{12,8},{16,20},{20,16},{24,28},{28,24},{32,36},... | collective-permute-start | bytes 36872 | tf_op jit(solution)/shard_map/ppermute | solution.py:404
  28.4 6.7 %collective-permute-start.7 = (f32[24,128]{1,0:T(8,128)S(1)}, f32[24,128]{1,0:T(8,128)S(1)}, u32[]{:S(2)}, u32[]{:S(2)}) collective-permute-start(f32[24,128]{1,0:T(8,128)S(1)} %pad_maximum_fusion.4), channel_id=1, source_target_pairs={{4,8},{8,4},{12,16},{16,12},{20,24},{24,20},{28,32},{32,28},{36,40... | collective-permute-start | bytes 36872 | tf_op jit(solution)/shard_map/ppermute | solution.py:404
  30.2 4.8 %copy-start = (f32[32,8,128]{2,1,0:T(8,128)S(1)}, f32[32,8,128]{2,1,0:T(8,128)}, u32[]{:S(2)}) copy-start(f32[32,8,128]{2,1,0:T(8,128)} %param.15) | copy-start | bytes 393220
  35.9 2.9 %collective-permute-start.9 = (f32[64,128]{1,0:T(8,128)S(1)}, f32[64,128]{1,0:T(8,128)S(1)}, u32[]{:S(2)}, u32[]{:S(2)}) collective-permute-start(f32[64,128]{1,0:T(8,128)S(1)} %get-tuple-element.50), channel_id=1, source_target_pairs={{0,4},{4,0},{8,12},{12,8},{16,20},{20,16},{24,28},{28,24},{32,36},... | collective-permute-start | bytes 98312 | tf_op jit(solution)/shard_map/ppermute | solution.py:404
  37.1 7.0 %collective-permute-start.11 = (f32[112,128]{1,0:T(8,128)S(1)}, f32[112,128]{1,0:T(8,128)S(1)}, u32[]{:S(2)}, u32[]{:S(2)}) collective-permute-start(f32[112,128]{1,0:T(8,128)S(1)} %shard_map.156), channel_id=1, source_target_pairs={{4,8},{8,4},{12,16},{16,12},{20,24},{24,20},{28,32},{32,28},{36,40... | collective-permute-start | bytes 172040 | tf_op jit(solution)/shard_map/ppermute | solution.py:404
  40.9 1.3 %collective-permute-start.10 = (f32[48,128]{1,0:T(8,128)S(1)}, f32[48,128]{1,0:T(8,128)S(1)}, u32[]{:S(2)}, u32[]{:S(2)}) collective-permute-start(f32[48,128]{1,0:T(8,128)S(1)} %get-tuple-element.51), channel_id=1, source_target_pairs={{0,4},{4,0},{8,12},{12,8},{16,20},{20,16},{24,28},{28,24},{32,36},... | collective-permute-start | bytes 73736 | tf_op jit(solution)/shard_map/ppermute | solution.py:404
  44.1 5.1 %collective-permute-start.12 = (f32[56,128]{1,0:T(8,128)S(1)}, f32[56,128]{1,0:T(8,128)S(1)}, u32[]{:S(2)}, u32[]{:S(2)}) collective-permute-start(f32[56,128]{1,0:T(8,128)S(1)} %pad_maximum_fusion.2), channel_id=1, source_target_pairs={{0,1},{1,2},{2,3},{3,0},{4,5},{5,6},{6,7},{7,4},{8,9},{9,10},{10,1... | collective-permute-start | bytes 86024 | tf_op jit(solution)/shard_map/ppermute | solution.py:393
  45.8 3.9 %collective-permute-start.13 = (f32[56,128]{1,0:T(8,128)S(1)}, f32[56,128]{1,0:T(8,128)S(1)}, u32[]{:S(2)}, u32[]{:S(2)}) collective-permute-start(f32[56,128]{1,0:T(8,128)S(1)} %pad_maximum_fusion.3), channel_id=1, source_target_pairs={{1,0},{2,1},{3,2},{0,3},{5,4},{6,5},{7,6},{4,7},{9,8},{10,9},{11,1... | collective-permute-start | bytes 86024 | tf_op jit(solution)/shard_map/ppermute | solution.py:398
  54.2 4.9 %collective-permute-start.14 = (f32[24,128]{1,0:T(8,128)S(1)}, f32[24,128]{1,0:T(8,128)S(1)}, u32[]{:S(2)}, u32[]{:S(2)}) collective-permute-start(f32[24,128]{1,0:T(8,128)S(1)} %get-tuple-element.56), channel_id=1, source_target_pairs={{0,1},{1,2},{2,3},{3,0},{4,5},{5,6},{6,7},{7,4},{8,9},{9,10},{10,1... | collective-permute-start | bytes 36872 | tf_op jit(solution)/shard_map/ppermute | solution.py:393
  55.5 3.7 %collective-permute-start.15 = (f32[24,128]{1,0:T(8,128)S(1)}, f32[24,128]{1,0:T(8,128)S(1)}, u32[]{:S(2)}, u32[]{:S(2)}) collective-permute-start(f32[24,128]{1,0:T(8,128)S(1)} %get-tuple-element.58), channel_id=1, source_target_pairs={{1,0},{2,1},{3,2},{0,3},{5,4},{6,5},{7,6},{4,7},{9,8},{10,9},{11,1... | collective-permute-start | bytes 36872 | tf_op jit(solution)/shard_map/ppermute | solution.py:398
  59.2 1.8 %collective-permute-start.17 = (f32[24,128]{1,0:T(8,128)S(1)}, f32[24,128]{1,0:T(8,128)S(1)}, u32[]{:S(2)}, u32[]{:S(2)}) collective-permute-start(f32[24,128]{1,0:T(8,128)S(1)} %pad_maximum_fusion.7), channel_id=1, source_target_pairs={{0,4},{4,0},{8,12},{12,8},{16,20},{20,16},{24,28},{28,24},{32,36},... | collective-permute-start | bytes 36872 | tf_op jit(solution)/shard_map/ppermute | solution.py:404
  59.2 6.5 %collective-permute-start.16 = (f32[24,128]{1,0:T(8,128)S(1)}, f32[24,128]{1,0:T(8,128)S(1)}, u32[]{:S(2)}, u32[]{:S(2)}) collective-permute-start(f32[24,128]{1,0:T(8,128)S(1)} %pad_maximum_fusion.6), channel_id=1, source_target_pairs={{4,8},{8,4},{12,16},{16,12},{20,24},{24,20},{28,32},{32,28},{36,40... | collective-permute-start | bytes 36872 | tf_op jit(solution)/shard_map/ppermute | solution.py:404
  (8 other events, 8.1 us)

commit v7 on v5

--- a/solution.py
+++ b/solution.py
@@ -110,8 +110,9 @@
     cross[48:112, :] = cross_edge[...]
 
 
-def rest_kernel(row, col, weight, _, chip, here):
+def rest_kernel(row, col, weight, chip_edge, _, chip, here):
     gather_cells(row, col, weight, ((chip, x_places()[0]), (here, 1)))
+    chip[48:112, :] = chip_edge[...]
 
 
 def collar_kernel(stem, entry, demand, second, need):
@@ -126,7 +127,7 @@
 
 
 def terms_kernel(
-    head, cond, head_old, alpha_dry, wet, reversal, chip_edges, cross, side_minus, side_plus,
+    head, cond, head_old, alpha_dry, wet, reversal, chip, cross, side_minus, side_plus,
     back_minus, back_here, back_plus, back_chip, row, col,
     numerator, denominator, halo,
 ):
@@ -134,8 +135,8 @@
     pieces += [(back_chip, dy * 8, x_places()[0] * 3 + dy) for dy in range(3)]
     sink = SINK_GAIN * sink_of(pieces, row, col)
     even = x_places()[0] == 2
-    from_plus = jnp.where(even, chip_edges[...], cross[48:112, :])
-    from_minus = jnp.where(even, cross[48:112, :], chip_edges[...])
+    from_plus = jnp.where(even, chip[48:112, :], cross[48:112, :])
+    from_minus = jnp.where(even, cross[48:112, :], chip[48:112, :])
     halo[...] = jnp.zeros_like(halo)
     turned = []
     for i in range(4):
@@ -385,13 +386,13 @@
 
 def spread(row, col, chip_edge, cross, edge_minus, edge_plus, weight):
     from_cross = swap(cross, "gx", 1)
-    chip_edges = swap(chip_edge, "gx", 0)
-    chip, here = call(rest_kernel, [SLOT] * 2, micros=2)(row, col, weight, chip_edges)
+    gate = lax.ppermute(edge_minus, "gx", [(2, 3), (3, 2)])
+    chip, here = call(rest_kernel, [MESSAGE, SLOT], micros=2)(row, col, weight, chip_edge, gate)
     from_chip = swap(chip, "gx", 0)
     parts = (from_chip, here, from_cross)
     side_minus = up(jnp.concatenate([x[32:48] for x in parts] + [edge_plus], 0), "gy")
     side_plus = down(jnp.concatenate([x[0:16] for x in parts] + [edge_minus], 0), "gy")
-    return (*parts, side_minus, side_plus), chip_edges
+    return (*parts, side_minus, side_plus)
 
 
 def give_back(minus, here, plus):
@@ -435,7 +436,7 @@
         stem_link.reshape(1, BLOCKS), entry_seg.reshape(1, BLOCKS), demand.reshape(1, PLANTS)
     )
     for iteration in range(PICARD):
-        got, chip_edges = spread(row, col, *messages)
+        got = spread(row, col, *messages)
         *sums, collar = call(
             root_kernel,
             [((24, 128), F32)] * 3 + [((1, PLANTS), F32)],
@@ -448,7 +449,7 @@
             [((CELLS, LANES), F32)] * 2,
             [((128, 128), F32)],
         )(
-            head, cond, head_old, alpha, wet, reversal, chip_edges, got[2], got[3], got[4],
+            head, cond, head_old, alpha, wet, reversal, got[0], got[2], got[3], got[4],
             *near, from_chip, row, col,
         )
         if iteration < PICARD - 1:

time: 67 us -> 67.7 us (1.010)
    ppermute x0 -> x2, starting transfers between devices: none -> 1.5 us  [spread(): gate = lax.ppermute(edge_minus, 'gx', [(2, 3), (3, 2)])]
    ppermute x10 -> x8, starting transfers between devices: 10.2 us -> 9.3 us  [swap(): lax.ppermute(x, axis, [p for i, j in pairs for p in ((i, j), (j, i))])]
    ppermute x10 -> x8, waiting for transfers between devices: 12.1 us -> 12.1 us  [swap(): lax.ppermute(x, axis, [p for i, j in pairs for p in ((i, j), (j, i))])]
  transfers between devices with their start and end apart: 18 -> 18, of which waited for: 12 -> 11; matrix products, arithmetic and copies ran while one was open for 0% -> 0% of each run, Pallas kernels for 12% -> 12%
where the time goes in v7:
time: 67.7 us; the launch traced here: 67.5 us
  starting transfers between devices  24.8 us (37%)
  Pallas kernels  20.3 us (30%)
  waiting for transfers between devices  19.2 us (28%)
  other arithmetic  1.46 us (2%)
  between operations  0.94 us (1%)
  local copies, waits for them, and re-layouts  0.77 us (1%)
    ppermute x8, waiting for transfers between devices, swap(): lax.ppermute(x, axis, [p for i, j in pairs for p in ((i, j), (j, i))])  12.1 us
    ppermute x8, starting transfers between devices, swap(): lax.ppermute(x, axis, [p for i, j in pairs for p in ((i, j), (j, i))])  9.3 us
    pallas_call x2, Pallas kernels, on_device(): call(root_kernel, [((24, 128), F32)] * 3 + [((1, PLANTS), F32)], [((144,...  9.05 us
    ppermute x4, starting transfers between devices, down(): return lax.ppermute(x, axis, [((i + 1) % size, i) for i in range(size)])  7.26 us
    ppermute x4, starting transfers between devices, up(): return lax.ppermute(x, axis, [(i, (i + 1) % size) for i in range(size)])  6.7 us
    ppermute x4, waiting for transfers between devices, up(): return lax.ppermute(x, axis, [(i, (i + 1) % size) for i in range(size)])  6.13 us
    pallas_call x2, Pallas kernels, spread(): call(rest_kernel, [MESSAGE, SLOT], micros=2)  4.18 us
    pallas_call x2, Pallas kernels, on_device(): call(terms_kernel, [((CELLS, LANES), F32)] * 2, [((128, 128), F32)])  2.63 us
  transfers between devices with their start and end apart: 18, of which 11 were waited for; matrix products, arithmetic and copies ran while one was open for 0% of the time, Pallas kernels for 12%

profile of v7, /device:TPU:0, one launch (start us, length us, event | category | flops | bytes accessed | tf_op | source)
XLA Modules:
  0.0 67.5 jit_solution(4204993223956792823)
XLA Ops:
  3.8 4.8 %collective-permute-start.2 = (f32[112,128]{1,0:T(8,128)S(1)}, f32[112,128]{1,0:T(8,128)S(1)}, u32[]{:S(2)}, u32[]{:S(2)}) collective-permute-start(f32[112,128]{1,0:T(8,128)S(1)} %get-tuple-element.36), channel_id=1, source_target_pairs={{4,8},{8,4},{12,16},{16,12},{20,24},{24,20},{28,32},{32,28},{36,40... | collective-permute-start | bytes 172040 | tf_op jit(solution)/shard_map/ppermute | solution.py:384
  8.8 2.1 %shard_map.150 = (f32[112,128]{1,0:T(8,128)S(1)}, f32[48,128]{1,0:T(8,128)S(1)}) custom-call(s32[72,128]{1,0:T(8,128)S(1)} %bitcast.30, s32[72,128]{1,0:T(8,128)S(1)} %bitcast.38, bf16[256,512]{1,0:T(8,128)(2,1)S(1)} %get-tuple-element.31.weight, f32[64,128]{1,0:T(8,128)S(1)} %get-tuple-element.32.chip_edge, f32[8,128]{1,0:T(8,128)S(1)} %collective-permute-done._), custom_call_target="tpu_custom_call" | custom-call | flops 2000000000 | bytes 6000000 | tf_op jit(solution)/shard_map/pallas_call | solution.py:390
  12.2 1.9 %collective-permute-start.3 = (f32[56,128]{1,0:T(8,128)S(1)}, f32[56,128]{1,0:T(8,128)S(1)}, u32[]{:S(2)}, u32[]{:S(2)}) collective-permute-start(f32[56,128]{1,0:T(8,128)S(1)} %pad_maximum_fusion), channel_id=1, source_target_pairs={{0,1},{1,2},{2,3},{3,0},{4,5},{5,6},{6,7},{7,4},{8,9},{9,10},{10,1... | collective-permute-start | bytes 86024 | tf_op jit(solution)/shard_map/ppermute | solution.py:373
  14.2 2.2 %collective-permute-start.4 = (f32[56,128]{1,0:T(8,128)S(1)}, f32[56,128]{1,0:T(8,128)S(1)}, u32[]{:S(2)}, u32[]{:S(2)}) collective-permute-start(f32[56,128]{1,0:T(8,128)S(1)} %pad_maximum_fusion.1), channel_id=1, source_target_pairs={{1,0},{2,1},{3,2},{0,3},{5,4},{6,5},{7,6},{4,7},{9,8},{10,9},{11,1... | collective-permute-start | bytes 86024 | tf_op jit(solution)/shard_map/ppermute | solution.py:378
  18.2 4.5 %shard_map.152 = (f32[24,128]{1,0:T(8,128)S(1)}, f32[24,128]{1,0:T(8,128)S(1)}, f32[24,128]{1,0:T(8,128)S(1)}, f32[1,16]{1,0:T(1,128)}) custom-call(f32[112,128]{1,0:T(8,128)S(1)} %collective-permute-done.1.chip, f32[48,128]{1,0:T(8,128)S(1)} %get-tuple-element.35.here, f32[112,128]{1,0:T(8,128)S(1)} %collective-permute-done.2.cross, ...), custom_call_target="tpu_custom_call" | custom-call | flops 6000000000 | bytes 18000000 | tf_op jit(solution)/shard_map/pallas_call | solution.py:440
  22.7 1.8 %collective-permute-start.5 = (f32[24,128]{1,0:T(8,128)S(1)}, f32[24,128]{1,0:T(8,128)S(1)}, u32[]{:S(2)}, u32[]{:S(2)}) collective-permute-start(f32[24,128]{1,0:T(8,128)S(1)} %get-tuple-element.40), channel_id=1, source_target_pairs={{0,1},{1,2},{2,3},{3,0},{4,5},{5,6},{6,7},{7,4},{8,9},{9,10},{10,1... | collective-permute-start | bytes 36872 | tf_op jit(solution)/shard_map/ppermute | solution.py:373
  24.5 1.5 %collective-permute-start.6 = (f32[24,128]{1,0:T(8,128)S(1)}, f32[24,128]{1,0:T(8,128)S(1)}, u32[]{:S(2)}, u32[]{:S(2)}) collective-permute-start(f32[24,128]{1,0:T(8,128)S(1)} %get-tuple-element.42), channel_id=1, source_target_pairs={{1,0},{2,1},{3,2},{0,3},{5,4},{6,5},{7,6},{4,7},{9,8},{10,9},{11,1... | collective-permute-start | bytes 36872 | tf_op jit(solution)/shard_map/ppermute | solution.py:378
  26.0 1.7 %collective-permute-done.5.back_minus = f32[24,128]{1,0:T(8,128)S(1)} collective-permute-done((f32[24,128]{1,0:T(8,128)S(1)}, f32[24,128]{1,0:T(8,128)S(1)}, u32[]{:S(2)}, u32[]{:S(2)}) %collective-permute-start.5) | collective-permute-done | bytes 12320 | tf_op jit(solution)/shard_map/ppermute | solution.py:373
  28.2 1.3 %collective-permute-start.7 = (f32[24,128]{1,0:T(8,128)S(1)}, f32[24,128]{1,0:T(8,128)S(1)}, u32[]{:S(2)}, u32[]{:S(2)}) collective-permute-start(f32[24,128]{1,0:T(8,128)S(1)} %pad_maximum_fusion.4), channel_id=1, source_target_pairs={{4,8},{8,4},{12,16},{16,12},{20,24},{24,20},{28,32},{32,28},{36,40... | collective-permute-start | bytes 36872 | tf_op jit(solution)/shard_map/ppermute | solution.py:384
  29.6 1.3 %shard_map.153 = (f32[256,128]{1,0:T(8,128)S(1)}, f32[256,128]{1,0:T(8,128)S(1)}) custom-call(f32[256,128]{1,0:T(8,128)S(1)} %bitcast.18, f32[256,128]{1,0:T(8,128)S(1)} %multiply_multiply_fusion.cond, f32[256,128]{1,0:T(8,128)S(1)} %bitcast.19, f32[256,128]{1,0:T(8,128)S(1)} %bitcast.24, s32[256,128]{1,0:T(8,128)S(1)} %bitcast.21, f32[256,128]{1,0:T(8,128)S(1)} %bitcast.27, ...), custom_call_target="tpu_custom_call" | custom-call | flops 1000000000 | bytes 3000000 | tf_op jit(solution)/shard_map/pallas_call | solution.py:447
  30.9 3.8 %collective-permute-done.7.cross = f32[24,128]{1,0:T(8,128)S(1)} collective-permute-done((f32[24,128]{1,0:T(8,128)S(1)}, f32[24,128]{1,0:T(8,128)S(1)}, u32[]{:S(2)}, u32[]{:S(2)}) %collective-permute-start.7) | collective-permute-done | bytes 12320 | tf_op jit(solution)/shard_map/ppermute | solution.py:384
  37.6 1.3 %collective-permute-start.11 = (f32[112,128]{1,0:T(8,128)S(1)}, f32[112,128]{1,0:T(8,128)S(1)}, u32[]{:S(2)}, u32[]{:S(2)}) collective-permute-start(f32[112,128]{1,0:T(8,128)S(1)} %shard_map.156), channel_id=1, source_target_pairs={{4,8},{8,4},{12,16},{16,12},{20,24},{24,20},{28,32},{32,28},{36,40... | collective-permute-start | bytes 172040 | tf_op jit(solution)/shard_map/ppermute | solution.py:384
  38.9 2.1 %shard_map.155 = (f32[112,128]{1,0:T(8,128)S(1)}, f32[48,128]{1,0:T(8,128)S(1)}) custom-call(s32[72,128]{1,0:T(8,128)S(1)} %bitcast.34, s32[72,128]{1,0:T(8,128)S(1)} %bitcast.42, bf16[256,512]{1,0:T(8,128)(2,1)S(1)} %get-tuple-element.45.weight, f32[64,128]{1,0:T(8,128)S(1)} %get-tuple-element.46.chip_edge, f32[8,128]{1,0:T(8,128)S(1)} %collective-permute-done.9._), custom_call_target="tpu_custom_call" | custom-call | flops 2000000000 | bytes 6000000 | tf_op jit(solution)/shard_map/pallas_call | solution.py:390
  41.1 3.5 %collective-permute-done.11.cross = f32[112,128]{1,0:T(8,128)S(1)} collective-permute-done((f32[112,128]{1,0:T(8,128)S(1)}, f32[112,128]{1,0:T(8,128)S(1)}, u32[]{:S(2)}, u32[]{:S(2)}) %collective-permute-start.11) | collective-permute-done | bytes 57376 | tf_op jit(solution)/shard_map/ppermute | solution.py:384
  44.6 1.7 %collective-permute-start.12 = (f32[56,128]{1,0:T(8,128)S(1)}, f32[56,128]{1,0:T(8,128)S(1)}, u32[]{:S(2)}, u32[]{:S(2)}) collective-permute-start(f32[56,128]{1,0:T(8,128)S(1)} %pad_maximum_fusion.2), channel_id=1, source_target_pairs={{0,1},{1,2},{2,3},{3,0},{4,5},{5,6},{6,7},{7,4},{8,9},{9,10},{10,1... | collective-permute-start | bytes 86024 | tf_op jit(solution)/shard_map/ppermute | solution.py:373
  46.3 1.6 %collective-permute-start.13 = (f32[56,128]{1,0:T(8,128)S(1)}, f32[56,128]{1,0:T(8,128)S(1)}, u32[]{:S(2)}, u32[]{:S(2)}) collective-permute-start(f32[56,128]{1,0:T(8,128)S(1)} %pad_maximum_fusion.3), channel_id=1, source_target_pairs={{1,0},{2,1},{3,2},{0,3},{5,4},{6,5},{7,6},{4,7},{9,8},{10,9},{11,1... | collective-permute-start | bytes 86024 | tf_op jit(solution)/shard_map/ppermute | solution.py:378
  47.9 1.8 %collective-permute-done.12.side_minus = f32[56,128]{1,0:T(8,128)S(1)} collective-permute-done((f32[56,128]{1,0:T(8,128)S(1)}, f32[56,128]{1,0:T(8,128)S(1)}, u32[]{:S(2)}, u32[]{:S(2)}) %collective-permute-start.12) | collective-permute-done | bytes 28704 | tf_op jit(solution)/shard_map/ppermute | solution.py:373
  50.1 4.5 %shard_map.157 = (f32[24,128]{1,0:T(8,128)S(1)}, f32[24,128]{1,0:T(8,128)S(1)}, f32[24,128]{1,0:T(8,128)S(1)}, f32[1,16]{1,0:T(1,128)}) custom-call(f32[112,128]{1,0:T(8,128)S(1)} %collective-permute-done.10.chip, f32[48,128]{1,0:T(8,128)S(1)} %get-tuple-element.49.here, f32[112,128]{1,0:T(8,128)S(1)} %collective-permute-done.11.cross, ...), custom_call_target="tpu_custom_call" | custom-call | flops 6000000000 | bytes 18000000 | tf_op jit(solution)/shard_map/pallas_call | solution.py:440
  54.7 1.3 %collective-permute-start.14 = (f32[24,128]{1,0:T(8,128)S(1)}, f32[24,128]{1,0:T(8,128)S(1)}, u32[]{:S(2)}, u32[]{:S(2)}) collective-permute-start(f32[24,128]{1,0:T(8,128)S(1)} %get-tuple-element.52), channel_id=1, source_target_pairs={{0,1},{1,2},{2,3},{3,0},{4,5},{5,6},{6,7},{7,4},{8,9},{9,10},{10,1... | collective-permute-start | bytes 36872 | tf_op jit(solution)/shard_map/ppermute | solution.py:373
  56.0 1.9 %collective-permute-start.15 = (f32[24,128]{1,0:T(8,128)S(1)}, f32[24,128]{1,0:T(8,128)S(1)}, u32[]{:S(2)}, u32[]{:S(2)}) collective-permute-start(f32[24,128]{1,0:T(8,128)S(1)} %get-tuple-element.54), channel_id=1, source_target_pairs={{1,0},{2,1},{3,2},{0,3},{5,4},{6,5},{7,6},{4,7},{9,8},{10,9},{11,1... | collective-permute-start | bytes 36872 | tf_op jit(solution)/shard_map/ppermute | solution.py:378
  57.9 1.7 %collective-permute-done.14.back_minus = f32[24,128]{1,0:T(8,128)S(1)} collective-permute-done((f32[24,128]{1,0:T(8,128)S(1)}, f32[24,128]{1,0:T(8,128)S(1)}, u32[]{:S(2)}, u32[]{:S(2)}) %collective-permute-start.14) | collective-permute-done | bytes 12320 | tf_op jit(solution)/shard_map/ppermute | solution.py:373
  59.7 1.6 %collective-permute-start.16 = (f32[24,128]{1,0:T(8,128)S(1)}, f32[24,128]{1,0:T(8,128)S(1)}, u32[]{:S(2)}, u32[]{:S(2)}) collective-permute-start(f32[24,128]{1,0:T(8,128)S(1)} %pad_maximum_fusion.6), channel_id=1, source_target_pairs={{4,8},{8,4},{12,16},{16,12},{20,24},{24,20},{28,32},{32,28},{36,40... | collective-permute-start | bytes 36872 | tf_op jit(solution)/shard_map/ppermute | solution.py:384
  61.3 1.3 %shard_map.158 = (f32[256,128]{1,0:T(8,128)S(1)}, f32[256,128]{1,0:T(8,128)S(1)}) custom-call(f32[256,128]{1,0:T(8,128)S(1)} %get-tuple-element.55.head, f32[256,128]{1,0:T(8,128)S(1)} %get-tuple-element.56.cond, f32[256,128]{1,0:T(8,128)S(1)} %bitcast.20, f32[256,128]{1,0:T(8,128)S(1)} %bitcast.26, s32[256,128]{1,0:T(8,128)S(1)} %bitcast.23, ...), custom_call_target="tpu_custom_call" | custom-call | flops 1000000000 | bytes 3000000 | tf_op jit(solution)/shard_map/pallas_call | solution.py:447
  62.7 3.6 %collective-permute-done.16.cross = f32[24,128]{1,0:T(8,128)S(1)} collective-permute-done((f32[24,128]{1,0:T(8,128)S(1)}, f32[24,128]{1,0:T(8,128)S(1)}, u32[]{:S(2)}, u32[]{:S(2)}) %collective-permute-start.16) | collective-permute-done | bytes 12320 | tf_op jit(solution)/shard_map/ppermute | solution.py:384
  (73 shorter events, 11.6 us)
Async XLA Ops:
  2.0 6.7 %copy-start.12 = (s32[128,128]{1,0:T(8,128)S(1)}, s32[128,128]{1,0:T(8,128)}, u32[]{:S(2)}) copy-start(s32[128,128]{1,0:T(8,128)} %param.26) | copy-start | bytes 196612
  2.0 6.7 %copy-start.13 = (s32[128,128]{1,0:T(8,128)S(1)}, s32[128,128]{1,0:T(8,128)}, u32[]{:S(2)}) copy-start(s32[128,128]{1,0:T(8,128)} %param.25) | copy-start | bytes 196612
  3.2 5.6 %collective-permute-start = (f32[8,128]{1,0:T(8,128)S(1)}, f32[8,128]{1,0:T(8,128)S(1)}, u32[]{:S(2)}, u32[]{:S(2)}) collective-permute-start(f32[8,128]{1,0:T(8,128)S(1)} %get-tuple-element.33), channel_id=1, source_target_pairs={{8,12},{12,8},{9,13},{13,9},{10,14},{14,10},{11,15},{15,11}} | collective-permute-start | bytes 12296 | tf_op jit(solution)/shard_map/ppermute | solution.py:389
  3.8 7.2 %collective-permute-start.2 = (f32[112,128]{1,0:T(8,128)S(1)}, f32[112,128]{1,0:T(8,128)S(1)}, u32[]{:S(2)}, u32[]{:S(2)}) collective-permute-start(f32[112,128]{1,0:T(8,128)S(1)} %get-tuple-element.36), channel_id=1, source_target_pairs={{4,8},{8,4},{12,16},{16,12},{20,24},{24,20},{28,32},{32,28},{36,40... | collective-permute-start | bytes 172040 | tf_op jit(solution)/shard_map/ppermute | solution.py:384
  10.9 1.3 %collective-permute-start.1 = (f32[112,128]{1,0:T(8,128)S(1)}, f32[112,128]{1,0:T(8,128)S(1)}, u32[]{:S(2)}, u32[]{:S(2)}) collective-permute-start(f32[112,128]{1,0:T(8,128)S(1)} %get-tuple-element.34), channel_id=1, source_target_pairs={{0,4},{4,0},{8,12},{12,8},{16,20},{20,16},{24,28},{28,24},{32,36},... | collective-permute-start | bytes 172040 | tf_op jit(solution)/shard_map/ppermute | solution.py:384
  12.2 5.9 %collective-permute-start.3 = (f32[56,128]{1,0:T(8,128)S(1)}, f32[56,128]{1,0:T(8,128)S(1)}, u32[]{:S(2)}, u32[]{:S(2)}) collective-permute-start(f32[56,128]{1,0:T(8,128)S(1)} %pad_maximum_fusion), channel_id=1, source_target_pairs={{0,1},{1,2},{2,3},{3,0},{4,5},{5,6},{6,7},{7,4},{8,9},{9,10},{10,1... | collective-permute-start | bytes 86024 | tf_op jit(solution)/shard_map/ppermute | solution.py:373
  14.2 4.0 %collective-permute-start.4 = (f32[56,128]{1,0:T(8,128)S(1)}, f32[56,128]{1,0:T(8,128)S(1)}, u32[]{:S(2)}, u32[]{:S(2)}) collective-permute-start(f32[56,128]{1,0:T(8,128)S(1)} %pad_maximum_fusion.1), channel_id=1, source_target_pairs={{1,0},{2,1},{3,2},{0,3},{5,4},{6,5},{7,6},{4,7},{9,8},{10,9},{11,1... | collective-permute-start | bytes 86024 | tf_op jit(solution)/shard_map/ppermute | solution.py:378
  18.1 11.4 %copy-start.2 = (s32[32,8,128]{2,1,0:T(8,128)S(1)}, s32[32,8,128]{2,1,0:T(8,128)}, u32[]{:S(2)}) copy-start(s32[32,8,128]{2,1,0:T(8,128)} %param.17) | copy-start | bytes 393220
  18.1 11.4 %copy-start.3 = (f32[32,8,128]{2,1,0:T(8,128)S(1)}, f32[32,8,128]{2,1,0:T(8,128)}, u32[]{:S(2)}) copy-start(f32[32,8,128]{2,1,0:T(8,128)} %param.16) | copy-start | bytes 393220
  18.2 11.4 %copy-start.4 = (f32[32,8,128]{2,1,0:T(8,128)S(1)}, f32[32,8,128]{2,1,0:T(8,128)}, u32[]{:S(2)}) copy-start(f32[32,8,128]{2,1,0:T(8,128)} %param.18) | copy-start | bytes 393220
  22.7 5.0 %collective-permute-start.5 = (f32[24,128]{1,0:T(8,128)S(1)}, f32[24,128]{1,0:T(8,128)S(1)}, u32[]{:S(2)}, u32[]{:S(2)}) collective-permute-start(f32[24,128]{1,0:T(8,128)S(1)} %get-tuple-element.40), channel_id=1, source_target_pairs={{0,1},{1,2},{2,3},{3,0},{4,5},{5,6},{6,7},{7,4},{8,9},{9,10},{10,1... | collective-permute-start | bytes 36872 | tf_op jit(solution)/shard_map/ppermute | solution.py:373
  24.5 3.7 %collective-permute-start.6 = (f32[24,128]{1,0:T(8,128)S(1)}, f32[24,128]{1,0:T(8,128)S(1)}, u32[]{:S(2)}, u32[]{:S(2)}) collective-permute-start(f32[24,128]{1,0:T(8,128)S(1)} %get-tuple-element.42), channel_id=1, source_target_pairs={{1,0},{2,1},{3,2},{0,3},{5,4},{6,5},{7,6},{4,7},{9,8},{10,9},{11,1... | collective-permute-start | bytes 36872 | tf_op jit(solution)/shard_map/ppermute | solution.py:378
  28.2 1.4 %collective-permute-start.8 = (f32[24,128]{1,0:T(8,128)S(1)}, f32[24,128]{1,0:T(8,128)S(1)}, u32[]{:S(2)}, u32[]{:S(2)}) collective-permute-start(f32[24,128]{1,0:T(8,128)S(1)} %pad_maximum_fusion.5), channel_id=1, source_target_pairs={{0,4},{4,0},{8,12},{12,8},{16,20},{20,16},{24,28},{28,24},{32,36},... | collective-permute-start | bytes 36872 | tf_op jit(solution)/shard_map/ppermute | solution.py:384
  28.2 6.5 %collective-permute-start.7 = (f32[24,128]{1,0:T(8,128)S(1)}, f32[24,128]{1,0:T(8,128)S(1)}, u32[]{:S(2)}, u32[]{:S(2)}) collective-permute-start(f32[24,128]{1,0:T(8,128)S(1)} %pad_maximum_fusion.4), channel_id=1, source_target_pairs={{4,8},{8,4},{12,16},{16,12},{20,24},{24,20},{28,32},{32,28},{36,40... | collective-permute-start | bytes 36872 | tf_op jit(solution)/shard_map/ppermute | solution.py:384
  29.6 5.2 %copy-start = (f32[32,8,128]{2,1,0:T(8,128)S(1)}, f32[32,8,128]{2,1,0:T(8,128)}, u32[]{:S(2)}) copy-start(f32[32,8,128]{2,1,0:T(8,128)} %param.15) | copy-start | bytes 393220
  35.6 3.3 %collective-permute-start.9 = (f32[8,128]{1,0:T(8,128)S(1)}, f32[8,128]{1,0:T(8,128)S(1)}, u32[]{:S(2)}, u32[]{:S(2)}) collective-permute-start(f32[8,128]{1,0:T(8,128)S(1)} %get-tuple-element.47), channel_id=1, source_target_pairs={{8,12},{12,8},{9,13},{13,9},{10,14},{14,10},{11,15},{15,11}} | collective-permute-start | bytes 12296 | tf_op jit(solution)/shard_map/ppermute | solution.py:389
  37.6 7.0 %collective-permute-start.11 = (f32[112,128]{1,0:T(8,128)S(1)}, f32[112,128]{1,0:T(8,128)S(1)}, u32[]{:S(2)}, u32[]{:S(2)}) collective-permute-start(f32[112,128]{1,0:T(8,128)S(1)} %shard_map.156), channel_id=1, source_target_pairs={{4,8},{8,4},{12,16},{16,12},{20,24},{24,20},{28,32},{32,28},{36,40... | collective-permute-start | bytes 172040 | tf_op jit(solution)/shard_map/ppermute | solution.py:384
  41.0 3.6 %collective-permute-start.10 = (f32[112,128]{1,0:T(8,128)S(1)}, f32[112,128]{1,0:T(8,128)S(1)}, u32[]{:S(2)}, u32[]{:S(2)}) collective-permute-start(f32[112,128]{1,0:T(8,128)S(1)} %get-tuple-element.48), channel_id=1, source_target_pairs={{0,4},{4,0},{8,12},{12,8},{16,20},{20,16},{24,28},{28,24},{32,36},... | collective-permute-start | bytes 172040 | tf_op jit(solution)/shard_map/ppermute | solution.py:384
  44.6 5.2 %collective-permute-start.12 = (f32[56,128]{1,0:T(8,128)S(1)}, f32[56,128]{1,0:T(8,128)S(1)}, u32[]{:S(2)}, u32[]{:S(2)}) collective-permute-start(f32[56,128]{1,0:T(8,128)S(1)} %pad_maximum_fusion.2), channel_id=1, source_target_pairs={{0,1},{1,2},{2,3},{3,0},{4,5},{5,6},{6,7},{7,4},{8,9},{9,10},{10,1... | collective-permute-start | bytes 86024 | tf_op jit(solution)/shard_map/ppermute | solution.py:373
  46.3 3.9 %collective-permute-start.13 = (f32[56,128]{1,0:T(8,128)S(1)}, f32[56,128]{1,0:T(8,128)S(1)}, u32[]{:S(2)}, u32[]{:S(2)}) collective-permute-start(f32[56,128]{1,0:T(8,128)S(1)} %pad_maximum_fusion.3), channel_id=1, source_target_pairs={{1,0},{2,1},{3,2},{0,3},{5,4},{6,5},{7,6},{4,7},{9,8},{10,9},{11,1... | collective-permute-start | bytes 86024 | tf_op jit(solution)/shard_map/ppermute | solution.py:378
  54.7 4.9 %collective-permute-start.14 = (f32[24,128]{1,0:T(8,128)S(1)}, f32[24,128]{1,0:T(8,128)S(1)}, u32[]{:S(2)}, u32[]{:S(2)}) collective-permute-start(f32[24,128]{1,0:T(8,128)S(1)} %get-tuple-element.52), channel_id=1, source_target_pairs={{0,1},{1,2},{2,3},{3,0},{4,5},{5,6},{6,7},{7,4},{8,9},{9,10},{10,1... | collective-permute-start | bytes 36872 | tf_op jit(solution)/shard_map/ppermute | solution.py:373
  56.0 3.7 %collective-permute-start.15 = (f32[24,128]{1,0:T(8,128)S(1)}, f32[24,128]{1,0:T(8,128)S(1)}, u32[]{:S(2)}, u32[]{:S(2)}) collective-permute-start(f32[24,128]{1,0:T(8,128)S(1)} %get-tuple-element.54), channel_id=1, source_target_pairs={{1,0},{2,1},{3,2},{0,3},{5,4},{6,5},{7,6},{4,7},{9,8},{10,9},{11,1... | collective-permute-start | bytes 36872 | tf_op jit(solution)/shard_map/ppermute | solution.py:378
  59.7 1.7 %collective-permute-start.17 = (f32[24,128]{1,0:T(8,128)S(1)}, f32[24,128]{1,0:T(8,128)S(1)}, u32[]{:S(2)}, u32[]{:S(2)}) collective-permute-start(f32[24,128]{1,0:T(8,128)S(1)} %pad_maximum_fusion.7), channel_id=1, source_target_pairs={{0,4},{4,0},{8,12},{12,8},{16,20},{20,16},{24,28},{28,24},{32,36},... | collective-permute-start | bytes 36872 | tf_op jit(solution)/shard_map/ppermute | solution.py:384
  59.7 6.5 %collective-permute-start.16 = (f32[24,128]{1,0:T(8,128)S(1)}, f32[24,128]{1,0:T(8,128)S(1)}, u32[]{:S(2)}, u32[]{:S(2)}) collective-permute-start(f32[24,128]{1,0:T(8,128)S(1)} %pad_maximum_fusion.6), channel_id=1, source_target_pairs={{4,8},{8,4},{12,16},{16,12},{20,24},{24,20},{28,32},{32,28},{36,40... | collective-permute-start | bytes 36872 | tf_op jit(solution)/shard_map/ppermute | solution.py:384
  (8 other events, 8.1 us)

commit v8 on v6

--- a/solution.py
+++ b/solution.py
@@ -105,21 +105,21 @@
 
 
 def start_kernel(
-    head, cond, row, col, chip_edge, cross, edge_minus, edge_plus, weight, chip, here
+    head, cond, row, col, chip_edge, cross, edge_minus, edge_plus, weight, chip
 ):
     lay_cells(head, cond, weight, chip_edge, cross, edge_minus, edge_plus)
     gather_cells(row, col, weight, ((cross, x_places()[1]),))
 
     @pl.when(leads())
     def _():
-        gather_cells(row, col, weight, ((chip, x_places()[0]), (here, 1)))
-
-
-def first_rest_kernel(row, col, weight, _, chip_in, here_in, chip, here):
+        gather_cells(row, col, weight, ((chip, x_places()[0]),))
+
+
+def first_rest_kernel(row, col, weight, _, chip_in, chip, here):
     @pl.when(leads())
     def _():
         chip[...] = chip_in[...]
-        here[...] = here_in[...]
+        gather_cells(row, col, weight, ((here, 1),))
 
     @pl.when(jnp.logical_not(leads()))
     def _():
@@ -453,7 +453,7 @@
     row, col = (x.reshape(SLOTS, LANES) for x in (send_row, send_col))
     head_old = head
     cond = conduct(head, sat, alpha * (1.0 + wet.astype(F32)))
-    messages = call(start_kernel, [EDGE, MESSAGE] + SIDES + [SLOT] * 2, micros=2)(head, cond, row, col)
+    messages = call(start_kernel, [EDGE, MESSAGE] + SIDES + [SLOT], micros=2)(head, cond, row, col)
     collar_link, need = call(collar_kernel, [((BLOCKS, LANES), F32), ((1, LANES), F32)])(
         stem_link.reshape(1, BLOCKS), entry_seg.reshape(1, BLOCKS), demand.reshape(1, PLANTS)
     )

time: 67.2 us -> 66.2 us (0.985)
  waiting for transfers between devices: 20.6 us -> 17.8 us
  starting transfers between devices: 23 us -> 24.6 us
    ppermute x10, waiting for transfers between devices: 13.4 us -> 10.7 us  [swap(): lax.ppermute(x, axis, [p for i, j in pairs for p in ((i, j), (j, i))])]
    ppermute x10, starting transfers between devices: 8.98 us -> 10.6 us  [swap(): lax.ppermute(x, axis, [p for i, j in pairs for p in ((i, j), (j, i))])]
    pallas_call x2, Pallas kernels: 2.1 us -> 3.2 us  [spread(): call(first_rest_kernel if early else rest_kernel, [SLOT] * 2, micros=2)]
    pallas_call x1, Pallas kernels: 3.19 us -> 2.24 us  [on_device(): call(start_kernel, [EDGE, MESSAGE] + SIDES + [SLOT], micros=2)]
  transfers between devices with their start and end apart: 18 -> 18, of which waited for: 13 -> 13; matrix products, arithmetic and copies ran while one was open for 0% -> 0% of each run, Pallas kernels for 9% -> 11%
where the time goes in v8:
time: 66.2 us; the launch traced here: 66.1 us
  starting transfers between devices  24.6 us (37%)
  Pallas kernels  20.5 us (31%)
  waiting for transfers between devices  17.8 us (27%)
  other arithmetic  1.46 us (2%)
  between operations  0.92 us (1%)
  local copies, waits for them, and re-layouts  0.77 us (1%)
    ppermute x10, waiting for transfers between devices, swap(): lax.ppermute(x, axis, [p for i, j in pairs for p in ((i, j), (j, i))])  10.7 us
    ppermute x10, starting transfers between devices, swap(): lax.ppermute(x, axis, [p for i, j in pairs for p in ((i, j), (j, i))])  10.6 us
    pallas_call x2, Pallas kernels, on_device(): call(root_kernel, [((24, 128), F32)] * 3 + [((1, PLANTS), F32)], [((144,...  9.04 us
    ppermute x4, starting transfers between devices, down(): return lax.ppermute(x, axis, [((i + 1) % size, i) for i in range(size)])  7.27 us
    ppermute x4, starting transfers between devices, up(): return lax.ppermute(x, axis, [(i, (i + 1) % size) for i in range(size)])  6.73 us
    ppermute x4, waiting for transfers between devices, up(): return lax.ppermute(x, axis, [(i, (i + 1) % size) for i in range(size)])  6.13 us
    pallas_call x2, Pallas kernels, spread(): call(first_rest_kernel if early else rest_kernel, [SLOT] * 2, micros=2)  3.2 us
    pallas_call x2, Pallas kernels, on_device(): call(terms_kernel, [((CELLS, LANES), F32)] * 2, [((128, 128), F32)])  2.64 us
  transfers between devices with their start and end apart: 18, of which 13 were waited for; matrix products, arithmetic and copies ran while one was open for 0% of the time, Pallas kernels for 11%

profile of v8, /device:TPU:0, one launch (start us, length us, event | category | flops | bytes accessed | tf_op | source)
XLA Modules:
  0.0 66.1 jit_solution(8275213014365877218)
XLA Ops:
  0.7 1.3 %multiply_multiply_fusion.cond = f32[256,128]{1,0:T(8,128)S(1)} fusion(s32[32,8,128]{2,1,0:T(8,128)} %param.17, f32[32,8,128]{2,1,0:T(8,128)} %param.16, f32[32,8,128]{2,1,0:T(8,128)} %param.15, f32[32,8,128]{2,1,0:T(8,128)} %param.14), kind=kLoop, calls=%fused_computation | loop fusion | flops 491520 | bytes 655360 | tf_op jit(solution)/shard_map/mul | solution.py:29
  2.0 2.2 %shard_map.149 = (f32[64,128]{1,0:T(8,128)S(1)}, f32[112,128]{1,0:T(8,128)S(1)}, f32[8,128]{1,0:T(8,128)S(1)}, f32[8,128]{1,0:T(8,128)S(1)}, bf16[256,512]{1,0:T(8,128)(2,1)S(1)}, /*index=5*/f32[48,128]{1,0:T(8,128)S(1)}) custom-call(f32[256,128]{1,0:T(8,128)S(1)} %bitcast.17, f32[256,128]{1,0:T(8,128)S(1)} %multiply_multiply_fusion.cond, ...), custom_call_target="tpu_custom_call" | custom-call | flops 2000000000 | bytes 6000000 | tf_op jit(solution)/shard_map/pallas_call | solution.py:456
  4.4 4.3 %collective-permute-start.2 = (f32[112,128]{1,0:T(8,128)S(1)}, f32[112,128]{1,0:T(8,128)S(1)}, u32[]{:S(2)}, u32[]{:S(2)}) collective-permute-start(f32[112,128]{1,0:T(8,128)S(1)} %get-tuple-element.37), channel_id=1, source_target_pairs={{4,8},{8,4},{12,16},{16,12},{20,24},{24,20},{28,32},{32,28},{36,40... | collective-permute-start | bytes 172040 | tf_op jit(solution)/shard_map/ppermute | solution.py:404
  11.4 2.0 %collective-permute-start.3 = (f32[56,128]{1,0:T(8,128)S(1)}, f32[56,128]{1,0:T(8,128)S(1)}, u32[]{:S(2)}, u32[]{:S(2)}) collective-permute-start(f32[56,128]{1,0:T(8,128)S(1)} %pad_maximum_fusion), channel_id=1, source_target_pairs={{0,1},{1,2},{2,3},{3,0},{4,5},{5,6},{6,7},{7,4},{8,9},{9,10},{10,1... | collective-permute-start | bytes 86024 | tf_op jit(solution)/shard_map/ppermute | solution.py:393
  13.4 2.2 %collective-permute-start.4 = (f32[56,128]{1,0:T(8,128)S(1)}, f32[56,128]{1,0:T(8,128)S(1)}, u32[]{:S(2)}, u32[]{:S(2)}) collective-permute-start(f32[56,128]{1,0:T(8,128)S(1)} %pad_maximum_fusion.1), channel_id=1, source_target_pairs={{1,0},{2,1},{3,2},{0,3},{5,4},{6,5},{7,6},{4,7},{9,8},{10,9},{11,1... | collective-permute-start | bytes 86024 | tf_op jit(solution)/shard_map/ppermute | solution.py:398
  17.4 4.5 %shard_map.152 = (f32[24,128]{1,0:T(8,128)S(1)}, f32[24,128]{1,0:T(8,128)S(1)}, f32[24,128]{1,0:T(8,128)S(1)}, f32[1,16]{1,0:T(1,128)}) custom-call(f32[48,128]{1,0:T(8,128)S(1)} %collective-permute-done.1.chip, f32[48,128]{1,0:T(8,128)S(1)} %get-tuple-element.36.here, f32[112,128]{1,0:T(8,128)S(1)} %collective-permute-done.2.cross, ...), custom_call_target="tpu_custom_call" | custom-call | flops 6000000000 | bytes 18000000 | tf_op jit(solution)/shard_map/pallas_call | solution.py:462
  21.9 1.8 %collective-permute-start.5 = (f32[24,128]{1,0:T(8,128)S(1)}, f32[24,128]{1,0:T(8,128)S(1)}, u32[]{:S(2)}, u32[]{:S(2)}) collective-permute-start(f32[24,128]{1,0:T(8,128)S(1)} %get-tuple-element.42), channel_id=1, source_target_pairs={{0,1},{1,2},{2,3},{3,0},{4,5},{5,6},{6,7},{7,4},{8,9},{9,10},{10,1... | collective-permute-start | bytes 36872 | tf_op jit(solution)/shard_map/ppermute | solution.py:393
  23.7 1.5 %collective-permute-start.6 = (f32[24,128]{1,0:T(8,128)S(1)}, f32[24,128]{1,0:T(8,128)S(1)}, u32[]{:S(2)}, u32[]{:S(2)}) collective-permute-start(f32[24,128]{1,0:T(8,128)S(1)} %get-tuple-element.44), channel_id=1, source_target_pairs={{1,0},{2,1},{3,2},{0,3},{5,4},{6,5},{7,6},{4,7},{9,8},{10,9},{11,1... | collective-permute-start | bytes 36872 | tf_op jit(solution)/shard_map/ppermute | solution.py:398
  25.2 1.7 %collective-permute-done.5.back_minus = f32[24,128]{1,0:T(8,128)S(1)} collective-permute-done((f32[24,128]{1,0:T(8,128)S(1)}, f32[24,128]{1,0:T(8,128)S(1)}, u32[]{:S(2)}, u32[]{:S(2)}) %collective-permute-start.5) | collective-permute-done | bytes 12320 | tf_op jit(solution)/shard_map/ppermute | solution.py:393
  27.4 2.2 %collective-permute-start.7 = (f32[24,128]{1,0:T(8,128)S(1)}, f32[24,128]{1,0:T(8,128)S(1)}, u32[]{:S(2)}, u32[]{:S(2)}) collective-permute-start(f32[24,128]{1,0:T(8,128)S(1)} %pad_maximum_fusion.4), channel_id=1, source_target_pairs={{4,8},{8,4},{12,16},{16,12},{20,24},{24,20},{28,32},{32,28},{36,40... | collective-permute-start | bytes 36872 | tf_op jit(solution)/shard_map/ppermute | solution.py:404
  29.7 1.3 %shard_map.153 = (f32[256,128]{1,0:T(8,128)S(1)}, f32[256,128]{1,0:T(8,128)S(1)}) custom-call(f32[256,128]{1,0:T(8,128)S(1)} %bitcast.18, f32[256,128]{1,0:T(8,128)S(1)} %multiply_multiply_fusion.cond, f32[256,128]{1,0:T(8,128)S(1)} %bitcast.19, f32[256,128]{1,0:T(8,128)S(1)} %bitcast.24, s32[256,128]{1,0:T(8,128)S(1)} %bitcast.21, f32[256,128]{1,0:T(8,128)S(1)} %bitcast.27, ...), custom_call_target="tpu_custom_call" | custom-call | flops 1000000000 | bytes 3000000 | tf_op jit(solution)/shard_map/pallas_call | solution.py:469
  31.0 3.1 %collective-permute-done.7.cross = f32[24,128]{1,0:T(8,128)S(1)} collective-permute-done((f32[24,128]{1,0:T(8,128)S(1)}, f32[24,128]{1,0:T(8,128)S(1)}, u32[]{:S(2)}, u32[]{:S(2)}) %collective-permute-start.7) | collective-permute-done | bytes 12320 | tf_op jit(solution)/shard_map/ppermute | solution.py:404
  36.2 2.0 %collective-permute-start.11 = (f32[112,128]{1,0:T(8,128)S(1)}, f32[112,128]{1,0:T(8,128)S(1)}, u32[]{:S(2)}, u32[]{:S(2)}) collective-permute-start(f32[112,128]{1,0:T(8,128)S(1)} %shard_map.156), channel_id=1, source_target_pairs={{4,8},{8,4},{12,16},{16,12},{20,24},{24,20},{28,32},{32,28},{36,40... | collective-permute-start | bytes 172040 | tf_op jit(solution)/shard_map/ppermute | solution.py:404
  38.2 2.1 %shard_map.155 = (f32[48,128]{1,0:T(8,128)S(1)}, f32[48,128]{1,0:T(8,128)S(1)}) custom-call(s32[72,128]{1,0:T(8,128)S(1)} %bitcast.34, s32[72,128]{1,0:T(8,128)S(1)} %bitcast.42, bf16[256,512]{1,0:T(8,128)(2,1)S(1)} %get-tuple-element.47.weight, f32[64,128]{1,0:T(8,128)S(1)} %collective-permute-done.9._.chip_edges), custom_call_target="tpu_custom_call" | custom-call | flops 2000000000 | bytes 6000000 | tf_op jit(solution)/shard_map/pallas_call | solution.py:410
  41.6 1.6 %collective-permute-done.11.cross = f32[112,128]{1,0:T(8,128)S(1)} collective-permute-done((f32[112,128]{1,0:T(8,128)S(1)}, f32[112,128]{1,0:T(8,128)S(1)}, u32[]{:S(2)}, u32[]{:S(2)}) %collective-permute-start.11) | collective-permute-done | bytes 57376 | tf_op jit(solution)/shard_map/ppermute | solution.py:404
  43.2 1.6 %collective-permute-start.12 = (f32[56,128]{1,0:T(8,128)S(1)}, f32[56,128]{1,0:T(8,128)S(1)}, u32[]{:S(2)}, u32[]{:S(2)}) collective-permute-start(f32[56,128]{1,0:T(8,128)S(1)} %pad_maximum_fusion.2), channel_id=1, source_target_pairs={{0,1},{1,2},{2,3},{3,0},{4,5},{5,6},{6,7},{7,4},{8,9},{9,10},{10,1... | collective-permute-start | bytes 86024 | tf_op jit(solution)/shard_map/ppermute | solution.py:393
  44.8 1.6 %collective-permute-start.13 = (f32[56,128]{1,0:T(8,128)S(1)}, f32[56,128]{1,0:T(8,128)S(1)}, u32[]{:S(2)}, u32[]{:S(2)}) collective-permute-start(f32[56,128]{1,0:T(8,128)S(1)} %pad_maximum_fusion.3), channel_id=1, source_target_pairs={{1,0},{2,1},{3,2},{0,3},{5,4},{6,5},{7,6},{4,7},{9,8},{10,9},{11,1... | collective-permute-start | bytes 86024 | tf_op jit(solution)/shard_map/ppermute | solution.py:398
  46.4 1.8 %collective-permute-done.12.side_minus = f32[56,128]{1,0:T(8,128)S(1)} collective-permute-done((f32[56,128]{1,0:T(8,128)S(1)}, f32[56,128]{1,0:T(8,128)S(1)}, u32[]{:S(2)}, u32[]{:S(2)}) %collective-permute-start.12) | collective-permute-done | bytes 28704 | tf_op jit(solution)/shard_map/ppermute | solution.py:393
  48.7 4.5 %shard_map.157 = (f32[24,128]{1,0:T(8,128)S(1)}, f32[24,128]{1,0:T(8,128)S(1)}, f32[24,128]{1,0:T(8,128)S(1)}, f32[1,16]{1,0:T(1,128)}) custom-call(f32[48,128]{1,0:T(8,128)S(1)} %collective-permute-done.10.chip, f32[48,128]{1,0:T(8,128)S(1)} %get-tuple-element.50.here, f32[112,128]{1,0:T(8,128)S(1)} %collective-permute-done.11.cross, ...), custom_call_target="tpu_custom_call" | custom-call | flops 6000000000 | bytes 18000000 | tf_op jit(solution)/shard_map/pallas_call | solution.py:462
  54.5 2.0 %collective-permute-start.15 = (f32[24,128]{1,0:T(8,128)S(1)}, f32[24,128]{1,0:T(8,128)S(1)}, u32[]{:S(2)}, u32[]{:S(2)}) collective-permute-start(f32[24,128]{1,0:T(8,128)S(1)} %get-tuple-element.56), channel_id=1, source_target_pairs={{1,0},{2,1},{3,2},{0,3},{5,4},{6,5},{7,6},{4,7},{9,8},{10,9},{11,1... | collective-permute-start | bytes 36872 | tf_op jit(solution)/shard_map/ppermute | solution.py:398
  56.5 1.7 %collective-permute-done.14.back_minus = f32[24,128]{1,0:T(8,128)S(1)} collective-permute-done((f32[24,128]{1,0:T(8,128)S(1)}, f32[24,128]{1,0:T(8,128)S(1)}, u32[]{:S(2)}, u32[]{:S(2)}) %collective-permute-start.14) | collective-permute-done | bytes 12320 | tf_op jit(solution)/shard_map/ppermute | solution.py:393
  58.3 1.7 %collective-permute-start.16 = (f32[24,128]{1,0:T(8,128)S(1)}, f32[24,128]{1,0:T(8,128)S(1)}, u32[]{:S(2)}, u32[]{:S(2)}) collective-permute-start(f32[24,128]{1,0:T(8,128)S(1)} %pad_maximum_fusion.6), channel_id=1, source_target_pairs={{4,8},{8,4},{12,16},{16,12},{20,24},{24,20},{28,32},{32,28},{36,40... | collective-permute-start | bytes 36872 | tf_op jit(solution)/shard_map/ppermute | solution.py:404
  60.0 1.3 %shard_map.158 = (f32[256,128]{1,0:T(8,128)S(1)}, f32[256,128]{1,0:T(8,128)S(1)}) custom-call(f32[256,128]{1,0:T(8,128)S(1)} %get-tuple-element.57.head, f32[256,128]{1,0:T(8,128)S(1)} %get-tuple-element.58.cond, f32[256,128]{1,0:T(8,128)S(1)} %bitcast.20, f32[256,128]{1,0:T(8,128)S(1)} %bitcast.26, s32[256,128]{1,0:T(8,128)S(1)} %bitcast.23, ...), custom_call_target="tpu_custom_call" | custom-call | flops 1000000000 | bytes 3000000 | tf_op jit(solution)/shard_map/pallas_call | solution.py:469
  61.3 3.4 %collective-permute-done.16.cross = f32[24,128]{1,0:T(8,128)S(1)} collective-permute-done((f32[24,128]{1,0:T(8,128)S(1)}, f32[24,128]{1,0:T(8,128)S(1)}, u32[]{:S(2)}, u32[]{:S(2)}) %collective-permute-start.16) | collective-permute-done | bytes 12320 | tf_op jit(solution)/shard_map/ppermute | solution.py:404
  (73 shorter events, 11.5 us)
Async XLA Ops:
  2.0 6.7 %copy-start.12 = (s32[128,128]{1,0:T(8,128)S(1)}, s32[128,128]{1,0:T(8,128)}, u32[]{:S(2)}) copy-start(s32[128,128]{1,0:T(8,128)} %param.26) | copy-start | bytes 196612
  2.0 6.6 %copy-start.13 = (s32[128,128]{1,0:T(8,128)S(1)}, s32[128,128]{1,0:T(8,128)}, u32[]{:S(2)}) copy-start(s32[128,128]{1,0:T(8,128)} %param.25) | copy-start | bytes 196612
  4.3 4.5 %collective-permute-start = (f32[64,128]{1,0:T(8,128)S(1)}, f32[64,128]{1,0:T(8,128)S(1)}, u32[]{:S(2)}, u32[]{:S(2)}) collective-permute-start(f32[64,128]{1,0:T(8,128)S(1)} %get-tuple-element.33), channel_id=1, source_target_pairs={{0,4},{4,0},{8,12},{12,8},{16,20},{20,16},{24,28},{28,24},{32,36},... | collective-permute-start | bytes 98312 | tf_op jit(solution)/shard_map/ppermute | solution.py:404
  4.4 7.0 %collective-permute-start.2 = (f32[112,128]{1,0:T(8,128)S(1)}, f32[112,128]{1,0:T(8,128)S(1)}, u32[]{:S(2)}, u32[]{:S(2)}) collective-permute-start(f32[112,128]{1,0:T(8,128)S(1)} %get-tuple-element.37), channel_id=1, source_target_pairs={{4,8},{8,4},{12,16},{16,12},{20,24},{24,20},{28,32},{32,28},{36,40... | collective-permute-start | bytes 172040 | tf_op jit(solution)/shard_map/ppermute | solution.py:404
  9.9 1.3 %collective-permute-start.1 = (f32[48,128]{1,0:T(8,128)S(1)}, f32[48,128]{1,0:T(8,128)S(1)}, u32[]{:S(2)}, u32[]{:S(2)}) collective-permute-start(f32[48,128]{1,0:T(8,128)S(1)} %get-tuple-element.35), channel_id=1, source_target_pairs={{0,4},{4,0},{8,12},{12,8},{16,20},{20,16},{24,28},{28,24},{32,36},... | collective-permute-start | bytes 73736 | tf_op jit(solution)/shard_map/ppermute | solution.py:404
  11.4 6.0 %collective-permute-start.3 = (f32[56,128]{1,0:T(8,128)S(1)}, f32[56,128]{1,0:T(8,128)S(1)}, u32[]{:S(2)}, u32[]{:S(2)}) collective-permute-start(f32[56,128]{1,0:T(8,128)S(1)} %pad_maximum_fusion), channel_id=1, source_target_pairs={{0,1},{1,2},{2,3},{3,0},{4,5},{5,6},{6,7},{7,4},{8,9},{9,10},{10,1... | collective-permute-start | bytes 86024 | tf_op jit(solution)/shard_map/ppermute | solution.py:393
  13.4 4.0 %collective-permute-start.4 = (f32[56,128]{1,0:T(8,128)S(1)}, f32[56,128]{1,0:T(8,128)S(1)}, u32[]{:S(2)}, u32[]{:S(2)}) collective-permute-start(f32[56,128]{1,0:T(8,128)S(1)} %pad_maximum_fusion.1), channel_id=1, source_target_pairs={{1,0},{2,1},{3,2},{0,3},{5,4},{6,5},{7,6},{4,7},{9,8},{10,9},{11,1... | collective-permute-start | bytes 86024 | tf_op jit(solution)/shard_map/ppermute | solution.py:398
  17.3 12.3 %copy-start.2 = (s32[32,8,128]{2,1,0:T(8,128)S(1)}, s32[32,8,128]{2,1,0:T(8,128)}, u32[]{:S(2)}) copy-start(s32[32,8,128]{2,1,0:T(8,128)} %param.17) | copy-start | bytes 393220
  17.4 12.3 %copy-start.3 = (f32[32,8,128]{2,1,0:T(8,128)S(1)}, f32[32,8,128]{2,1,0:T(8,128)}, u32[]{:S(2)}) copy-start(f32[32,8,128]{2,1,0:T(8,128)} %param.16) | copy-start | bytes 393220
  17.4 12.3 %copy-start.4 = (f32[32,8,128]{2,1,0:T(8,128)S(1)}, f32[32,8,128]{2,1,0:T(8,128)}, u32[]{:S(2)}) copy-start(f32[32,8,128]{2,1,0:T(8,128)} %param.18) | copy-start | bytes 393220
  21.9 5.0 %collective-permute-start.5 = (f32[24,128]{1,0:T(8,128)S(1)}, f32[24,128]{1,0:T(8,128)S(1)}, u32[]{:S(2)}, u32[]{:S(2)}) collective-permute-start(f32[24,128]{1,0:T(8,128)S(1)} %get-tuple-element.42), channel_id=1, source_target_pairs={{0,1},{1,2},{2,3},{3,0},{4,5},{5,6},{6,7},{7,4},{8,9},{9,10},{10,1... | collective-permute-start | bytes 36872 | tf_op jit(solution)/shard_map/ppermute | solution.py:393
  23.7 3.7 %collective-permute-start.6 = (f32[24,128]{1,0:T(8,128)S(1)}, f32[24,128]{1,0:T(8,128)S(1)}, u32[]{:S(2)}, u32[]{:S(2)}) collective-permute-start(f32[24,128]{1,0:T(8,128)S(1)} %get-tuple-element.44), channel_id=1, source_target_pairs={{1,0},{2,1},{3,2},{0,3},{5,4},{6,5},{7,6},{4,7},{9,8},{10,9},{11,1... | collective-permute-start | bytes 36872 | tf_op jit(solution)/shard_map/ppermute | solution.py:398
  27.4 2.2 %collective-permute-start.8 = (f32[24,128]{1,0:T(8,128)S(1)}, f32[24,128]{1,0:T(8,128)S(1)}, u32[]{:S(2)}, u32[]{:S(2)}) collective-permute-start(f32[24,128]{1,0:T(8,128)S(1)} %pad_maximum_fusion.5), channel_id=1, source_target_pairs={{0,4},{4,0},{8,12},{12,8},{16,20},{20,16},{24,28},{28,24},{32,36},... | collective-permute-start | bytes 36872 | tf_op jit(solution)/shard_map/ppermute | solution.py:404
  27.4 6.7 %collective-permute-start.7 = (f32[24,128]{1,0:T(8,128)S(1)}, f32[24,128]{1,0:T(8,128)S(1)}, u32[]{:S(2)}, u32[]{:S(2)}) collective-permute-start(f32[24,128]{1,0:T(8,128)S(1)} %pad_maximum_fusion.4), channel_id=1, source_target_pairs={{4,8},{8,4},{12,16},{16,12},{20,24},{24,20},{28,32},{32,28},{36,40... | collective-permute-start | bytes 36872 | tf_op jit(solution)/shard_map/ppermute | solution.py:404
  29.7 4.5 %copy-start = (f32[32,8,128]{2,1,0:T(8,128)S(1)}, f32[32,8,128]{2,1,0:T(8,128)}, u32[]{:S(2)}) copy-start(f32[32,8,128]{2,1,0:T(8,128)} %param.15) | copy-start | bytes 393220
  35.0 3.3 %collective-permute-start.9 = (f32[64,128]{1,0:T(8,128)S(1)}, f32[64,128]{1,0:T(8,128)S(1)}, u32[]{:S(2)}, u32[]{:S(2)}) collective-permute-start(f32[64,128]{1,0:T(8,128)S(1)} %get-tuple-element.48), channel_id=1, source_target_pairs={{0,4},{4,0},{8,12},{12,8},{16,20},{20,16},{24,28},{28,24},{32,36},... | collective-permute-start | bytes 98312 | tf_op jit(solution)/shard_map/ppermute | solution.py:404
  36.2 7.0 %collective-permute-start.11 = (f32[112,128]{1,0:T(8,128)S(1)}, f32[112,128]{1,0:T(8,128)S(1)}, u32[]{:S(2)}, u32[]{:S(2)}) collective-permute-start(f32[112,128]{1,0:T(8,128)S(1)} %shard_map.156), channel_id=1, source_target_pairs={{4,8},{8,4},{12,16},{16,12},{20,24},{24,20},{28,32},{32,28},{36,40... | collective-permute-start | bytes 172040 | tf_op jit(solution)/shard_map/ppermute | solution.py:404
  40.3 1.3 %collective-permute-start.10 = (f32[48,128]{1,0:T(8,128)S(1)}, f32[48,128]{1,0:T(8,128)S(1)}, u32[]{:S(2)}, u32[]{:S(2)}) collective-permute-start(f32[48,128]{1,0:T(8,128)S(1)} %get-tuple-element.49), channel_id=1, source_target_pairs={{0,4},{4,0},{8,12},{12,8},{16,20},{20,16},{24,28},{28,24},{32,36},... | collective-permute-start | bytes 73736 | tf_op jit(solution)/shard_map/ppermute | solution.py:404
  43.2 5.1 %collective-permute-start.12 = (f32[56,128]{1,0:T(8,128)S(1)}, f32[56,128]{1,0:T(8,128)S(1)}, u32[]{:S(2)}, u32[]{:S(2)}) collective-permute-start(f32[56,128]{1,0:T(8,128)S(1)} %pad_maximum_fusion.2), channel_id=1, source_target_pairs={{0,1},{1,2},{2,3},{3,0},{4,5},{5,6},{6,7},{7,4},{8,9},{9,10},{10,1... | collective-permute-start | bytes 86024 | tf_op jit(solution)/shard_map/ppermute | solution.py:393
  44.8 3.9 %collective-permute-start.13 = (f32[56,128]{1,0:T(8,128)S(1)}, f32[56,128]{1,0:T(8,128)S(1)}, u32[]{:S(2)}, u32[]{:S(2)}) collective-permute-start(f32[56,128]{1,0:T(8,128)S(1)} %pad_maximum_fusion.3), channel_id=1, source_target_pairs={{1,0},{2,1},{3,2},{0,3},{5,4},{6,5},{7,6},{4,7},{9,8},{10,9},{11,1... | collective-permute-start | bytes 86024 | tf_op jit(solution)/shard_map/ppermute | solution.py:398
  53.2 4.9 %collective-permute-start.14 = (f32[24,128]{1,0:T(8,128)S(1)}, f32[24,128]{1,0:T(8,128)S(1)}, u32[]{:S(2)}, u32[]{:S(2)}) collective-permute-start(f32[24,128]{1,0:T(8,128)S(1)} %get-tuple-element.54), channel_id=1, source_target_pairs={{0,1},{1,2},{2,3},{3,0},{4,5},{5,6},{6,7},{7,4},{8,9},{9,10},{10,1... | collective-permute-start | bytes 36872 | tf_op jit(solution)/shard_map/ppermute | solution.py:393
  54.5 3.7 %collective-permute-start.15 = (f32[24,128]{1,0:T(8,128)S(1)}, f32[24,128]{1,0:T(8,128)S(1)}, u32[]{:S(2)}, u32[]{:S(2)}) collective-permute-start(f32[24,128]{1,0:T(8,128)S(1)} %get-tuple-element.56), channel_id=1, source_target_pairs={{1,0},{2,1},{3,2},{0,3},{5,4},{6,5},{7,6},{4,7},{9,8},{10,9},{11,1... | collective-permute-start | bytes 36872 | tf_op jit(solution)/shard_map/ppermute | solution.py:398
  58.2 1.8 %collective-permute-start.17 = (f32[24,128]{1,0:T(8,128)S(1)}, f32[24,128]{1,0:T(8,128)S(1)}, u32[]{:S(2)}, u32[]{:S(2)}) collective-permute-start(f32[24,128]{1,0:T(8,128)S(1)} %pad_maximum_fusion.7), channel_id=1, source_target_pairs={{0,4},{4,0},{8,12},{12,8},{16,20},{20,16},{24,28},{28,24},{32,36},... | collective-permute-start | bytes 36872 | tf_op jit(solution)/shard_map/ppermute | solution.py:404
  58.3 6.5 %collective-permute-start.16 = (f32[24,128]{1,0:T(8,128)S(1)}, f32[24,128]{1,0:T(8,128)S(1)}, u32[]{:S(2)}, u32[]{:S(2)}) collective-permute-start(f32[24,128]{1,0:T(8,128)S(1)} %pad_maximum_fusion.6), channel_id=1, source_target_pairs={{4,8},{8,4},{12,16},{16,12},{20,24},{24,20},{28,32},{32,28},{36,40... | collective-permute-start | bytes 36872 | tf_op jit(solution)/shard_map/ppermute | solution.py:404
  (8 other events, 8.1 us)

commit v9 on v8

--- a/solution.py
+++ b/solution.py
@@ -20,6 +20,12 @@
 def split(x):
     hi = x.astype(BF16)
     return (hi, (x - hi.astype(F32)).astype(BF16))
+
+
+def inverted(x):
+    near = pltpu.reciprocal(x, approx=True)
+    near = near * (2.0 - x * near)
+    return near * (2.0 - x * near)
 
 
 def conduct(head, sat_conduct, alpha):
@@ -265,7 +271,7 @@
         lower, upper = (-left, -right)
         for step in range(7):
             stride = 2**step
-            inverse = 1.0 / diagonal
+            inverse = inverted(diagonal)
             low = -lower * pltpu.roll(inverse, stride, 1)
             high = -upper * pltpu.roll(inverse, 128 - stride, 1)
             first, second = (
@@ -276,7 +282,7 @@
             if step < 6:
                 lower = low * pltpu.roll(lower, stride, 1)
                 upper = high * pltpu.roll(upper, 128 - stride, 1)
-        inverse = 1.0 / diagonal
+        inverse = inverted(diagonal)
         free, collar = (first * inverse, second * inverse)
 
         def per_plant(x):

time: 66.2 us -> 66.3 us (level)
  no operation moved by 1% of the time
where the time goes in v9:
time: 66.3 us; the launch traced here: 66.1 us
  starting transfers between devices  24.6 us (37%)
  Pallas kernels  20.5 us (31%)
  waiting for transfers between devices  17.9 us (27%)
  other arithmetic  1.46 us (2%)
  between operations  0.92 us (1%)
  local copies, waits for them, and re-layouts  0.77 us (1%)
    ppermute x10, waiting for transfers between devices, swap(): lax.ppermute(x, axis, [p for i, j in pairs for p in ((i, j), (j, i))])  10.7 us
    ppermute x10, starting transfers between devices, swap(): lax.ppermute(x, axis, [p for i, j in pairs for p in ((i, j), (j, i))])  10.6 us
    pallas_call x2, Pallas kernels, on_device(): call(root_kernel, [((24, 128), F32)] * 3 + [((1, PLANTS), F32)], [((144,...  9.08 us
    ppermute x4, starting transfers between devices, down(): return lax.ppermute(x, axis, [((i + 1) % size, i) for i in range(size)])  7.26 us
    ppermute x4, starting transfers between devices, up(): return lax.ppermute(x, axis, [(i, (i + 1) % size) for i in range(size)])  6.73 us
    ppermute x4, waiting for transfers between devices, up(): return lax.ppermute(x, axis, [(i, (i + 1) % size) for i in range(size)])  6.13 us
    pallas_call x2, Pallas kernels, spread(): call(first_rest_kernel if early else rest_kernel, [SLOT] * 2, micros=2)  3.21 us
    pallas_call x2, Pallas kernels, on_device(): call(terms_kernel, [((CELLS, LANES), F32)] * 2, [((128, 128), F32)])  2.64 us
  transfers between devices with their start and end apart: 18, of which 13 were waited for; matrix products, arithmetic and copies ran while one was open for 0% of the time, Pallas kernels for 11%

profile of v9, /device:TPU:0, one launch (start us, length us, event | category | flops | bytes accessed | tf_op | source)
XLA Modules:
  0.0 66.1 jit_solution(7580836693016246089)
XLA Ops:
  2.0 2.2 %shard_map.149 = (f32[64,128]{1,0:T(8,128)S(1)}, f32[112,128]{1,0:T(8,128)S(1)}, f32[8,128]{1,0:T(8,128)S(1)}, f32[8,128]{1,0:T(8,128)S(1)}, bf16[256,512]{1,0:T(8,128)(2,1)S(1)}, /*index=5*/f32[48,128]{1,0:T(8,128)S(1)}) custom-call(f32[256,128]{1,0:T(8,128)S(1)} %bitcast.17, f32[256,128]{1,0:T(8,128)S(1)} %multiply_multiply_fusion.cond, ...), custom_call_target="tpu_custom_call" | custom-call | flops 2000000000 | bytes 6000000 | tf_op jit(solution)/shard_map/pallas_call | solution.py:462
  4.4 4.3 %collective-permute-start.2 = (f32[112,128]{1,0:T(8,128)S(1)}, f32[112,128]{1,0:T(8,128)S(1)}, u32[]{:S(2)}, u32[]{:S(2)}) collective-permute-start(f32[112,128]{1,0:T(8,128)S(1)} %get-tuple-element.37), channel_id=1, source_target_pairs={{4,8},{8,4},{12,16},{16,12},{20,24},{24,20},{28,32},{32,28},{36,40... | collective-permute-start | bytes 172040 | tf_op jit(solution)/shard_map/ppermute | solution.py:410
  11.4 2.0 %collective-permute-start.3 = (f32[56,128]{1,0:T(8,128)S(1)}, f32[56,128]{1,0:T(8,128)S(1)}, u32[]{:S(2)}, u32[]{:S(2)}) collective-permute-start(f32[56,128]{1,0:T(8,128)S(1)} %pad_maximum_fusion), channel_id=1, source_target_pairs={{0,1},{1,2},{2,3},{3,0},{4,5},{5,6},{6,7},{7,4},{8,9},{9,10},{10,1... | collective-permute-start | bytes 86024 | tf_op jit(solution)/shard_map/ppermute | solution.py:399
  13.4 2.2 %collective-permute-start.4 = (f32[56,128]{1,0:T(8,128)S(1)}, f32[56,128]{1,0:T(8,128)S(1)}, u32[]{:S(2)}, u32[]{:S(2)}) collective-permute-start(f32[56,128]{1,0:T(8,128)S(1)} %pad_maximum_fusion.1), channel_id=1, source_target_pairs={{1,0},{2,1},{3,2},{0,3},{5,4},{6,5},{7,6},{4,7},{9,8},{10,9},{11,1... | collective-permute-start | bytes 86024 | tf_op jit(solution)/shard_map/ppermute | solution.py:404
  17.4 4.5 %shard_map.152 = (f32[24,128]{1,0:T(8,128)S(1)}, f32[24,128]{1,0:T(8,128)S(1)}, f32[24,128]{1,0:T(8,128)S(1)}, f32[1,16]{1,0:T(1,128)}) custom-call(f32[48,128]{1,0:T(8,128)S(1)} %collective-permute-done.1.chip, f32[48,128]{1,0:T(8,128)S(1)} %get-tuple-element.36.here, f32[112,128]{1,0:T(8,128)S(1)} %collective-permute-done.2.cross, ...), custom_call_target="tpu_custom_call" | custom-call | flops 6000000000 | bytes 18000000 | tf_op jit(solution)/shard_map/pallas_call | solution.py:468
  21.9 1.8 %collective-permute-start.5 = (f32[24,128]{1,0:T(8,128)S(1)}, f32[24,128]{1,0:T(8,128)S(1)}, u32[]{:S(2)}, u32[]{:S(2)}) collective-permute-start(f32[24,128]{1,0:T(8,128)S(1)} %get-tuple-element.42), channel_id=1, source_target_pairs={{0,1},{1,2},{2,3},{3,0},{4,5},{5,6},{6,7},{7,4},{8,9},{9,10},{10,1... | collective-permute-start | bytes 36872 | tf_op jit(solution)/shard_map/ppermute | solution.py:399
  23.7 1.5 %collective-permute-start.6 = (f32[24,128]{1,0:T(8,128)S(1)}, f32[24,128]{1,0:T(8,128)S(1)}, u32[]{:S(2)}, u32[]{:S(2)}) collective-permute-start(f32[24,128]{1,0:T(8,128)S(1)} %get-tuple-element.44), channel_id=1, source_target_pairs={{1,0},{2,1},{3,2},{0,3},{5,4},{6,5},{7,6},{4,7},{9,8},{10,9},{11,1... | collective-permute-start | bytes 36872 | tf_op jit(solution)/shard_map/ppermute | solution.py:404
  25.2 1.7 %collective-permute-done.5.back_minus = f32[24,128]{1,0:T(8,128)S(1)} collective-permute-done((f32[24,128]{1,0:T(8,128)S(1)}, f32[24,128]{1,0:T(8,128)S(1)}, u32[]{:S(2)}, u32[]{:S(2)}) %collective-permute-start.5) | collective-permute-done | bytes 12320 | tf_op jit(solution)/shard_map/ppermute | solution.py:399
  27.5 2.2 %collective-permute-start.7 = (f32[24,128]{1,0:T(8,128)S(1)}, f32[24,128]{1,0:T(8,128)S(1)}, u32[]{:S(2)}, u32[]{:S(2)}) collective-permute-start(f32[24,128]{1,0:T(8,128)S(1)} %pad_maximum_fusion.4), channel_id=1, source_target_pairs={{4,8},{8,4},{12,16},{16,12},{20,24},{24,20},{28,32},{32,28},{36,40... | collective-permute-start | bytes 36872 | tf_op jit(solution)/shard_map/ppermute | solution.py:410
  29.7 1.3 %shard_map.153 = (f32[256,128]{1,0:T(8,128)S(1)}, f32[256,128]{1,0:T(8,128)S(1)}) custom-call(f32[256,128]{1,0:T(8,128)S(1)} %bitcast.18, f32[256,128]{1,0:T(8,128)S(1)} %multiply_multiply_fusion.cond, f32[256,128]{1,0:T(8,128)S(1)} %bitcast.19, f32[256,128]{1,0:T(8,128)S(1)} %bitcast.24, s32[256,128]{1,0:T(8,128)S(1)} %bitcast.21, f32[256,128]{1,0:T(8,128)S(1)} %bitcast.27, ...), custom_call_target="tpu_custom_call" | custom-call | flops 1000000000 | bytes 3000000 | tf_op jit(solution)/shard_map/pallas_call | solution.py:475
  31.0 3.1 %collective-permute-done.7.cross = f32[24,128]{1,0:T(8,128)S(1)} collective-permute-done((f32[24,128]{1,0:T(8,128)S(1)}, f32[24,128]{1,0:T(8,128)S(1)}, u32[]{:S(2)}, u32[]{:S(2)}) %collective-permute-start.7) | collective-permute-done | bytes 12320 | tf_op jit(solution)/shard_map/ppermute | solution.py:410
  36.2 2.0 %collective-permute-start.11 = (f32[112,128]{1,0:T(8,128)S(1)}, f32[112,128]{1,0:T(8,128)S(1)}, u32[]{:S(2)}, u32[]{:S(2)}) collective-permute-start(f32[112,128]{1,0:T(8,128)S(1)} %shard_map.156), channel_id=1, source_target_pairs={{4,8},{8,4},{12,16},{16,12},{20,24},{24,20},{28,32},{32,28},{36,40... | collective-permute-start | bytes 172040 | tf_op jit(solution)/shard_map/ppermute | solution.py:410
  38.2 2.1 %shard_map.155 = (f32[48,128]{1,0:T(8,128)S(1)}, f32[48,128]{1,0:T(8,128)S(1)}) custom-call(s32[72,128]{1,0:T(8,128)S(1)} %bitcast.34, s32[72,128]{1,0:T(8,128)S(1)} %bitcast.42, bf16[256,512]{1,0:T(8,128)(2,1)S(1)} %get-tuple-element.47.weight, f32[64,128]{1,0:T(8,128)S(1)} %collective-permute-done.9._.chip_edges), custom_call_target="tpu_custom_call" | custom-call | flops 2000000000 | bytes 6000000 | tf_op jit(solution)/shard_map/pallas_call | solution.py:416
  41.6 1.6 %collective-permute-done.11.cross = f32[112,128]{1,0:T(8,128)S(1)} collective-permute-done((f32[112,128]{1,0:T(8,128)S(1)}, f32[112,128]{1,0:T(8,128)S(1)}, u32[]{:S(2)}, u32[]{:S(2)}) %collective-permute-start.11) | collective-permute-done | bytes 57376 | tf_op jit(solution)/shard_map/ppermute | solution.py:410
  43.2 1.6 %collective-permute-start.12 = (f32[56,128]{1,0:T(8,128)S(1)}, f32[56,128]{1,0:T(8,128)S(1)}, u32[]{:S(2)}, u32[]{:S(2)}) collective-permute-start(f32[56,128]{1,0:T(8,128)S(1)} %pad_maximum_fusion.2), channel_id=1, source_target_pairs={{0,1},{1,2},{2,3},{3,0},{4,5},{5,6},{6,7},{7,4},{8,9},{9,10},{10,1... | collective-permute-start | bytes 86024 | tf_op jit(solution)/shard_map/ppermute | solution.py:399
  44.9 1.6 %collective-permute-start.13 = (f32[56,128]{1,0:T(8,128)S(1)}, f32[56,128]{1,0:T(8,128)S(1)}, u32[]{:S(2)}, u32[]{:S(2)}) collective-permute-start(f32[56,128]{1,0:T(8,128)S(1)} %pad_maximum_fusion.3), channel_id=1, source_target_pairs={{1,0},{2,1},{3,2},{0,3},{5,4},{6,5},{7,6},{4,7},{9,8},{10,9},{11,1... | collective-permute-start | bytes 86024 | tf_op jit(solution)/shard_map/ppermute | solution.py:404
  46.5 1.8 %collective-permute-done.12.side_minus = f32[56,128]{1,0:T(8,128)S(1)} collective-permute-done((f32[56,128]{1,0:T(8,128)S(1)}, f32[56,128]{1,0:T(8,128)S(1)}, u32[]{:S(2)}, u32[]{:S(2)}) %collective-permute-start.12) | collective-permute-done | bytes 28704 | tf_op jit(solution)/shard_map/ppermute | solution.py:399
  48.7 4.5 %shard_map.157 = (f32[24,128]{1,0:T(8,128)S(1)}, f32[24,128]{1,0:T(8,128)S(1)}, f32[24,128]{1,0:T(8,128)S(1)}, f32[1,16]{1,0:T(1,128)}) custom-call(f32[48,128]{1,0:T(8,128)S(1)} %collective-permute-done.10.chip, f32[48,128]{1,0:T(8,128)S(1)} %get-tuple-element.50.here, f32[112,128]{1,0:T(8,128)S(1)} %collective-permute-done.11.cross, ...), custom_call_target="tpu_custom_call" | custom-call | flops 6000000000 | bytes 18000000 | tf_op jit(solution)/shard_map/pallas_call | solution.py:468
  53.3 1.3 %collective-permute-start.14 = (f32[24,128]{1,0:T(8,128)S(1)}, f32[24,128]{1,0:T(8,128)S(1)}, u32[]{:S(2)}, u32[]{:S(2)}) collective-permute-start(f32[24,128]{1,0:T(8,128)S(1)} %get-tuple-element.54), channel_id=1, source_target_pairs={{0,1},{1,2},{2,3},{3,0},{4,5},{5,6},{6,7},{7,4},{8,9},{9,10},{10,1... | collective-permute-start | bytes 36872 | tf_op jit(solution)/shard_map/ppermute | solution.py:399
  54.6 1.9 %collective-permute-start.15 = (f32[24,128]{1,0:T(8,128)S(1)}, f32[24,128]{1,0:T(8,128)S(1)}, u32[]{:S(2)}, u32[]{:S(2)}) collective-permute-start(f32[24,128]{1,0:T(8,128)S(1)} %get-tuple-element.56), channel_id=1, source_target_pairs={{1,0},{2,1},{3,2},{0,3},{5,4},{6,5},{7,6},{4,7},{9,8},{10,9},{11,1... | collective-permute-start | bytes 36872 | tf_op jit(solution)/shard_map/ppermute | solution.py:404
  56.5 1.7 %collective-permute-done.14.back_minus = f32[24,128]{1,0:T(8,128)S(1)} collective-permute-done((f32[24,128]{1,0:T(8,128)S(1)}, f32[24,128]{1,0:T(8,128)S(1)}, u32[]{:S(2)}, u32[]{:S(2)}) %collective-permute-start.14) | collective-permute-done | bytes 12320 | tf_op jit(solution)/shard_map/ppermute | solution.py:399
  58.3 1.7 %collective-permute-start.16 = (f32[24,128]{1,0:T(8,128)S(1)}, f32[24,128]{1,0:T(8,128)S(1)}, u32[]{:S(2)}, u32[]{:S(2)}) collective-permute-start(f32[24,128]{1,0:T(8,128)S(1)} %pad_maximum_fusion.6), channel_id=1, source_target_pairs={{4,8},{8,4},{12,16},{16,12},{20,24},{24,20},{28,32},{32,28},{36,40... | collective-permute-start | bytes 36872 | tf_op jit(solution)/shard_map/ppermute | solution.py:410
  60.0 1.3 %shard_map.158 = (f32[256,128]{1,0:T(8,128)S(1)}, f32[256,128]{1,0:T(8,128)S(1)}) custom-call(f32[256,128]{1,0:T(8,128)S(1)} %get-tuple-element.57.head, f32[256,128]{1,0:T(8,128)S(1)} %get-tuple-element.58.cond, f32[256,128]{1,0:T(8,128)S(1)} %bitcast.20, f32[256,128]{1,0:T(8,128)S(1)} %bitcast.26, s32[256,128]{1,0:T(8,128)S(1)} %bitcast.23, ...), custom_call_target="tpu_custom_call" | custom-call | flops 1000000000 | bytes 3000000 | tf_op jit(solution)/shard_map/pallas_call | solution.py:475
  61.4 3.5 %collective-permute-done.16.cross = f32[24,128]{1,0:T(8,128)S(1)} collective-permute-done((f32[24,128]{1,0:T(8,128)S(1)}, f32[24,128]{1,0:T(8,128)S(1)}, u32[]{:S(2)}, u32[]{:S(2)}) %collective-permute-start.16) | collective-permute-done | bytes 12320 | tf_op jit(solution)/shard_map/ppermute | solution.py:410
  (73 shorter events, 11.5 us)
Async XLA Ops:
  2.0 6.7 %copy-start.12 = (s32[128,128]{1,0:T(8,128)S(1)}, s32[128,128]{1,0:T(8,128)}, u32[]{:S(2)}) copy-start(s32[128,128]{1,0:T(8,128)} %param.26) | copy-start | bytes 196612
  2.0 6.6 %copy-start.13 = (s32[128,128]{1,0:T(8,128)S(1)}, s32[128,128]{1,0:T(8,128)}, u32[]{:S(2)}) copy-start(s32[128,128]{1,0:T(8,128)} %param.25) | copy-start | bytes 196612
  4.3 4.5 %collective-permute-start = (f32[64,128]{1,0:T(8,128)S(1)}, f32[64,128]{1,0:T(8,128)S(1)}, u32[]{:S(2)}, u32[]{:S(2)}) collective-permute-start(f32[64,128]{1,0:T(8,128)S(1)} %get-tuple-element.33), channel_id=1, source_target_pairs={{0,4},{4,0},{8,12},{12,8},{16,20},{20,16},{24,28},{28,24},{32,36},... | collective-permute-start | bytes 98312 | tf_op jit(solution)/shard_map/ppermute | solution.py:410
  4.4 7.0 %collective-permute-start.2 = (f32[112,128]{1,0:T(8,128)S(1)}, f32[112,128]{1,0:T(8,128)S(1)}, u32[]{:S(2)}, u32[]{:S(2)}) collective-permute-start(f32[112,128]{1,0:T(8,128)S(1)} %get-tuple-element.37), channel_id=1, source_target_pairs={{4,8},{8,4},{12,16},{16,12},{20,24},{24,20},{28,32},{32,28},{36,40... | collective-permute-start | bytes 172040 | tf_op jit(solution)/shard_map/ppermute | solution.py:410
  9.9 1.3 %collective-permute-start.1 = (f32[48,128]{1,0:T(8,128)S(1)}, f32[48,128]{1,0:T(8,128)S(1)}, u32[]{:S(2)}, u32[]{:S(2)}) collective-permute-start(f32[48,128]{1,0:T(8,128)S(1)} %get-tuple-element.35), channel_id=1, source_target_pairs={{0,4},{4,0},{8,12},{12,8},{16,20},{20,16},{24,28},{28,24},{32,36},... | collective-permute-start | bytes 73736 | tf_op jit(solution)/shard_map/ppermute | solution.py:410
  11.4 6.0 %collective-permute-start.3 = (f32[56,128]{1,0:T(8,128)S(1)}, f32[56,128]{1,0:T(8,128)S(1)}, u32[]{:S(2)}, u32[]{:S(2)}) collective-permute-start(f32[56,128]{1,0:T(8,128)S(1)} %pad_maximum_fusion), channel_id=1, source_target_pairs={{0,1},{1,2},{2,3},{3,0},{4,5},{5,6},{6,7},{7,4},{8,9},{9,10},{10,1... | collective-permute-start | bytes 86024 | tf_op jit(solution)/shard_map/ppermute | solution.py:399
  13.4 4.0 %collective-permute-start.4 = (f32[56,128]{1,0:T(8,128)S(1)}, f32[56,128]{1,0:T(8,128)S(1)}, u32[]{:S(2)}, u32[]{:S(2)}) collective-permute-start(f32[56,128]{1,0:T(8,128)S(1)} %pad_maximum_fusion.1), channel_id=1, source_target_pairs={{1,0},{2,1},{3,2},{0,3},{5,4},{6,5},{7,6},{4,7},{9,8},{10,9},{11,1... | collective-permute-start | bytes 86024 | tf_op jit(solution)/shard_map/ppermute | solution.py:404
  17.3 12.3 %copy-start.2 = (s32[32,8,128]{2,1,0:T(8,128)S(1)}, s32[32,8,128]{2,1,0:T(8,128)}, u32[]{:S(2)}) copy-start(s32[32,8,128]{2,1,0:T(8,128)} %param.17) | copy-start | bytes 393220
  17.4 12.3 %copy-start.3 = (f32[32,8,128]{2,1,0:T(8,128)S(1)}, f32[32,8,128]{2,1,0:T(8,128)}, u32[]{:S(2)}) copy-start(f32[32,8,128]{2,1,0:T(8,128)} %param.16) | copy-start | bytes 393220
  17.4 12.3 %copy-start.4 = (f32[32,8,128]{2,1,0:T(8,128)S(1)}, f32[32,8,128]{2,1,0:T(8,128)}, u32[]{:S(2)}) copy-start(f32[32,8,128]{2,1,0:T(8,128)} %param.18) | copy-start | bytes 393220
  21.9 5.0 %collective-permute-start.5 = (f32[24,128]{1,0:T(8,128)S(1)}, f32[24,128]{1,0:T(8,128)S(1)}, u32[]{:S(2)}, u32[]{:S(2)}) collective-permute-start(f32[24,128]{1,0:T(8,128)S(1)} %get-tuple-element.42), channel_id=1, source_target_pairs={{0,1},{1,2},{2,3},{3,0},{4,5},{5,6},{6,7},{7,4},{8,9},{9,10},{10,1... | collective-permute-start | bytes 36872 | tf_op jit(solution)/shard_map/ppermute | solution.py:399
  23.7 3.7 %collective-permute-start.6 = (f32[24,128]{1,0:T(8,128)S(1)}, f32[24,128]{1,0:T(8,128)S(1)}, u32[]{:S(2)}, u32[]{:S(2)}) collective-permute-start(f32[24,128]{1,0:T(8,128)S(1)} %get-tuple-element.44), channel_id=1, source_target_pairs={{1,0},{2,1},{3,2},{0,3},{5,4},{6,5},{7,6},{4,7},{9,8},{10,9},{11,1... | collective-permute-start | bytes 36872 | tf_op jit(solution)/shard_map/ppermute | solution.py:404
  27.4 2.2 %collective-permute-start.8 = (f32[24,128]{1,0:T(8,128)S(1)}, f32[24,128]{1,0:T(8,128)S(1)}, u32[]{:S(2)}, u32[]{:S(2)}) collective-permute-start(f32[24,128]{1,0:T(8,128)S(1)} %pad_maximum_fusion.5), channel_id=1, source_target_pairs={{0,4},{4,0},{8,12},{12,8},{16,20},{20,16},{24,28},{28,24},{32,36},... | collective-permute-start | bytes 36872 | tf_op jit(solution)/shard_map/ppermute | solution.py:410
  27.5 6.7 %collective-permute-start.7 = (f32[24,128]{1,0:T(8,128)S(1)}, f32[24,128]{1,0:T(8,128)S(1)}, u32[]{:S(2)}, u32[]{:S(2)}) collective-permute-start(f32[24,128]{1,0:T(8,128)S(1)} %pad_maximum_fusion.4), channel_id=1, source_target_pairs={{4,8},{8,4},{12,16},{16,12},{20,24},{24,20},{28,32},{32,28},{36,40... | collective-permute-start | bytes 36872 | tf_op jit(solution)/shard_map/ppermute | solution.py:410
  29.7 4.5 %copy-start = (f32[32,8,128]{2,1,0:T(8,128)S(1)}, f32[32,8,128]{2,1,0:T(8,128)}, u32[]{:S(2)}) copy-start(f32[32,8,128]{2,1,0:T(8,128)} %param.15) | copy-start | bytes 393220
  35.0 3.3 %collective-permute-start.9 = (f32[64,128]{1,0:T(8,128)S(1)}, f32[64,128]{1,0:T(8,128)S(1)}, u32[]{:S(2)}, u32[]{:S(2)}) collective-permute-start(f32[64,128]{1,0:T(8,128)S(1)} %get-tuple-element.48), channel_id=1, source_target_pairs={{0,4},{4,0},{8,12},{12,8},{16,20},{20,16},{24,28},{28,24},{32,36},... | collective-permute-start | bytes 98312 | tf_op jit(solution)/shard_map/ppermute | solution.py:410
  36.2 7.0 %collective-permute-start.11 = (f32[112,128]{1,0:T(8,128)S(1)}, f32[112,128]{1,0:T(8,128)S(1)}, u32[]{:S(2)}, u32[]{:S(2)}) collective-permute-start(f32[112,128]{1,0:T(8,128)S(1)} %shard_map.156), channel_id=1, source_target_pairs={{4,8},{8,4},{12,16},{16,12},{20,24},{24,20},{28,32},{32,28},{36,40... | collective-permute-start | bytes 172040 | tf_op jit(solution)/shard_map/ppermute | solution.py:410
  40.3 1.3 %collective-permute-start.10 = (f32[48,128]{1,0:T(8,128)S(1)}, f32[48,128]{1,0:T(8,128)S(1)}, u32[]{:S(2)}, u32[]{:S(2)}) collective-permute-start(f32[48,128]{1,0:T(8,128)S(1)} %get-tuple-element.49), channel_id=1, source_target_pairs={{0,4},{4,0},{8,12},{12,8},{16,20},{20,16},{24,28},{28,24},{32,36},... | collective-permute-start | bytes 73736 | tf_op jit(solution)/shard_map/ppermute | solution.py:410
  43.2 5.1 %collective-permute-start.12 = (f32[56,128]{1,0:T(8,128)S(1)}, f32[56,128]{1,0:T(8,128)S(1)}, u32[]{:S(2)}, u32[]{:S(2)}) collective-permute-start(f32[56,128]{1,0:T(8,128)S(1)} %pad_maximum_fusion.2), channel_id=1, source_target_pairs={{0,1},{1,2},{2,3},{3,0},{4,5},{5,6},{6,7},{7,4},{8,9},{9,10},{10,1... | collective-permute-start | bytes 86024 | tf_op jit(solution)/shard_map/ppermute | solution.py:399
  44.9 3.9 %collective-permute-start.13 = (f32[56,128]{1,0:T(8,128)S(1)}, f32[56,128]{1,0:T(8,128)S(1)}, u32[]{:S(2)}, u32[]{:S(2)}) collective-permute-start(f32[56,128]{1,0:T(8,128)S(1)} %pad_maximum_fusion.3), channel_id=1, source_target_pairs={{1,0},{2,1},{3,2},{0,3},{5,4},{6,5},{7,6},{4,7},{9,8},{10,9},{11,1... | collective-permute-start | bytes 86024 | tf_op jit(solution)/shard_map/ppermute | solution.py:404
  53.3 4.9 %collective-permute-start.14 = (f32[24,128]{1,0:T(8,128)S(1)}, f32[24,128]{1,0:T(8,128)S(1)}, u32[]{:S(2)}, u32[]{:S(2)}) collective-permute-start(f32[24,128]{1,0:T(8,128)S(1)} %get-tuple-element.54), channel_id=1, source_target_pairs={{0,1},{1,2},{2,3},{3,0},{4,5},{5,6},{6,7},{7,4},{8,9},{9,10},{10,1... | collective-permute-start | bytes 36872 | tf_op jit(solution)/shard_map/ppermute | solution.py:399
  54.6 3.7 %collective-permute-start.15 = (f32[24,128]{1,0:T(8,128)S(1)}, f32[24,128]{1,0:T(8,128)S(1)}, u32[]{:S(2)}, u32[]{:S(2)}) collective-permute-start(f32[24,128]{1,0:T(8,128)S(1)} %get-tuple-element.56), channel_id=1, source_target_pairs={{1,0},{2,1},{3,2},{0,3},{5,4},{6,5},{7,6},{4,7},{9,8},{10,9},{11,1... | collective-permute-start | bytes 36872 | tf_op jit(solution)/shard_map/ppermute | solution.py:404
  58.3 1.8 %collective-permute-start.17 = (f32[24,128]{1,0:T(8,128)S(1)}, f32[24,128]{1,0:T(8,128)S(1)}, u32[]{:S(2)}, u32[]{:S(2)}) collective-permute-start(f32[24,128]{1,0:T(8,128)S(1)} %pad_maximum_fusion.7), channel_id=1, source_target_pairs={{0,4},{4,0},{8,12},{12,8},{16,20},{20,16},{24,28},{28,24},{32,36},... | collective-permute-start | bytes 36872 | tf_op jit(solution)/shard_map/ppermute | solution.py:410
  58.3 6.5 %collective-permute-start.16 = (f32[24,128]{1,0:T(8,128)S(1)}, f32[24,128]{1,0:T(8,128)S(1)}, u32[]{:S(2)}, u32[]{:S(2)}) collective-permute-start(f32[24,128]{1,0:T(8,128)S(1)} %pad_maximum_fusion.6), channel_id=1, source_target_pairs={{4,8},{8,4},{12,16},{16,12},{20,24},{24,20},{28,32},{32,28},{36,40... | collective-permute-start | bytes 36872 | tf_op jit(solution)/shard_map/ppermute | solution.py:410
  (8 other events, 8.1 us)
